TPU v7x, 32 devices: a whole 2x2x4 slice. The times are simulated.
32 devices in a mesh: fsdp: 8 (over z, y), tensor: 4 (over x, core).
Axes of the slice: x: 2, y: 2, z: 4, core: 2. Of those that a mesh axis runs over, the one named last changes fastest.
Arguments:
- image_rows: float32 [96, 196, 512], P(('fsdp', 'tensor')), may hold values from -6 to 6
- cotangent: float32 [96, 196, 512], P(('fsdp', 'tensor')), may hold values from -6 to 6
- live_counts: int32 [8], P('fsdp'), may hold values from 6 to 12, as said below
- qkv_weight: float32 [2, 512, 3, 512], P(None, 'fsdp', None, 'tensor'), may hold values from -0.25 to 0.25
- qkv_first: float32 [2, 512, 3, 512], P(None, 'fsdp', None, 'tensor'), may hold values from -80 to 80
- qkv_second: float32 [2, 512, 3, 512], P(None, 'fsdp', None, 'tensor'), may hold values from 14.112 to 56.448
- out_weight: float32 [2, 512, 512], P(None, 'tensor', 'fsdp'), may hold values from -0.75 to 0.75
- out_first: float32 [2, 512, 512], P(None, 'tensor', 'fsdp'), may hold values from -40 to 40
- out_second: float32 [2, 512, 512], P(None, 'tensor', 'fsdp'), may hold values from 3.552 to 14.112
- up_weight: float32 [2, 512, 2048], P(None, 'fsdp', 'tensor'), may hold values from -0.25 to 0.25
- up_first: float32 [2, 512, 2048], P(None, 'fsdp', 'tensor'), may hold values from -28 to 28
- up_second: float32 [2, 512, 2048], P(None, 'fsdp', 'tensor'), may hold values from 1.728 to 6.912
- down_weight: float32 [2, 2048, 512], P(None, 'tensor', 'fsdp'), may hold values from -0.125 to 0.125
- down_first: float32 [2, 2048, 512], P(None, 'tensor', 'fsdp'), may hold values from -48 to 48
- down_second: float32 [2, 2048, 512], P(None, 'tensor', 'fsdp'), may hold values from 5.952 to 23.712
- rel_table: float32 [2, 16, 169], P(None, 'tensor'), may hold values from -3 to 3
- rel_first: float32 [2, 16, 169], P(None, 'tensor'), may hold values from -40 to 40
- rel_second: float32 [2, 16, 169], P(None, 'tensor'), may hold values from 3.552 to 14.112
- qv_bias: float32 [2, 2, 512], P(None, None, 'tensor'), may hold values from -1.75 to 1.75
- qv_first: float32 [2, 2, 512], P(None, None, 'tensor'), may hold values from -80 to 80
- qv_second: float32 [2, 2, 512], P(None, None, 'tensor'), may hold values from 14.112 to 56.448
- hidden_bias: float32 [2, 2048], P(None, 'tensor'), may hold values from -1.75 to 1.75
- hidden_first: float32 [2, 2048], P(None, 'tensor'), may hold values from -28 to 28
- hidden_second: float32 [2, 2048], P(None, 'tensor'), may hold values from 1.728 to 6.912
- norm_gain: float32 [2, 2, 512], replicated, may hold values from 0.4 to 1.6
- gain_first: float32 [2, 2, 512], replicated, may hold values from -80 to 80
- gain_second: float32 [2, 2, 512], replicated, may hold values from 14.112 to 56.448
- norm_bias: float32 [2, 4, 512], replicated, may hold values from -1.75 to 1.75
- bias_first: float32 [2, 4, 512], replicated, may hold values from -80 to 80
- bias_second: float32 [2, 4, 512], replicated, may hold values from 14.112 to 56.448
Outputs:
- block_out: float32 [96, 196, 512], P(('fsdp', 'tensor'))
- input_grad: float32 [96, 196, 512], P(('fsdp', 'tensor'))
- qkv_weight_next: float32 [2, 512, 3, 512], P(None, 'fsdp', None, 'tensor')
- qkv_first_next: float32 [2, 512, 3, 512], P(None, 'fsdp', None, 'tensor')
- qkv_second_next: float32 [2, 512, 3, 512], P(None, 'fsdp', None, 'tensor')
- out_weight_next: float32 [2, 512, 512], P(None, 'tensor', 'fsdp')
- out_first_next: float32 [2, 512, 512], P(None, 'tensor', 'fsdp')
- out_second_next: float32 [2, 512, 512], P(None, 'tensor', 'fsdp')
- up_weight_next: float32 [2, 512, 2048], P(None, 'fsdp', 'tensor')
- up_first_next: float32 [2, 512, 2048], P(None, 'fsdp', 'tensor')
- up_second_next: float32 [2, 512, 2048], P(None, 'fsdp', 'tensor')
- down_weight_next: float32 [2, 2048, 512], P(None, 'tensor', 'fsdp')
- down_first_next: float32 [2, 2048, 512], P(None, 'tensor', 'fsdp')
- down_second_next: float32 [2, 2048, 512], P(None, 'tensor', 'fsdp')
- rel_table_next: float32 [2, 16, 169], P(None, 'tensor')
- rel_first_next: float32 [2, 16, 169], P(None, 'tensor')
- rel_second_next: float32 [2, 16, 169], P(None, 'tensor')
- qv_bias_next: float32 [2, 2, 512], P(None, None, 'tensor')
- qv_first_next: float32 [2, 2, 512], P(None, None, 'tensor')
- qv_second_next: float32 [2, 2, 512], P(None, None, 'tensor')
- hidden_bias_next: float32 [2, 2048], P(None, 'tensor')
- hidden_first_next: float32 [2, 2048], P(None, 'tensor')
- hidden_second_next: float32 [2, 2048], P(None, 'tensor')
- norm_gain_next: float32 [2, 2, 512], replicated
- gain_first_next: float32 [2, 2, 512], replicated
- gain_second_next: float32 [2, 2, 512], replicated
- norm_bias_next: float32 [2, 4, 512], replicated
- bias_first_next: float32 [2, 4, 512], replicated
- bias_second_next: float32 [2, 4, 512], replicated
Inputs may be any that keep to these rules, and one draw needn't show every extreme that they name: Image slot s of fsdp index i is live when s < live_counts[i]; an index's 12 slots lie in order over its 3-slot devices along tensor. At least one index has all 12 slots live.
All inputs are finite; a program needn't handle non-finite values.
Results may differ from a plain program's by a relative error of at most 0.015.
Values may be sent and summed in bfloat16 or wider, within the bound.
A program may use at most 192 MiB of HBM per device.

v0:
```python
import jax
import jax.numpy as jnp
from jax import lax
from jax.sharding import PartitionSpec as P

HEAD_DIM = 32
SIDE = 14
WIN = 7
SHIFT = 3
BLOCKS = 2
ADAM_STEP = 10


HIGHEST = lax.Precision.HIGHEST
NORM_EPS = 1e-05
BETA_ONE = 0.9
BETA_TWO = 0.999
MATRIX_RATE = 0.04
SMALL_RATE = 0.3
WEIGHT_DECAY = 0.05
ADAM_EPS = 1e-08
MASK_FILL = -100.0


def rounded(values):
    return lax.optimization_barrier(values.astype(jnp.bfloat16)).astype(jnp.float32)


def to_windows(field_rows):
    leading = field_rows.shape[:-3]
    channels = field_rows.shape[-1]
    per_side = SIDE // WIN
    lead_dims = len(leading)
    field_rows = field_rows.reshape(leading + (per_side, WIN, per_side, WIN, channels))
    field_rows = jnp.moveaxis(field_rows, lead_dims + 2, lead_dims + 1)
    return field_rows.reshape(leading + (per_side * per_side, WIN * WIN, channels))


def from_windows(field_rows):
    leading = field_rows.shape[:-3]
    channels = field_rows.shape[-1]
    per_side = SIDE // WIN
    lead_dims = len(leading)
    field_rows = field_rows.reshape(leading + (per_side, per_side, WIN, WIN, channels))
    field_rows = jnp.moveaxis(field_rows, lead_dims + 1, lead_dims + 2)
    return field_rows.reshape(leading + (SIDE, SIDE, channels))


def windowed(token_rows, shifted):
    image_count = token_rows.shape[0] // (SIDE * SIDE)
    grid_rows = token_rows.reshape(image_count, SIDE, SIDE, token_rows.shape[1])
    if shifted:
        grid_rows = jnp.roll(grid_rows, (-SHIFT, -SHIFT), (1, 2))
    return to_windows(grid_rows).reshape(token_rows.shape)


def unwindowed(token_rows, shifted):
    image_count = token_rows.shape[0] // (SIDE * SIDE)
    grid_rows = from_windows(
        token_rows.reshape(image_count, (SIDE // WIN) ** 2, WIN * WIN, token_rows.shape[1])
    )
    if shifted:
        grid_rows = jnp.roll(grid_rows, (SHIFT, SHIFT), (1, 2))
    return grid_rows.reshape(token_rows.shape)


def rel_lookup():
    position = jnp.arange(WIN * WIN, dtype=jnp.int32)
    row_pos = position // WIN
    col_pos = position % WIN
    return (row_pos[:, None] - row_pos[None, :] + WIN - 1) * (2 * WIN - 1) + (
        col_pos[:, None] - col_pos[None, :] + WIN - 1
    )


def window_mask(shifted):
    if not shifted:
        return jnp.zeros(((SIDE // WIN) ** 2, WIN * WIN, WIN * WIN), jnp.float32)
    coords = jnp.arange(SIDE, dtype=jnp.int32)
    bands = (coords >= SIDE - WIN).astype(jnp.int32) + (coords >= SIDE - SHIFT).astype(jnp.int32)
    region = bands[:, None] * 3 + bands[None, :]
    labels = to_windows(region[:, :, None])[:, :, 0]
    return jnp.where(labels[:, :, None] == labels[:, None, :], 0.0, MASK_FILL).astype(jnp.float32)


def inner_rows(left, right):
    return lax.dot_general(
        left, right, (((0,), (0,)), ((), ())), preferred_element_type=jnp.float32
    )


def times_t(left, right):
    return lax.dot_general(
        left, right, (((1,), (1,)), ((), ())), preferred_element_type=jnp.float32
    )


def exact_gelu(values):
    return jax.nn.gelu(values, approximate=False)


def norm_parts(values):
    row_mean = jnp.mean(values, -1, keepdims=True)
    centred = values - row_mean
    inv_std = lax.rsqrt(jnp.mean(centred * centred, -1, keepdims=True) + NORM_EPS)
    return (centred * inv_std, inv_std)


def norm_back(grad_out, unit_rows, inv_std, gain_row):
    grad_unit = grad_out * gain_row
    grad_in = inv_std * (
        grad_unit
        - jnp.mean(grad_unit, -1, keepdims=True)
        - unit_rows * jnp.mean(grad_unit * unit_rows, -1, keepdims=True)
    )
    return (grad_in, jnp.sum(grad_out * unit_rows, 0), jnp.sum(grad_out, 0))


def head_view(token_rows, heads_here):
    image_count = token_rows.shape[0] // (SIDE * SIDE)
    return token_rows.reshape(image_count, (SIDE // WIN) ** 2, WIN * WIN, heads_here, HEAD_DIM)


def head_scores(query_rows, key_rows, additive, heads_here):
    raw_scores = jnp.einsum(
        "bwqhe,bwkhe->bwhqk",
        head_view(query_rows, heads_here),
        head_view(key_rows, heads_here),
        preferred_element_type=jnp.float32,
    )
    return raw_scores * HEAD_DIM ** (-0.5) + additive


def log_sum(scores):
    row_max = jnp.max(scores, -1, keepdims=True)
    return row_max + jnp.log(jnp.sum(jnp.exp(scores - row_max), -1, keepdims=True))


def adam(weight, first_moment, second_moment, gradient, step_rate, decay_rate):
    first_new = BETA_ONE * first_moment + (1.0 - BETA_ONE) * gradient
    second_new = BETA_TWO * second_moment + (1.0 - BETA_TWO) * gradient * gradient
    first_hat = first_new / (1.0 - BETA_ONE**ADAM_STEP)
    second_hat = second_new / (1.0 - BETA_TWO**ADAM_STEP)
    weight_new = weight - step_rate * (
        first_hat / (jnp.sqrt(second_hat) + ADAM_EPS) + decay_rate * weight
    )
    return (weight_new, first_new, second_new)


def shards(
    image_rows,
    cotangent,
    live_counts,
    qkv_weight,
    qkv_first,
    qkv_second,
    out_weight,
    out_first,
    out_second,
    up_weight,
    up_first,
    up_second,
    down_weight,
    down_first,
    down_second,
    rel_table,
    rel_first,
    rel_second,
    qv_bias,
    qv_first,
    qv_second,
    hidden_bias,
    hidden_first,
    hidden_second,
    norm_gain,
    gain_first,
    gain_second,
    norm_bias,
    bias_first,
    bias_second,
):
    local_images = image_rows.shape[0]
    model_width = image_rows.shape[2]
    local_rows = local_images * SIDE * SIDE
    my_tensor = lax.axis_index("tensor")
    slot_ids = my_tensor * local_images + jnp.arange(local_images, dtype=jnp.int32)
    live_mask = (slot_ids < live_counts[0]).astype(jnp.float32)
    residual_grad = (cotangent * live_mask[:, None, None]).reshape(local_rows, model_width)
    residual = image_rows.reshape(local_rows, model_width)
    qkv_w, out_w, up_w, down_w = (
        lax.all_gather(qkv_weight.astype(jnp.bfloat16), "fsdp", axis=1, tiled=True),
        lax.all_gather(out_weight.astype(jnp.bfloat16), "fsdp", axis=2, tiled=True),
        lax.all_gather(up_weight.astype(jnp.bfloat16), "fsdp", axis=1, tiled=True),
        lax.all_gather(down_weight.astype(jnp.bfloat16), "fsdp", axis=2, tiled=True),
    )
    table_w = rel_table.astype(jnp.bfloat16)
    qv_w = qv_bias.astype(jnp.bfloat16)
    hidden_w = hidden_bias.astype(jnp.bfloat16)
    head_width = qkv_w.shape[3]
    heads_here = head_width // HEAD_DIM
    offset_used = jnp.concatenate([norm_bias[:, :2], rounded(norm_bias[:, 2:])], 1)
    rel_count = rel_table.shape[2]
    onehot_rows = (
        jnp.arange(rel_count, dtype=jnp.int32)[:, None] == rel_lookup().reshape(1, -1)
    ).astype(jnp.float32)
    onehot_low = onehot_rows.astype(jnp.bfloat16)
    kept_state = []
    for layer_idx in range(BLOCKS):
        shifted = layer_idx % 2 == 1
        gain_rows = norm_gain[layer_idx]
        offset_rows = offset_used[layer_idx]
        unit_one, inv_one = norm_parts(residual)
        normed_one = (unit_one * gain_rows[0] + offset_rows[0]).astype(jnp.bfloat16)
        normed_all = lax.all_gather(normed_one, "tensor", axis=0, tiled=True)
        window_rows = windowed(normed_all, shifted)
        qkv_rows = jnp.dot(
            window_rows,
            qkv_w[layer_idx].reshape(model_width, 3 * head_width),
            preferred_element_type=jnp.float32,
        )
        query_rows = (qkv_rows[:, :head_width] + qv_w[layer_idx, 0]).astype(jnp.bfloat16)
        key_rows = qkv_rows[:, head_width : 2 * head_width].astype(jnp.bfloat16)
        value_rows = (qkv_rows[:, 2 * head_width :] + qv_w[layer_idx, 1]).astype(jnp.bfloat16)
        rel_bias = jnp.dot(
            table_w[layer_idx], onehot_low, preferred_element_type=jnp.float32
        ).reshape(heads_here, WIN * WIN, WIN * WIN)
        additive = rel_bias[None, None] + window_mask(shifted)[None, :, None]
        scores = head_scores(query_rows, key_rows, additive, heads_here)
        log_total = log_sum(scores)
        prob_low = jnp.exp(scores - log_total).astype(jnp.bfloat16)
        attended = (
            jnp.einsum(
                "bwhqk,bwkhe->bwqhe",
                prob_low,
                head_view(value_rows, heads_here),
                preferred_element_type=jnp.float32,
            )
            .reshape(query_rows.shape)
            .astype(jnp.bfloat16)
        )
        partial_value = unwindowed(
            jnp.dot(attended, out_w[layer_idx], preferred_element_type=jnp.float32), shifted
        )
        branch = lax.psum_scatter(partial_value, "tensor", scatter_dimension=0, tiled=True)
        middle = residual + branch + offset_rows[2]
        unit_two, inv_two = norm_parts(middle)
        normed_two = (unit_two * gain_rows[1] + offset_rows[1]).astype(jnp.bfloat16)
        normed_two_all = lax.all_gather(normed_two, "tensor", axis=0, tiled=True)
        hidden_pre = (
            jnp.dot(normed_two_all, up_w[layer_idx], preferred_element_type=jnp.float32)
            + hidden_w[layer_idx]
        )
        hidden_act, gelu_back = jax.vjp(exact_gelu, hidden_pre)
        hidden_low = hidden_act.astype(jnp.bfloat16)
        partial_two = jnp.dot(hidden_low, down_w[layer_idx], preferred_element_type=jnp.float32)
        branch_two = lax.psum_scatter(partial_two, "tensor", scatter_dimension=0, tiled=True)
        kept_state.append(
            (
                shifted,
                gain_rows,
                unit_one,
                inv_one,
                unit_two,
                inv_two,
                window_rows,
                query_rows,
                key_rows,
                value_rows,
                additive,
                log_total,
                attended,
                normed_two_all,
                gelu_back,
                hidden_low,
            )
        )
        residual = middle + branch_two + offset_rows[3]
    qkv_grads = [None] * BLOCKS
    out_grads = [None] * BLOCKS
    up_grads = [None] * BLOCKS
    down_grads = [None] * BLOCKS
    table_grads = [None] * BLOCKS
    qv_grads = [None] * BLOCKS
    hidden_grads = [None] * BLOCKS
    gain_grads = [None] * BLOCKS
    shift_grads = [None] * BLOCKS
    inv_root = HEAD_DIM ** (-0.5)
    for layer_idx in range(BLOCKS - 1, -1, -1):
        (
            shifted,
            gain_rows,
            unit_one,
            inv_one,
            unit_two,
            inv_two,
            window_rows,
            query_rows,
            key_rows,
            value_rows,
            additive,
            log_total,
            attended,
            normed_two_all,
            gelu_back,
            hidden_low,
        ) = kept_state[layer_idx]
        top_bias = jnp.sum(residual_grad, 0)
        grad_low = residual_grad.astype(jnp.bfloat16)
        grad_all = lax.all_gather(grad_low, "tensor", axis=0, tiled=True)
        down_grads[layer_idx] = inner_rows(hidden_low, grad_all)
        pre_low = gelu_back(times_t(grad_all, down_w[layer_idx]))[0].astype(jnp.bfloat16)
        hidden_grads[layer_idx] = jnp.sum(pre_low.astype(jnp.float32), 0)
        up_grads[layer_idx] = inner_rows(normed_two_all, pre_low)
        norm_two_part = times_t(pre_low, up_w[layer_idx])
        norm_two_grad = lax.psum_scatter(norm_two_part, "tensor", scatter_dimension=0, tiled=True)
        into_two, gain_two, shift_two = norm_back(norm_two_grad, unit_two, inv_two, gain_rows[1])
        grad_middle = residual_grad + into_two
        out_bias_sum = jnp.sum(grad_middle, 0)
        middle_low = grad_middle.astype(jnp.bfloat16)
        middle_all = lax.all_gather(middle_low, "tensor", axis=0, tiled=True)
        middle_win = windowed(middle_all, shifted)
        out_grads[layer_idx] = inner_rows(attended, middle_win)
        attended_grad = times_t(middle_win, out_w[layer_idx]).astype(jnp.bfloat16)
        prob_rows = jnp.exp(head_scores(query_rows, key_rows, additive, heads_here) - log_total)
        attended_heads = head_view(attended_grad, heads_here)
        query_heads = head_view(query_rows, heads_here)
        key_heads = head_view(key_rows, heads_here)
        prob_grad = jnp.einsum(
            "bwqhe,bwkhe->bwhqk",
            attended_heads,
            head_view(value_rows, heads_here),
            preferred_element_type=jnp.float32,
        )
        score_low = (
            prob_rows * (prob_grad - jnp.sum(prob_rows * prob_grad, -1, keepdims=True))
        ).astype(jnp.bfloat16)
        score_sum = jnp.sum(score_low.astype(jnp.float32), (0, 1)).reshape(heads_here, -1)
        table_grads[layer_idx] = lax.dot_general(
            score_sum,
            onehot_rows,
            (((1,), (1,)), ((), ())),
            precision=HIGHEST,
            preferred_element_type=jnp.float32,
        )
        query_grad = (
            (
                jnp.einsum(
                    "bwhqk,bwkhe->bwqhe", score_low, key_heads, preferred_element_type=jnp.float32
                )
                * inv_root
            )
            .astype(jnp.bfloat16)
            .reshape(query_rows.shape)
        )
        key_grad = (
            (
                jnp.einsum(
                    "bwhqk,bwqhe->bwkhe", score_low, query_heads, preferred_element_type=jnp.float32
                )
                * inv_root
            )
            .astype(jnp.bfloat16)
            .reshape(query_rows.shape)
        )
        value_grad = (
            jnp.einsum(
                "bwhqk,bwqhe->bwkhe",
                prob_rows.astype(jnp.bfloat16),
                attended_heads,
                preferred_element_type=jnp.float32,
            )
            .astype(jnp.bfloat16)
            .reshape(query_rows.shape)
        )
        qkv_rows_grad = jnp.concatenate([query_grad, key_grad, value_grad], 1)
        qv_grads[layer_idx] = jnp.stack(
            [jnp.sum(query_grad.astype(jnp.float32), 0), jnp.sum(value_grad.astype(jnp.float32), 0)]
        )
        qkv_grads[layer_idx] = inner_rows(window_rows, qkv_rows_grad).reshape(
            model_width, 3, head_width
        )
        norm_one_part = unwindowed(
            times_t(qkv_rows_grad, qkv_w[layer_idx].reshape(model_width, 3 * head_width)), shifted
        )
        norm_one_grad = lax.psum_scatter(norm_one_part, "tensor", scatter_dimension=0, tiled=True)
        into_one, gain_one, shift_one = norm_back(norm_one_grad, unit_one, inv_one, gain_rows[0])
        residual_grad = grad_middle + into_one
        gain_grads[layer_idx] = jnp.stack([gain_one, gain_two])
        shift_grads[layer_idx] = jnp.stack([shift_one, shift_two, out_bias_sum, top_bias])
    qkv_local = jnp.stack(qkv_grads)
    out_local = jnp.stack(out_grads)
    up_local = jnp.stack(up_grads)
    down_local = jnp.stack(down_grads)
    table_local = jnp.stack(table_grads)
    qv_local = jnp.stack(qv_grads)
    hidden_local = jnp.stack(hidden_grads)
    gain_local = jnp.stack(gain_grads)
    shift_local = jnp.stack(shift_grads)
    qkv_part, out_part, up_part, down_part = (qkv_local, out_local, up_local, down_local)
    table_sum, qv_sum, hidden_sum = lax.psum((table_local, qv_local, hidden_local), "fsdp")
    gain_sum, shift_sum = lax.psum((gain_local, shift_local), ("fsdp", "tensor"))
    qkv_sum, out_sum, up_sum, down_sum = (
        lax.psum_scatter(qkv_part, "fsdp", scatter_dimension=1, tiled=True),
        lax.psum_scatter(out_part, "fsdp", scatter_dimension=2, tiled=True),
        lax.psum_scatter(up_part, "fsdp", scatter_dimension=1, tiled=True),
        lax.psum_scatter(down_part, "fsdp", scatter_dimension=2, tiled=True),
    )
    qkv_next = adam(qkv_weight, qkv_first, qkv_second, qkv_sum, MATRIX_RATE, WEIGHT_DECAY)
    out_next = adam(out_weight, out_first, out_second, out_sum, MATRIX_RATE, WEIGHT_DECAY)
    up_next = adam(up_weight, up_first, up_second, up_sum, MATRIX_RATE, WEIGHT_DECAY)
    down_next = adam(down_weight, down_first, down_second, down_sum, MATRIX_RATE, WEIGHT_DECAY)
    rel_next = adam(rel_table, rel_first, rel_second, table_sum, SMALL_RATE, 0.0)
    qv_next = adam(qv_bias, qv_first, qv_second, qv_sum, SMALL_RATE, 0.0)
    hidden_next = adam(hidden_bias, hidden_first, hidden_second, hidden_sum, SMALL_RATE, 0.0)
    gain_next = adam(norm_gain, gain_first, gain_second, gain_sum, SMALL_RATE, 0.0)
    offset_next = adam(norm_bias, bias_first, bias_second, shift_sum, SMALL_RATE, 0.0)
    return (
        residual.reshape(image_rows.shape),
        residual_grad.reshape(image_rows.shape),
        qkv_next[0],
        qkv_next[1],
        qkv_next[2],
        out_next[0],
        out_next[1],
        out_next[2],
        up_next[0],
        up_next[1],
        up_next[2],
        down_next[0],
        down_next[1],
        down_next[2],
        rel_next[0],
        rel_next[1],
        rel_next[2],
        qv_next[0],
        qv_next[1],
        qv_next[2],
        hidden_next[0],
        hidden_next[1],
        hidden_next[2],
        gain_next[0],
        gain_next[1],
        gain_next[2],
        offset_next[0],
        offset_next[1],
        offset_next[2],
    )


def solution(mesh):
    return jax.shard_map(
        shards,
        mesh=mesh,
        in_specs=(
            P(("fsdp", "tensor"), None, None),
            P(("fsdp", "tensor"), None, None),
            P("fsdp"),
            P(None, "fsdp", None, "tensor"),
            P(None, "fsdp", None, "tensor"),
            P(None, "fsdp", None, "tensor"),
            P(None, "tensor", "fsdp"),
            P(None, "tensor", "fsdp"),
            P(None, "tensor", "fsdp"),
            P(None, "fsdp", "tensor"),
            P(None, "fsdp", "tensor"),
            P(None, "fsdp", "tensor"),
            P(None, "tensor", "fsdp"),
            P(None, "tensor", "fsdp"),
            P(None, "tensor", "fsdp"),
            P(None, "tensor", None),
            P(None, "tensor", None),
            P(None, "tensor", None),
            P(None, None, "tensor"),
            P(None, None, "tensor"),
            P(None, None, "tensor"),
            P(None, "tensor"),
            P(None, "tensor"),
            P(None, "tensor"),
            P(),
            P(),
            P(),
            P(),
            P(),
            P(),
        ),
        out_specs=(
            P(("fsdp", "tensor"), None, None),
            P(("fsdp", "tensor"), None, None),
            P(None, "fsdp", None, "tensor"),
            P(None, "fsdp", None, "tensor"),
            P(None, "fsdp", None, "tensor"),
            P(None, "tensor", "fsdp"),
            P(None, "tensor", "fsdp"),
            P(None, "tensor", "fsdp"),
            P(None, "fsdp", "tensor"),
            P(None, "fsdp", "tensor"),
            P(None, "fsdp", "tensor"),
            P(None, "tensor", "fsdp"),
            P(None, "tensor", "fsdp"),
            P(None, "tensor", "fsdp"),
            P(None, "tensor", None),
            P(None, "tensor", None),
            P(None, "tensor", None),
            P(None, None, "tensor"),
            P(None, None, "tensor"),
            P(None, None, "tensor"),
            P(None, "tensor"),
            P(None, "tensor"),
            P(None, "tensor"),
            P(),
            P(),
            P(),
            P(),
            P(),
            P(),
        ),
        check_vma=False,
    )
```

profile of v0, /device:TPU:0, one launch (start us, length us, event | category | flops | bytes accessed | tf_op | source)
XLA Modules:
  0.0 1319.8 jit_solution(13633468284552157036)
XLA Ops:
  14.3 32.5 %all_gather.38 = bf16[2,128,512]{1,0,2:T(2,128)(2,1)S(1)} all-gather(bf16[2,128,64]{1,0,2:T(2,128)(2,1)S(1)} %copy.438), channel_id=1, replica_groups=mesh['fsdp'=8,'tensor'=4] {'fsdp'}, dimensions={2}, use_global_device_ids=true | all-gather | bytes 294912 | tf_op jit(solution)/shard_map/all_gather | solution.py:192
  48.1 31.7 %all_gather.37 = bf16[2,512,3,128]{3,0,2,1:T(2,128)(2,1)S(1)} all-gather(bf16[2,64,3,128]{3,0,2,1:T(2,128)(2,1)S(1)} %copy.437), channel_id=1, replica_groups=mesh['fsdp'=8,'tensor'=4] {'fsdp'}, dimensions={1}, use_global_device_ids=true | all-gather | bytes 884736 | tf_op jit(solution)/shard_map/all_gather | solution.py:191
  147.5 6.4 reshape_reshape.30
  153.9 45.3 %fusion = f32[592,512]{1,0:T(8,128)S(1)} fusion(f32[2352,512]{1,0:T(8,128)} %reshape_reshape.30), kind=kCustom, calls=%all-reduce-scatter | all-reduce-scatter fusion | flops 1212417 | bytes 6029824
  211.2 25.9 %all-gather.25.cloned.1.call-done = bf16[4,588,512]{2,1,0:T(8,128)(2,1)} async-done(((bf16[1,588,512]{2,1,0:T(8,128)(2,1)}), bf16[4,588,512]{2,1,0:T(8,128)(2,1)}) %all-gather.25.cloned.1.call-update) | async-done | bytes 2408464 | tf_op jit(solution)/shard_map/all_gather | solution.py:248
  240.1 40.1 %all-gather.19.cloned.1.call-done = bf16[2,512,512]{2,1,0:T(8,128)(2,1)} async-done(((bf16[2,64,512]{2,1,0:T(8,128)(2,1)}), bf16[2,512,512]{2,1,0:T(8,128)(2,1)}) %all-gather.19.cloned.1.call-update) | async-done | bytes 1048592 | tf_op jit(solution)/shard_map/all_gather | solution.py:193
  280.1 14.7 %multiply_convert_fusion.3 = (bf16[2352,512]{1,0:T(8,128)(2,1)}, f32[2352,512]{1,0:T(8,128)}, f32[2352,512]{1,0:T(8,128)}) fusion(f32[512]{0:T(512)S(1)} %bitcast.356, bf16[2352,512]{1,0:T(8,128)(2,1)} %reshape.536, bf16[2,512,512]{2,1,0:T(8,128)(2,1)} %all-gather.19.cloned.1.call-done), kind=kOutput, calls=%fused_computation.41 | convolution fusion | flops 1312604160 | bytes 14977024 | tf_op jit(solution)/shard_map/dot_general | solution.py:250
  294.8 26.9 %all-gather.21.cloned.1.call-done = bf16[2,512,512]{1,2,0:T(8,128)(2,1)} async-done(((bf16[2,512,64]{1,2,0:T(8,128)(2,1)}), bf16[2,512,512]{1,2,0:T(8,128)(2,1)}) %all-gather.21.cloned.1.call-update) | async-done | bytes 1048592 | tf_op jit(solution)/shard_map/all_gather | solution.py:194
  327.1 45.2 %fusion.1 = f32[592,512]{1,0:T(8,128)S(1)} fusion(f32[2352,512]{1,0:T(8,128)} %fusion.68), kind=kCustom, calls=%all-reduce-scatter.1 | all-reduce-scatter fusion | flops 1212417 | bytes 6029824
  391.2 16.4 %all-gather.27.cloned.1.call-done = bf16[4,588,512]{2,1,0:T(8,128)(2,1)} async-done(((bf16[1,588,512]{2,1,0:T(8,128)(2,1)}), bf16[4,588,512]{2,1,0:T(8,128)(2,1)}) %all-gather.27.cloned.1.call-update) | async-done | bytes 2408464 | tf_op jit(solution)/shard_map/all_gather | solution.py:214
  482.2 6.8 reshape.508
  500.9 45.4 %fusion.2 = f32[592,512]{1,0:T(8,128)S(1)} fusion(f32[2352,512]{1,0:T(8,128)} %reshape.509), kind=kCustom, calls=%all-reduce-scatter.2 | all-reduce-scatter fusion | flops 1212417 | bytes 6029824
  558.4 25.5 %all-gather.29.cloned.1.call-done = bf16[4,588,512]{2,1,0:T(8,128)(2,1)} async-done(((bf16[1,588,512]{2,1,0:T(8,128)(2,1)}), bf16[4,588,512]{2,1,0:T(8,128)(2,1)}) %all-gather.29.cloned.1.call-update) | async-done | bytes 2408464 | tf_op jit(solution)/shard_map/all_gather | solution.py:248
  586.9 13.8 %multiply_convert_fusion.2 = (bf16[2352,512]{1,0:T(8,128)(2,1)}, f32[2352,512]{1,0:T(8,128)S(1)}, f32[2352,512]{1,0:T(8,128)S(1)}) fusion(f32[512]{0:T(512)S(1)} %bitcast.354, bf16[2352,512]{1,0:T(8,128)(2,1)} %reshape.540, bf16[2,512,512]{2,1,0:T(8,128)(2,1)} %all-gather.19.cloned.1.call-done), kind=kOutput, calls=%fused_computation.28 | convolution fusion | flops 1312604160 | bytes 14977024 | tf_op jit(solution)/shard_map/dot_general | solution.py:250
  608.7 46.2 %fusion.4 = f32[592,512]{1,0:T(8,128)} fusion(f32[2352,512]{1,0:T(8,128)} %fusion.69), kind=kCustom, calls=%all-reduce-scatter.4 | all-reduce-scatter fusion | flops 1212417 | bytes 6029824
  667.1 28.7 %all-gather.33.cloned.1.call-done = bf16[4,588,512]{2,1,0:T(8,128)(2,1)} async-done(((bf16[1,588,512]{2,1,0:T(8,128)(2,1)}), bf16[4,588,512]{2,1,0:T(8,128)(2,1)}) %all-gather.33.cloned.1.call-update) | async-done | bytes 2408464 | tf_op jit(solution)/shard_map/all_gather | solution.py:320
  781.0 6.8 reshape.515
  799.8 46.3 %fusion.5 = f32[592,512]{1,0:T(8,128)} fusion(f32[2352,512]{1,0:T(8,128)} %reshape.516), kind=kCustom, calls=%all-reduce-scatter.5 | all-reduce-scatter fusion | flops 1212417 | bytes 6029824
  858.3 28.7 %all-gather.35.cloned.1.call-done = bf16[4,588,512]{2,1,0:T(8,128)(2,1)} async-done(((bf16[1,588,512]{2,1,0:T(8,128)(2,1)}), bf16[4,588,512]{2,1,0:T(8,128)(2,1)}) %all-gather.35.cloned.1.call-update) | async-done | bytes 2408464 | tf_op jit(solution)/shard_map/all_gather | solution.py:309
  900.1 46.3 %fusion.6 = f32[592,512]{1,0:T(8,128)} fusion(f32[2352,512]{1,0:T(8,128)} %fusion.66), kind=kCustom, calls=%all-reduce-scatter.6 | all-reduce-scatter fusion | flops 1212417 | bytes 6029824
  1090.6 6.4 reshape_reshape.35
  1097.1 89.4 %fusion.96 = (f32[592,512]{1,0:T(8,128)}, f32[592,512]{1,0:T(8,128)}) fusion(f32[2352,512]{1,0:T(8,128)} %fusion.71, f32[2352,512]{1,0:T(8,128)} %reshape_reshape.35), kind=kCustom, calls=%all-reduce-scatter.8 | all-reduce-scatter fusion | flops 2424833 | bytes 12059136
  1210.2 37.4 %all-reduce.19 = (f32[2,4,169]{2,1,0:T(4,128)S(1)}, f32[2,2,128]{2,1,0:T(2,128)S(1)}, f32[2,512]{1,0:T(2,128)S(1)}) all-reduce(f32[2,4,169]{2,1,0:T(4,128)S(1)} %pad_maximum_fusion.13, f32[2,2,128]{2,1,0:T(2,128)S(1)} %pad_maximum_fusion.16, f32[2,512]{1,0:T(2,128)S(1)} %pad_maximum_fusion.15), channel_id=1, replica_groups=mesh['fsdp'=8,'tensor'=4] {'fsdp'}, use_global_device_ids=true, to_apply=%region_36.37 | all-reduce | flops 2888 | bytes 23104 | tf_op jit(solution)/shard_map/psum | solution.py:400
  1267.0 37.3 %all-reduce.18 = (f32[2,2,512]{2,1,0:T(2,128)S(1)}, f32[2,4,512]{2,1,0:T(4,128)S(1)}) all-reduce(f32[2,2,512]{2,1,0:T(2,128)S(1)} %pad_maximum_fusion.14, f32[2,4,512]{2,1,0:T(4,128)S(1)} %pad_maximum_fusion.12), channel_id=1, replica_groups=mesh['fsdp'=8,'tensor'=4] {'fsdp','tensor'}, use_global_device_ids=true, to_apply=%region_49.50 | all-reduce | flops 6144 | bytes 49152 | tf_op jit(solution)/shard_map/psum | solution.py:401
  (624 shorter events, 551.4 us)
Async XLA Ops:
  7.2 76.3 %all-gather.23.cloned.1.call-start = ((), (), s32[]{:S(2)}) async-start(), calls=%async_computation.6 | async-start | bytes 3031040 | tf_op jit(solution)/shard_map/all_gather | solution.py:214
  12.1 195.9 %copy-start.118 = (f32[1,1,512]{2,1,0:T(1,128)}, f32[1,1,512]{2,1,0:T(1,128)S(1)}, u32[]{:S(2)}) copy-start(f32[1,1,512]{2,1,0:T(1,128)S(1)} %get-tuple-element.206) | copy-start | bytes 6148
  12.1 367.9 %copy-start.120 = (f32[1,1,512]{2,1,0:T(1,128)}, f32[1,1,512]{2,1,0:T(1,128)S(1)}, u32[]{:S(2)}) copy-start(f32[1,1,512]{2,1,0:T(1,128)S(1)} %get-tuple-element.205) | copy-start | bytes 6148
  13.2 223.9 %all-gather.25.cloned.1.call-start = ((), (), s32[]{:S(2)}) async-start(), calls=%async_computation.7 | async-start | bytes 3031040 | tf_op jit(solution)/shard_map/all_gather | solution.py:248
  13.6 372.7 %copy-start.126 = (s32[2401]{0:T(1024)}, s32[2401]{0:T(1024)S(1)}, u32[]{:S(2)}) copy-start(s32[2401]{0:T(1024)S(1)} %add.542) | copy-start | bytes 28816
  199.3 3.1 collective-permute-start
  209.1 71.0 %all-gather.19.cloned.1.call-start = ((), (), s32[]{:S(2)}) async-start(), calls=%async_computation.2 | async-start | bytes 1179648 | tf_op jit(solution)/shard_map/all_gather | solution.py:193
  209.8 111.9 %all-gather.21.cloned.1.call-start = ((), (), s32[]{:S(2)}) async-start(), calls=%async_computation.3 | async-start | bytes 1179648 | tf_op jit(solution)/shard_map/all_gather | solution.py:194
  210.6 197.0 %all-gather.27.cloned.1.call-start = ((), (), s32[]{:S(2)}) async-start(), calls=%async_computation.8 | async-start | bytes 3031040 | tf_op jit(solution)/shard_map/all_gather | solution.py:214
  372.3 2.1 collective-permute-start.1
  381.1 174.1 %all-gather.31.cloned.1.call-start = ((), (), s32[]{:S(2)}) async-start(), calls=%async_computation.10 | async-start | bytes 3031040 | tf_op jit(solution)/shard_map/all_gather | solution.py:309
  386.2 197.7 %all-gather.29.cloned.1.call-start = ((), (), s32[]{:S(2)}) async-start(), calls=%async_computation.9 | async-start | bytes 3031040 | tf_op jit(solution)/shard_map/all_gather | solution.py:248
  546.4 2.1 collective-permute-start.2
  555.2 140.6 %all-gather.33.cloned.1.call-start = ((), (), s32[]{:S(2)}) async-start(), calls=%async_computation.11 | async-start | bytes 3031040 | tf_op jit(solution)/shard_map/all_gather | solution.py:320
  655.6 2.1 collective-permute-start.4
  667.0 220.0 %all-gather.35.cloned.1.call-start = ((), (), s32[]{:S(2)}) async-start(), calls=%async_computation.12 | async-start | bytes 3031040 | tf_op jit(solution)/shard_map/all_gather | solution.py:309
  847.0 2.1 collective-permute-start.5
  858.2 164.0 %all-gather.37.cloned.1.call-start = ((), (), s32[]{:S(2)}) async-start(), calls=%async_computation.13 | async-start | bytes 3031040 | tf_op jit(solution)/shard_map/all_gather | solution.py:320
  947.3 2.1 collective-permute-start.6
  958.7 346.9 %reduce-scatter.21.cloned.1.call-start = ((), (), s32[]{:S(2)}) async-start(), calls=%async_computation.5 | async-start | bytes 2359296 | tf_op jit(solution)/shard_map/reduce_scatter | solution.py:405
  1015.1 292.5 %all-reduce.24.cloned.1.call-start = ((), (), s32[]{:S(2)}) async-start(), calls=%async_computation.14 | async-start | bytes 5242880
  1097.1 214.1 %reduce-scatter.19.cloned.1.call-start = ((), (), s32[]{:S(2)}) async-start(), calls=%async_computation.4 | async-start | bytes 1769472 | tf_op jit(solution)/shard_map/reduce_scatter | solution.py:403
  1200.9 48.6 %collective-permute-start.7 = (f32[12,512]{1,0:T(8,128)S(1)}, f32[12,512]{1,0:T(8,128)S(1)}, u32[]{:S(2)}, u32[]{:S(2)}) collective-permute-start(f32[12,512]{1,0:T(8,128)S(1)} %slice.314), channel_id=1, source_target_pairs={{0,1},{1,2},{2,3},{4,5},{5,6},{6,7},{8,9},{9,10},{10,11},{12,13},{... | collective-permute-start | bytes 73736
  1202.1 58.1 %collective-permute-start.3 = (f32[12,512]{1,0:T(8,128)S(1)}, f32[12,512]{1,0:T(8,128)S(1)}, u32[]{:S(2)}, u32[]{:S(2)}) collective-permute-start(f32[12,512]{1,0:T(8,128)S(1)} %slice.310), channel_id=1, source_target_pairs={{0,1},{1,2},{2,3},{4,5},{5,6},{6,7},{8,9},{9,10},{10,11},{12,13},{... | collective-permute-start | bytes 73736
  (150 other events, 3057.0 us)
Sparse Core Ops, SparseCore 0:
  13.3 27.1 all-gather.22
  209.2 27.8 all-gather.24
  239.9 40.1 all-gather.18
  282.7 38.9 all-gather.20
  381.2 26.2 all-gather.26
  409.0 24.4 all-gather.30
  555.3 28.5 all-gather.28
  667.1 28.5 all-gather.32
  858.3 28.5 all-gather.34
  958.8 28.5 all-gather.36
  1015.2 71.8 reduce-scatter.20
  1097.2 120.4 all-reduce.23
  1221.1 64.9 reduce-scatter.18
where the time goes:
time: 1330 us; the launch traced here: 1320 us
  blocking collectives  503 us (38%)
  local copies, waits for them, and re-layouts  384 us (29%)
  waiting for transfers between devices  197 us (15%)
  matrix products  134 us (10%)
  other arithmetic  71.2 us (5%)
  between operations  18.2 us (1%)
    unnamed x7, blocking collectives  364 us
    unnamed x328, local copies, waits for them, and re-layouts  68.1 us
    reshape x16, local copies, waits for them, and re-layouts, head_view(): token_rows.reshape(image_count, (SIDE // WIN) ** 2, WIN * WIN, heads_here...  63.4 us
    concatenate x12, local copies, waits for them, and re-layouts, shards(): qkv_rows_grad = jnp.concatenate([query_grad, key_grad, value_grad], 1)  53.2 us
    all_gather x2, waiting for transfers between devices, shards(): normed_two_all = lax.all_gather(normed_two, 'tensor', axis=0, tiled=True)  51.4 us
    all_gather x1, waiting for transfers between devices, shards(): lax.all_gather(up_weight.astype(jnp.bfloat16), 'fsdp', axis=1, tiled=True)  40.1 us
    psum x1, blocking collectives, shards(): lax.psum((table_local, qv_local, hidden_local), 'fsdp')  37.4 us
    psum x1, blocking collectives, shards(): lax.psum((gain_local, shift_local), ('fsdp', 'tensor'))  37.3 us
  transfers between devices with their start and end apart: 21, of which 12 were waited for; matrix products, arithmetic and copies ran while one was open for 34% of the time, Pallas kernels for 0%

commit v1 on v0

v1 whole, which is shorter than its diff:
```python
import functools

import numpy as np
import jax
import jax.numpy as jnp
from jax import lax
from jax.experimental import pallas as pl
from jax.experimental.pallas import tpu as pltpu
from jax.sharding import PartitionSpec as P

HEAD_DIM = 32
SIDE = 14
WIN = 7
SHIFT = 3
BLOCKS = 2
ADAM_STEP = 10
TOKENS = SIDE * SIDE
WINS = (SIDE // WIN) ** 2
SPAN = WIN * WIN
PAD = 64
IMG_PAD = WINS * PAD
IMG_ROWS = 208
GROUP = 4

NORM_EPS = 1e-05
BETA_ONE = 0.9
BETA_TWO = 0.999
MATRIX_RATE = 0.04
SMALL_RATE = 0.3
WEIGHT_DECAY = 0.05
ADAM_EPS = 1e-08
MASK_FILL = -100.0
KEY_FILL = -1e30
INV_ROOT = HEAD_DIM ** (-0.5)
MIB = 1024 * 1024
F32 = jnp.float32
BF16 = jnp.bfloat16
NT = (((1,), (1,)), ((), ()))
TN = (((0,), (0,)), ((), ()))


def window_source(shifted):
    out = np.zeros((WINS, SPAN), np.int64)
    step = SHIFT if shifted else 0
    per = SIDE // WIN
    for w in range(WINS):
        for p in range(SPAN):
            r = (w // per) * WIN + p // WIN
            c = (w % per) * WIN + p % WIN
            out[w, p] = ((r + step) % SIDE) * SIDE + (c + step) % SIDE
    return out


def image_base(i):
    return (i * TOKENS) // 16 * 16


def permutations(images):
    perm = np.zeros((BLOCKS, images, IMG_PAD, IMG_ROWS), np.float32)
    for b in range(BLOCKS):
        src = window_source(b % 2 == 1)
        for i in range(images):
            off = i * TOKENS - image_base(i)
            for w in range(WINS):
                for p in range(SPAN):
                    perm[b, i, w * PAD + p, off + src[w, p]] = 1.0
    return perm


def mask_table():
    out = np.zeros((BLOCKS, WINS, PAD, PAD), np.float32)
    coords = np.arange(SIDE)
    bands = (coords >= SIDE - WIN).astype(int) + (coords >= SIDE - SHIFT).astype(int)
    region = (bands[:, None] * 3 + bands[None, :]).reshape(-1)
    base = window_source(False)
    for b in range(BLOCKS):
        for w in range(WINS):
            if b % 2 == 1:
                lab = region[base[w]]
                out[b, w, :SPAN, :SPAN] = np.where(lab[:, None] == lab[None, :], 0.0, MASK_FILL)
            out[b, w, SPAN:, :] = KEY_FILL
    return out


def rel_onehot(rels):
    out = np.zeros((rels, PAD, PAD), np.float32)
    pos = np.arange(SPAN)
    row, col = pos // WIN, pos % WIN
    for q in range(SPAN):
        e = (row[q] - row + WIN - 1) * (2 * WIN - 1) + col[q] - col + WIN - 1
        out[e, np.arange(SPAN), q] = 1.0
    return out


def dot(a, b, dims=None):
    if dims is None:
        return jnp.dot(a, b, preferred_element_type=F32)
    return lax.dot_general(a, b, dims, preferred_element_type=F32)


def lane_heads(width):
    return lax.broadcasted_iota(jnp.int32, (1, width), 1) // HEAD_DIM


def spread(rows, heads):
    zero = jnp.zeros_like(rows)
    return jnp.concatenate([jnp.where(heads == h, rows, zero) for h in range(GROUP)], 0)


def gather_diag(prod, heads):
    out = prod[0:PAD]
    for h in range(1, GROUP):
        out = jnp.where(heads == h, prod[h * PAD : (h + 1) * PAD], out)
    return out


def gelu_pair(u):
    au = jnp.abs(u)
    t = 1.0 / (1.0 + (0.3275911 * 0.7071067811865476) * au)
    e = jnp.exp(-0.5 * u * u)
    q = 1.061405429 * 0.5
    q = q * t - 1.453152027 * 0.5
    q = q * t + 1.421413741 * 0.5
    q = q * t - 0.284496736 * 0.5
    q = q * t + 0.254829592 * 0.5
    q = q * t * e
    phi = jnp.where(u >= 0, 1.0 - q, q)
    return u * phi, phi + u * e * 0.3989422804014327


def chunks(rows, size):
    return [(r, min(size, rows - r)) for r in range(0, rows, size)]


def norm_rows(x):
    mean = jnp.mean(x, -1, keepdims=True)
    cen = x - mean
    inv = lax.rsqrt(jnp.mean(cen * cen, -1, keepdims=True) + NORM_EPS)
    return cen * inv, inv


def put_rows(ref, vals):
    images = len(vals)
    for i in range(images):
        base = image_base(i)
        lead = 0
        if i > 0:
            lead = image_base(i - 1) + IMG_ROWS - base
            mix = vals[i - 1][IMG_ROWS - lead :] + vals[i][:lead]
            ref[base : base + lead, :] = mix.astype(ref.dtype)
        end = image_base(i + 1) - base if i + 1 < images else IMG_ROWS
        ref[base + lead : base + end, :] = vals[i][lead:end].astype(ref.dtype)


def norm_into(src, dst, gain, off):
    for r, n in chunks(src.shape[0], 112):
        unit, _ = norm_rows(src[r : r + n, :])
        dst[r : r + n, :] = (unit * gain + off).astype(BF16)


def fold(val):
    rows, cols = val.shape
    return jnp.sum(val.reshape(rows // 8, 8, cols), 0)


def back_norm(src, grad, gain, dst):
    width = src.shape[1]
    sums = [jnp.zeros((8, width), F32) for _ in range(3)]
    for r, n in chunks(src.shape[0], 112):
        unit, inv = norm_rows(src[r : r + n, :])
        gr = grad[r : r + n, :]
        e = gr * gain
        res = dst[r : r + n, :] + inv * (
            e - jnp.mean(e, -1, keepdims=True) - unit * jnp.mean(e * unit, -1, keepdims=True)
        )
        dst[r : r + n, :] = res
        for j, val in enumerate((gr * unit, gr, res)):
            sums[j] = sums[j] + fold(val)
    return [jnp.sum(s, 0, keepdims=True) for s in sums]


def column_sum(ref):
    total = jnp.zeros((8, ref.shape[1]), F32)
    for r, n in chunks(ref.shape[0], 112):
        total = total + fold(ref[r : r + n, :])
    return jnp.sum(total, 0, keepdims=True)


GAIN_ROW = 0
BIAS_ROW = GAIN_ROW + 2 * BLOCKS
QV_ROW = BIAS_ROW + 4 * BLOCKS
HID_ROW = QV_ROW + 2 * BLOCKS


def compute_kernel(
    x_in, ct_in, live, g_hbm, rel_add, mask, gains, offs, qvb, hb, perm, perm_t,
    x_out, dx_out, dg_hbm, dsum, small,
    wt, xs, ms, a_s, aw, qkv, pts, ow, osb, a2, gl, gp, ubuf, acc, dx, cut, awt, dwin, da,
    mlp_st, out_st, att_st, in_sem, out_sem, att_sem,
):
    images = x_in.shape[0]
    groups = wt.shape[1]
    rows, width = xs.shape[1:]
    lanes = GROUP * HEAD_DIM
    hid = gl.shape[3]
    c_out, c_up, c_down = 3 * lanes, 4 * lanes, 4 * lanes + hid
    c_end = c_down + hid
    heads = lane_heads(lanes)
    loads = []
    for b in range(BLOCKS):
        cp = pltpu.make_async_copy(g_hbm.at[b], wt.at[b], in_sem.at[b])
        cp.start()
        loads.append(cp)
    used = images * TOKENS
    floor = used // 8 * 8
    xs[0, floor:rows, :] = jnp.zeros((rows - floor, width), F32)
    dx[floor:rows, :] = jnp.zeros((rows - floor, width), F32)
    for i in range(images):
        xs[0, i * TOKENS : (i + 1) * TOKENS, :] = x_in[i]
        dx[i * TOKENS : (i + 1) * TOKENS, :] = ct_in[i] * live[i]

    for b in range(BLOCKS):
        loads[b].wait()
        off = [offs[b, j : j + 1, :] for j in range(4)]
        off2, off3 = (o.astype(BF16).astype(F32) for o in off[2:])
        norm_into(xs.at[b], a_s, gains[b, 0:1, :], off[0])
        for i in range(images):
            base = image_base(i)
            aw[b, i * IMG_PAD : (i + 1) * IMG_PAD, :] = dot(
                perm[b, i], a_s[base : base + IMG_ROWS, :]
            ).astype(BF16)

        def attend(t, carry):
            rows_qkv = dot(aw[b], wt[b, t, :, 0 : 3 * lanes])
            for j in range(3):
                part = rows_qkv[:, j * lanes : (j + 1) * lanes]
                if j != 1:
                    part = part + qvb[b, j // 2, pl.ds(t, 1), :].astype(BF16).astype(F32)
                qkv[b, t, :, j * lanes : (j + 1) * lanes] = part.astype(BF16)

            def window(w, c2):
                r = pl.multiple_of(w * PAD, PAD)
                q = qkv[b, t, pl.ds(r, PAD), 0:lanes]
                k = qkv[b, t, pl.ds(r, PAD), lanes : 2 * lanes]
                v = qkv[b, t, pl.ds(r, PAD), 2 * lanes : 3 * lanes]
                s = dot(k, spread(q, heads), NT) * INV_ROOT + rel_add[b, t].astype(F32)
                s = s + mask[b, lax.rem(w, WINS)]
                e = jnp.exp(s - jnp.max(s, 0, keepdims=True))
                p = (e * (1.0 / jnp.sum(e, 0, keepdims=True))).astype(BF16)
                pts[b, t, w] = p
                ow[pl.ds(r, PAD), :] = gather_diag(dot(p, v, TN), heads).astype(BF16)
                return c2

            lax.fori_loop(0, images * WINS, window, 0, unroll=2)
            put_rows(
                osb.at[b, t],
                [dot(perm_t[b, i], ow[i * IMG_PAD : (i + 1) * IMG_PAD, :]) for i in range(images)],
            )
            return carry

        lax.fori_loop(0, groups, attend, 0)
        y = dot(osb[b, 0], wt[b, 0, :, c_out:c_up], NT)
        for t in range(1, groups):
            y = y + dot(osb[b, t], wt[b, t, :, c_out:c_up], NT)
        ms[b] = xs[b] + y + off2
        norm_into(ms.at[b], a2.at[b], gains[b, 1:2, :], off[1])
        acc[...] = ms[b] + off3

        def mlp(t, carry):
            ubuf[...] = dot(a2[b], wt[b, t, :, c_up:c_down])
            hbias = hb[b, pl.ds(t, 1), :].astype(BF16).astype(F32)
            for r, n in chunks(rows, 32):
                g, d = gelu_pair(ubuf[r : r + n, :] + hbias)
                gl[b, t, r : r + n, :] = g.astype(BF16)
                gp[b, t, r : r + n, :] = d.astype(BF16)
            acc[...] += dot(gl[b, t], wt[b, t, :, c_down:c_end], NT)
            return carry

        lax.fori_loop(0, groups, mlp, 0)
        if b + 1 < BLOCKS:
            xs[b + 1] = acc[...]
    for i in range(images):
        x_out[i] = acc[i * TOKENS : (i + 1) * TOKENS, :]

    for b in range(BLOCKS - 1, -1, -1):
        small[BIAS_ROW + 4 * b + 3 : BIAS_ROW + 4 * b + 4, :] = column_sum(dx)
        cut[...] = dx[...].astype(BF16)
        dxt = jnp.transpose(cut[...])
        a_t = jnp.transpose(a2[b])
        acc[...] = jnp.zeros_like(acc)

        def mlp_copy(t, slot):
            return pltpu.make_async_copy(
                mlp_st.at[slot], dg_hbm.at[b, t, :, c_up:c_end], out_sem.at[slot]
            )

        def mlp_back(t, carry):
            slot = lax.rem(t, 2)

            @pl.when(t >= 2)
            def _():
                mlp_copy(t - 2, slot).wait()

            mlp_st[slot, :, hid : 2 * hid] = dot(dxt, gl[b, t]).astype(BF16)
            dh = dot(cut[...], wt[b, t, :, c_down:c_end])
            du = (dh * gp[b, t].astype(F32)).astype(BF16)
            gp[b, t] = du
            small[pl.ds(HID_ROW + b * groups + t, 1), :] = jnp.sum(
                fold(du.astype(F32)), 0, keepdims=True
            )
            mlp_st[slot, :, 0:hid] = dot(a_t, du).astype(BF16)
            acc[...] += dot(du, wt[b, t, :, c_up:c_down], NT)
            mlp_copy(t, slot).start()
            return carry

        lax.fori_loop(0, groups, mlp_back, 0)
        for t in range(groups - 2, groups):
            mlp_copy(t, t % 2).wait()
        sums = back_norm(ms.at[b], acc, gains[b, 1:2, :], dx)
        small[GAIN_ROW + 2 * b + 1 : GAIN_ROW + 2 * b + 2, :] = sums[0]
        small[BIAS_ROW + 4 * b + 1 : BIAS_ROW + 4 * b + 2, :] = sums[1]
        small[BIAS_ROW + 4 * b + 2 : BIAS_ROW + 4 * b + 3, :] = sums[2]
        cut[...] = dx[...].astype(BF16)
        dmt = jnp.transpose(cut[...])
        awt[...] = jnp.transpose(aw[b])
        da[...] = jnp.zeros_like(da)
        out_copies = []
        for t in range(groups):
            out_st[t] = dot(dmt, osb[b, t]).astype(BF16)
            cp = pltpu.make_async_copy(out_st.at[t], dg_hbm.at[b, t, :, c_out:c_up], out_sem.at[2 + t])
            cp.start()
            out_copies.append(cp)

        def att_copy(t, slot):
            return pltpu.make_async_copy(
                att_st.at[slot], dg_hbm.at[b, t, :, 0:c_out], att_sem.at[slot]
            )

        def attend_back(t, carry):
            slot = lax.rem(t, 2)

            @pl.when(t >= 2)
            def _():
                att_copy(t - 2, slot).wait()

            do_t = dot(cut[...], wt[b, t, :, c_out:c_up]).astype(BF16)
            for i in range(images):
                base = image_base(i)
                ow[i * IMG_PAD : (i + 1) * IMG_PAD, :] = dot(
                    perm[b, i], do_t[base : base + IMG_ROWS]
                ).astype(BF16)
            dsum[b, t] = jnp.zeros((PAD, GROUP * PAD), F32)

            def window(w, c2):
                r = pl.multiple_of(w * PAD, PAD)
                q = qkv[b, t, pl.ds(r, PAD), 0:lanes]
                k = qkv[b, t, pl.ds(r, PAD), lanes : 2 * lanes]
                v = qkv[b, t, pl.ds(r, PAD), 2 * lanes : 3 * lanes]
                p = pts[b, t, w]
                dob = spread(ow[pl.ds(r, PAD), :], heads)
                dp = dot(v, dob, NT)
                pf = p.astype(F32)
                ds = (pf * (dp - jnp.sum(pf * dp, 0, keepdims=True))).astype(BF16)
                dsum[b, t] += ds.astype(F32)
                dv = dot(p, dob)
                dk = dot(ds, spread(q, heads)) * INV_ROOT
                dq = gather_diag(dot(ds, k, TN), heads) * INV_ROOT
                dwin[pl.ds(r, PAD), 0:lanes] = dq.astype(BF16)
                dwin[pl.ds(r, PAD), lanes : 2 * lanes] = dk.astype(BF16)
                dwin[pl.ds(r, PAD), 2 * lanes : 3 * lanes] = dv.astype(BF16)
                return c2

            lax.fori_loop(0, images * WINS, window, 0, unroll=2)
            col = pl.ds(pl.multiple_of(t * lanes, lanes), lanes)
            for j in range(2):
                val = dwin[:, 2 * j * lanes : (2 * j + 1) * lanes].astype(F32)
                row = QV_ROW + 2 * b + j
                small[row : row + 1, col] = jnp.sum(fold(val), 0, keepdims=True)
            att_st[slot] = dot(awt[...], dwin[...]).astype(BF16)
            da[...] += dot(dwin[...], wt[b, t, :, 0:c_out], NT)
            att_copy(t, slot).start()
            return carry

        lax.fori_loop(0, groups, attend_back, 0)
        vals = []
        for i in range(images):
            part = da[i * IMG_PAD : (i + 1) * IMG_PAD, :]
            high = part.astype(BF16)
            rest = (part - high.astype(F32)).astype(BF16)
            vals.append(dot(perm_t[b, i], high) + dot(perm_t[b, i], rest))
        put_rows(acc, vals)
        sums = back_norm(xs.at[b], acc, gains[b, 0:1, :], dx)
        small[GAIN_ROW + 2 * b : GAIN_ROW + 2 * b + 1, :] = sums[0]
        small[BIAS_ROW + 4 * b : BIAS_ROW + 4 * b + 1, :] = sums[1]
        for cp in out_copies:
            cp.wait()
        for t in range(groups - 2, groups):
            att_copy(t, t % 2).wait()
    for i in range(images):
        dx_out[i] = dx[i * TOKENS : (i + 1) * TOKENS, :]


def compute_call(x, ct, live, gathered, rel_add, gains, offs, qvb, hb):
    images, _, width = x.shape
    groups = gathered.shape[1]
    cols = gathered.shape[3]
    lanes = GROUP * HEAD_DIM
    hid = (cols - 4 * lanes) // 2
    rows = -(-images * TOKENS // 16) * 16
    wrows = images * IMG_PAD
    perm = permutations(images)
    consts = (
        jnp.asarray(np.tile(mask_table(), (1, 1, 1, GROUP))),
        jnp.asarray(perm, BF16),
        jnp.asarray(np.swapaxes(perm, 2, 3), BF16),
    )
    vmem = pl.BlockSpec(memory_space=pltpu.VMEM)
    anyspace = pl.BlockSpec(memory_space=pl.ANY)
    small_rows = HID_ROW + BLOCKS * groups
    return pl.pallas_call(
        compute_kernel,
        out_shape=(
            jax.ShapeDtypeStruct(x.shape, F32),
            jax.ShapeDtypeStruct(x.shape, F32),
            jax.ShapeDtypeStruct(gathered.shape, BF16),
            jax.ShapeDtypeStruct((BLOCKS, groups, PAD, GROUP * PAD), F32),
            jax.ShapeDtypeStruct((small_rows, width), F32),
        ),
        in_specs=[
            vmem, vmem, pl.BlockSpec(memory_space=pltpu.SMEM), anyspace, vmem, vmem, vmem, vmem,
            vmem, vmem, vmem, vmem,
        ],
        out_specs=(vmem, vmem, anyspace, vmem, vmem),
        scratch_shapes=[
            pltpu.VMEM((BLOCKS, groups, width, cols), BF16),
            pltpu.VMEM((BLOCKS, rows, width), F32),
            pltpu.VMEM((BLOCKS, rows, width), F32),
            pltpu.VMEM((rows, width), BF16),
            pltpu.VMEM((BLOCKS, wrows, width), BF16),
            pltpu.VMEM((BLOCKS, groups, wrows, 3 * lanes), BF16),
            pltpu.VMEM((BLOCKS, groups, images * WINS, PAD, GROUP * PAD), BF16),
            pltpu.VMEM((wrows, lanes), BF16),
            pltpu.VMEM((BLOCKS, groups, rows, lanes), BF16),
            pltpu.VMEM((BLOCKS, rows, width), BF16),
            pltpu.VMEM((BLOCKS, groups, rows, hid), BF16),
            pltpu.VMEM((BLOCKS, groups, rows, hid), BF16),
            pltpu.VMEM((rows, hid), F32),
            pltpu.VMEM((rows, width), F32),
            pltpu.VMEM((rows, width), F32),
            pltpu.VMEM((rows, width), BF16),
            pltpu.VMEM((width, wrows), BF16),
            pltpu.VMEM((wrows, 3 * lanes), BF16),
            pltpu.VMEM((wrows, width), F32),
            pltpu.VMEM((2, width, 2 * hid), BF16),
            pltpu.VMEM((groups, width, lanes), BF16),
            pltpu.VMEM((2, width, 3 * lanes), BF16),
            pltpu.SemaphoreType.DMA((BLOCKS,)),
            pltpu.SemaphoreType.DMA((2 + groups,)),
            pltpu.SemaphoreType.DMA((2,)),
        ],
        compiler_params=pltpu.CompilerParams(vmem_limit_bytes=63 * MIB),
    )(x, ct, live, gathered, rel_add, consts[0], gains, offs, qvb, hb, consts[1], consts[2])

MESH = pl.DeviceIdType.MESH


class Digit:
    def __init__(self, name, axis, size, stride, dim):
        self.name, self.axis, self.size, self.stride, self.dim = name, axis, size, stride, dim

    def here(self):
        return lax.rem(lax.axis_index(self.axis) // self.stride, self.size)

    def peer(self, step):
        d = self.here()
        to = lax.rem(d + step, self.size)
        return to, {self.axis: lax.axis_index(self.axis) + (to - d) * self.stride}


def plan(n_fsdp, n_tensor):
    if (n_fsdp, n_tensor) == (8, 4):
        parts = [("x", "tensor", 2), ("core", "tensor", 2), ("z", "fsdp", 4), ("y", "fsdp", 2)]
    elif (n_fsdp, n_tensor) == (32, 4):
        parts = [("x", "tensor", 4), ("z", "fsdp", 4), ("y", "fsdp", 4), ("core", "fsdp", 2)]
    else:
        parts = [("x", "tensor", n_tensor), ("z", "fsdp", n_fsdp)]
    digits = {}
    for dim, (name, axis, size) in enumerate(parts):
        stride = 1
        for _, later_axis, later in parts[dim + 1 :]:
            if later_axis == axis:
                stride *= later
        digits[name] = Digit(name, axis, size, stride, dim)
    return digits


def orders(digits):
    one = [n for n in ("z", "x", "y", "core") if n in digits]
    two = [n for n in ("z", "y", "x", "core") if n in digits]
    return [[digits[n] for n in one], [digits[n] for n in two]]


def greet(peers):
    barrier = pltpu.get_barrier_semaphore()
    for device in peers:
        pl.semaphore_signal(barrier, inc=1, device_id=device, device_id_type=MESH)
    pl.semaphore_wait(barrier, len(peers))


def tensor_peers(n_tensor):
    t = lax.axis_index("tensor")
    return [{"tensor": lax.rem(t + s, n_tensor)} for s in range(1, n_tensor)]


def all_peers(digits, n_tensor):
    peers = [d.peer(s)[1] for d in digits.values() if d.axis == "fsdp" for s in range(1, d.size)]
    return peers + tensor_peers(n_tensor)


def pieces(cols, width):
    return [(c, min(width, cols - c)) for c in range(0, cols, width)]


def gather_kernel(n_fsdp, n_tensor, half, own, side, full, sides, local_sem, send, recv, side_send, side_recv):
    digits = plan(n_fsdp, n_tensor)
    dims = sorted(digits.values(), key=lambda d: d.dim)
    greet(all_peers(digits, n_tensor))
    t = lax.axis_index("tensor")
    mine = tuple(d.here() for d in dims)
    local = pltpu.make_async_copy(side, sides.at[t], local_sem.at[0])
    local.start()
    side_copies = []
    for j, device in enumerate(tensor_peers(n_tensor)):
        side_copies.append(pltpu.make_async_remote_copy(
            src_ref=side, dst_ref=sides.at[t], send_sem=side_send.at[j], recv_sem=side_recv.at[j],
            device_id=device, device_id_type=MESH))
    local_own = []
    for b in range(BLOCKS):
        cp = pltpu.make_async_copy(own.at[b], full.at[(b,) + mine], local_sem.at[1 + b])
        cp.start()
        local_own.append(cp)
    jobs = []
    for b in range(BLOCKS):
        for k, (c, n) in enumerate(pieces(own.shape[3 - 1], half)):
            jobs.append((b, c, n, orders(digits)[k % 2]))
    count = [0]
    started = []

    def launch(job, phase):
        b, c, n, order = job
        done = order[:phase]
        digit = order[phase]
        index = tuple(slice(None) if d in done else d.here() for d in dims)
        cols = pl.ds(c, n)
        copies = []
        for s in range(1, digit.size):
            _, device = digit.peer(s)
            dst = full.at[(b,) + index + (slice(None), cols)]
            src = own.at[b, :, cols] if phase == 0 else dst
            i = count[0]
            count[0] += 1
            copies.append(pltpu.make_async_remote_copy(
                src_ref=src, dst_ref=dst, send_sem=send.at[i], recv_sem=recv.at[i],
                device_id=device, device_id_type=MESH))
        for cp in copies:
            cp.start()
        started.extend(copies)
        return copies

    last = {}
    for j, job in enumerate(jobs):
        last[j] = launch(job, 0)
        if j == 1:
            for cp in side_copies:
                cp.start()
    for cp in local_own:
        cp.wait()
    phases = len(digits)
    pairs = len(jobs) // 2
    for step in range(pairs + phases - 1):
        for phase in range(phases - 1, 0, -1):
            pair = step - (phase - 1)
            if 0 <= pair < pairs:
                for j in (2 * pair, 2 * pair + 1):
                    for cp in last[j]:
                        cp.wait_recv()
                    last[j] = launch(jobs[j], phase)
    for j in range(len(jobs)):
        for cp in last[j]:
            cp.wait_recv()
    for cp in started:
        cp.wait_send()
    local.wait()
    for cp in side_copies:
        cp.wait()


def gather_call(own, side, n_fsdp, n_tensor, half=256):
    digits = plan(n_fsdp, n_tensor)
    sizes = tuple(d.size for d in sorted(digits.values(), key=lambda d: d.dim))
    total = sum(d.size - 1 for d in digits.values()) * BLOCKS * len(pieces(own.shape[2], half))
    anyspace = pl.BlockSpec(memory_space=pl.ANY)
    full, sides = pl.pallas_call(
        functools.partial(gather_kernel, n_fsdp, n_tensor, half),
        out_shape=(
            jax.ShapeDtypeStruct((BLOCKS,) + sizes + own.shape[1:], own.dtype),
            jax.ShapeDtypeStruct((n_tensor,) + side.shape, side.dtype),
        ),
        in_specs=[anyspace, anyspace],
        out_specs=(anyspace, anyspace),
        scratch_shapes=[
            pltpu.SemaphoreType.DMA((1 + BLOCKS,)),
            pltpu.SemaphoreType.DMA((total,)),
            pltpu.SemaphoreType.DMA((total,)),
            pltpu.SemaphoreType.DMA((n_tensor - 1,)),
            pltpu.SemaphoreType.DMA((n_tensor - 1,)),
        ],
        compiler_params=pltpu.CompilerParams(collective_id=0, has_side_effects=True),
    )(own, side)
    return full.reshape(BLOCKS, n_tensor, n_fsdp * own.shape[1], own.shape[2]), sides


def adam(weight, first, second, grad, rate, decay):
    first_new = BETA_ONE * first + (1.0 - BETA_ONE) * grad
    second_new = BETA_TWO * second + (1.0 - BETA_TWO) * grad * grad
    first_hat = first_new * (1.0 / (1.0 - BETA_ONE**ADAM_STEP))
    second_hat = second_new * (1.0 / (1.0 - BETA_TWO**ADAM_STEP))
    step = first_hat / (jnp.sqrt(second_hat) + ADAM_EPS)
    if decay:
        step = step + decay * weight
    return weight - rate * step, first_new, second_new


def pick(index, values):
    out = values[0]
    for i in range(1, len(values)):
        out = jnp.where(index == i, values[i], out)
    return out


def rel_row(groups):
    return HID_ROW + BLOCKS * groups


def reduce_jobs(digits, cols, half):
    jobs = []
    for b in range(BLOCKS - 1, -1, -1):
        for k, (c, n) in reversed(list(enumerate(pieces(cols, half)))):
            jobs.append((b, c, n, orders(digits)[k % 2][::-1], k % 2))
    return jobs


def stage_shapes(digits, rows, half, count):
    dims = sorted(digits.values(), key=lambda d: d.dim)
    shapes = []
    for order in orders(digits):
        order = order[::-1]
        for phase, digit in enumerate(order):
            left = tuple(d.size for d in dims if d not in order[: phase + 1])
            slots = digit.size if phase == len(order) - 1 else digit.size - 1
            shapes.append((-(-count // 2), slots) + left + (rows, half))
    return shapes


def reduce_kernel(n_fsdp, n_tensor, half, *refs):
    digits = plan(n_fsdp, n_tensor)
    dims = sorted(digits.values(), key=lambda d: d.dim)
    grads, small = refs[0], refs[1]
    params = [refs[2 + 3 * j : 5 + 3 * j] for j in range(9)]
    outs = [refs[29 + 3 * j : 32 + 3 * j] for j in range(9)]
    acc, local_sem, send, recv = refs[56:60]
    phases = len(digits)
    stage = [refs[60 + j * phases : 60 + (j + 1) * phases] for j in range(2)]
    small_slots = refs[60 + 2 * phases : 60 + 3 * phases]
    total = refs[60 + 3 * phases]
    rows = acc.shape[-2]
    lanes = GROUP * HEAD_DIM
    count = [0]
    started = []

    def remote(src, dst, device):
        i = count[0]
        count[0] += 1
        cp = pltpu.make_async_remote_copy(
            src_ref=src, dst_ref=dst, send_sem=send.at[i], recv_sem=recv.at[i],
            device_id=device, device_id_type=MESH)
        started.append(cp)
        return cp

    jobs = reduce_jobs(digits, acc.shape[-1], half)
    core = jobs[0][3][0]
    local = []
    for b in range(BLOCKS):
        index = tuple(core.here() if d is core else slice(None) for d in dims)
        cp = pltpu.make_async_copy(grads.at[(b,) + index], acc.at[b], local_sem.at[b])
        cp.start()
        local.append(cp)
    greet(all_peers(digits, n_tensor))
    reduced = [d for d in dims if d is not core]

    def launch(j, phase):
        b, c, n, order, kind = jobs[j]
        digit = order[phase]
        cols = pl.ds(c, n)
        copies = []
        for s in range(1, digit.size):
            to, device = digit.peer(s)
            if phase == 0:
                index = tuple(to if d is digit else slice(None) for d in dims)
                src = grads.at[(b,) + index + (slice(None), cols)]
            else:
                index = tuple(
                    to if d is digit else d.here() if d in order[:phase] else slice(None)
                    for d in reduced
                )
                src = acc.at[(b,) + index + (slice(None), cols)]
            slot = digit.here() if phase == phases - 1 else s - 1
            dst = stage[kind][phase].at[j // 2, slot]
            copies.append(remote(src, dst, device))
        for cp in copies:
            cp.start()
        return copies

    def absorb(j, phase):
        b, c, n, order, kind = jobs[j]
        digit = order[phase]
        cols = pl.ds(c, n)
        left = [d for d in reduced if d not in order[: phase + 1]]
        land = stage[kind][phase]
        steps = int(np.prod([d.size for d in left])) if left else 1

        def one(i, carry):
            place = {}
            rest = i
            for d in reversed(left):
                place[d.name] = lax.rem(rest, d.size)
                rest = rest // d.size
            index = (b,) + tuple(place[d.name] if d in left else d.here() for d in reduced)
            value = acc[index + (slice(None), cols)]
            for s in range(digit.size - 1):
                value = value + land[(j // 2, s) + tuple(place[d.name] for d in left)]
            acc[index + (slice(None), cols)] = value
            return carry

        lax.fori_loop(0, steps, one, 0)

    def finish(j):
        b, c, n, order, way = jobs[j]
        digit = order[-1]
        index = (b,) + tuple(d.here() for d in reduced)
        land = stage[way][phases - 1]
        land[j // 2, digit.here()] = acc[index + (slice(None), pl.ds(c, n))]
        grad = land[j // 2, 0].astype(F32)
        for s in range(1, digit.size):
            grad = grad + land[j // 2, s].astype(F32)
        for u in range(0, n, lanes):
            unit = (c + u) // lanes
            part = grad[:, u : u + lanes]
            if unit < 3:
                kind, place = 0, (b, slice(None), unit)
            elif unit == 3:
                kind, place, part = 1, (b,), jnp.transpose(part)
            else:
                hid = params[2][0].shape[2]
                at = c + u - 4 * lanes
                if at < hid:
                    kind, place = 2, (b, slice(None), slice(at, at + lanes))
                else:
                    kind, place, part = 3, (b, slice(at - hid, at - hid + lanes)), jnp.transpose(part)
            new = adam(*(p[place] for p in params[kind]), part, MATRIX_RATE, WEIGHT_DECAY)
            for ref, val in zip(outs[kind], new):
                ref[place] = val

    small_order = [digits[n] for n in ("core", "y", "x", "z") if n in digits]

    def small_launch(phase):
        digit = small_order[phase]
        copies = []
        for s in range(1, digit.size):
            _, device = digit.peer(s)
            place = small_slots[phase].at[digit.here()]
            copies.append(remote(place, place, device))
        for cp in copies:
            cp.start()
        return copies

    small_slots[0][small_order[0].here()] = small[...]
    last = {}
    last["small"] = small_launch(0)
    for j in range(len(jobs)):
        last[j] = launch(j, 0)
    for cp in local:
        cp.wait()
    pairs = len(jobs) // 2
    for step in range(pairs + phases - 1):
        if 0 < step <= phases:
            for cp in last["small"]:
                cp.wait_recv()
            digit = small_order[step - 1]
            value = small_slots[step - 1][0]
            for s in range(1, digit.size):
                value = value + small_slots[step - 1][s]
            if step < phases:
                small_slots[step][small_order[step].here()] = value
                last["small"] = small_launch(step)
            else:
                total[...] = value
        for phase in range(phases - 1, -1, -1):
            pair = step - phase
            if 0 <= pair < pairs:
                for j in (2 * pair, 2 * pair + 1):
                    for cp in last[j]:
                        cp.wait_recv()
                    if phase < phases - 1:
                        absorb(j, phase)
                        last[j] = launch(j, phase + 1)
                    else:
                        finish(j)
    t = lax.axis_index("tensor")
    groups = n_tensor
    width = total.shape[1]
    for b in range(BLOCKS):
        heads = params[4][0].shape[1]
        rels = params[4][0].shape[2]
        at = rel_row(groups) + b * heads * groups
        hid_at = HID_ROW + b * groups
        work = [
            (4, (b,), pick(t, [total[at + i * heads : at + (i + 1) * heads, 0:rels] for i in range(groups)])),
            (5, (b,), total[QV_ROW + 2 * b : QV_ROW + 2 * b + 2, pl.ds(pl.multiple_of(t * lanes, lanes), lanes)]),
            (6, (slice(b, b + 1),), pick(t, [total[hid_at + i : hid_at + i + 1, :] for i in range(groups)])),
            (7, (b,), total[GAIN_ROW + 2 * b : GAIN_ROW + 2 * b + 2, :]),
            (8, (b,), total[BIAS_ROW + 4 * b : BIAS_ROW + 4 * b + 4, :]),
        ]
        for kind, place, grad in work:
            new = adam(*(p[place] for p in params[kind]), grad, SMALL_RATE, 0.0)
            for ref, val in zip(outs[kind], new):
                ref[place] = val
    for cp in started:
        cp.wait_send()


def reduce_call(grads, small, params, n_fsdp, n_tensor, half=256):
    digits = plan(n_fsdp, n_tensor)
    dims = sorted(digits.values(), key=lambda d: d.dim)
    sizes = tuple(d.size for d in dims)
    rows = grads.shape[2] // n_fsdp
    cols = grads.shape[3]
    grads = grads.reshape((BLOCKS,) + sizes + (rows, cols))
    count = len(reduce_jobs(digits, cols, half))
    total = sum(d.size - 1 for d in digits.values()) * (count + 1)
    small_order = [digits[n] for n in ("core", "y", "x", "z") if n in digits]
    core = orders(digits)[0][-1]
    acc_shape = (BLOCKS,) + tuple(d.size for d in dims if d is not core) + (rows, cols)
    vmem = pl.BlockSpec(memory_space=pltpu.VMEM)
    flat = [p for group in params for p in group]
    return pl.pallas_call(
        functools.partial(reduce_kernel, n_fsdp, n_tensor, half),
        out_shape=tuple(jax.ShapeDtypeStruct(p.shape, p.dtype) for p in flat),
        in_specs=[pl.BlockSpec(memory_space=pl.ANY)] + [vmem] * (1 + len(flat)),
        out_specs=tuple(vmem for _ in flat),
        scratch_shapes=[
            pltpu.VMEM(acc_shape, BF16),
            pltpu.SemaphoreType.DMA((BLOCKS,)),
            pltpu.SemaphoreType.DMA((total,)),
            pltpu.SemaphoreType.DMA((total,)),
        ]
        + [pltpu.VMEM(s, BF16) for s in stage_shapes(digits, rows, half, count)]
        + [pltpu.VMEM((d.size,) + small.shape, F32) for d in small_order]
        + [pltpu.VMEM(small.shape, F32)],
        compiler_params=pltpu.CompilerParams(
            collective_id=1, has_side_effects=True, vmem_limit_bytes=60 * MIB
        ),
    )(grads, small, *flat)


def shards(n_fsdp, n_tensor, *args):
    image_rows, cotangent, live_counts = args[:3]
    qkv, out, up, down, rel, qv, hidden, gain, bias = [args[3 + 3 * j : 6 + 3 * j] for j in range(9)]
    images = image_rows.shape[0]
    slots = lax.axis_index("tensor") * images + jnp.arange(images, dtype=jnp.int32)
    live = (slots < live_counts[0]).astype(F32)
    own = jnp.concatenate(
        [
            qkv[0].reshape(BLOCKS, qkv[0].shape[1], -1).astype(BF16),
            jnp.swapaxes(out[0], 1, 2).astype(BF16),
            up[0].astype(BF16),
            jnp.swapaxes(down[0], 1, 2).astype(BF16),
        ],
        2,
    )
    heads, rels = rel[0].shape[1:]
    onehot = jnp.asarray(rel_onehot(rels).reshape(rels, -1), BF16)
    rel_own = lax.dot_general(
        rel[0].astype(BF16), onehot, (((2,), (0,)), ((), ())), preferred_element_type=F32
    )
    rel_own = rel_own.reshape(BLOCKS, heads, PAD, PAD).swapaxes(1, 2).reshape(BLOCKS * PAD, heads * PAD)
    hid = hidden[0].shape[1]
    tail = jnp.concatenate(
        [jnp.pad(qv[0].reshape(2 * BLOCKS, -1), ((0, 0), (0, hid - qv[0].shape[2]))), hidden[0],
         jnp.zeros((8 - 3 * BLOCKS, hid), F32)], 0)
    side = jnp.concatenate([jnp.pad(rel_own, ((0, 0), (0, hid - rel_own.shape[1]))), tail], 0)
    full, sides = gather_call(own, side, n_fsdp, n_tensor)
    rel_add = sides[:, : BLOCKS * PAD, : heads * PAD].reshape(n_tensor, BLOCKS, PAD, heads * PAD)
    rel_add = rel_add.swapaxes(0, 1)
    tail = sides[:, BLOCKS * PAD :]
    qvb = tail[:, : 2 * BLOCKS, : qv[0].shape[2]].reshape(n_tensor, BLOCKS, 2, -1).transpose(1, 2, 0, 3)
    hb = tail[:, 2 * BLOCKS : 3 * BLOCKS].swapaxes(0, 1)
    x_out, dx_out, grads, dsum, small = compute_call(
        image_rows, cotangent, live, full, rel_add, gain[0], bias[0], qvb, hb
    )
    table = dsum.reshape(BLOCKS, n_tensor, PAD, heads, PAD).transpose(0, 1, 3, 2, 4)
    table = jnp.dot(
        table.reshape(BLOCKS * n_tensor * heads, PAD * PAD),
        jnp.asarray(rel_onehot(rels).reshape(rels, -1).T),
        precision=lax.Precision.HIGHEST,
    )
    small = jnp.concatenate([small, jnp.pad(table, ((0, 0), (0, small.shape[1] - rels)))], 0)
    new = reduce_call(grads, small, (qkv, out, up, down, rel, qv, hidden, gain, bias), n_fsdp, n_tensor)
    return (x_out, dx_out) + tuple(new)


def solution(mesh):
    n_fsdp, n_tensor = mesh.shape["fsdp"], mesh.shape["tensor"]
    tokens = P(("fsdp", "tensor"), None, None)
    kinds = (
        P(None, "fsdp", None, "tensor"), P(None, "tensor", "fsdp"), P(None, "fsdp", "tensor"),
        P(None, "tensor", "fsdp"), P(None, "tensor", None), P(None, None, "tensor"),
        P(None, "tensor"), P(), P(),
    )
    thrice = tuple(k for k in kinds for _ in range(3))
    return jax.shard_map(
        functools.partial(shards, n_fsdp, n_tensor),
        mesh=mesh,
        in_specs=(tokens, tokens, P("fsdp")) + thrice,
        out_specs=(tokens, tokens) + thrice,
        check_vma=False,
    )
```

time: 1330 us -> 340 us (0.26)
  blocking collectives: 503 us -> 0 us
  local copies, waits for them, and re-layouts: 384 us -> 36.6 us
  Pallas kernels: 0 us -> 292 us
  waiting for transfers between devices: 197 us -> 0 us
  matrix products: 134 us -> 6.3 us
  other arithmetic: 71.2 us -> 2.8 us
  between operations: 18.2 us -> 1.67 us
    unnamed x7 -> x0, blocking collectives: 364 us -> none
    pallas_call x0 -> x3, Pallas kernels: none -> 292 us  [the longest x1 127 us: compute_call(): pl.pallas_call(compute_kernel, out_shape=(jax.ShapeDtypeStruct(x.shape, F...]
    all_gather x10 -> x0, waiting for transfers between devices: 192 us -> none  [the longest x2 51.4 us: shards(): normed_two_all = lax.all_gather(normed_two, 'tensor', axis=0, tiled=True)]
    reshape x36 -> x7, local copies, waits for them, and re-layouts: 132 us -> 3.43 us  [the longest x2 1.61 us: shards(): dsum.reshape(BLOCKS, n_tensor, PAD, heads, PAD).transpose(0, 1, 3, 2, 4)]
    dot_general x40 -> x2, matrix products: 134 us -> 6.3 us  [the longest x1 4.59 us: shards(): jnp.dot(table.reshape(BLOCKS * n_tensor * heads, PAD * PAD), jnp.asarray(...]
    psum x2 -> x0, blocking collectives: 74.7 us -> none  [the longest x1 37.4 us: shards(): lax.psum((table_local, qv_local, hidden_local), 'fsdp')]
    all_gather x2 -> x0, blocking collectives: 64.3 us -> none  [the longest x1 32.5 us: shards(): lax.all_gather(out_weight.astype(jnp.bfloat16), 'fsdp', axis=2, tiled=True)]
    concatenate x12 -> x1, local copies, waits for them, and re-layouts: 53.2 us -> 0.08 us  [shards(): jnp.concatenate([jnp.pad(rel_own, ((0, 0), (0, hid - rel_own.shape[1]))),...]
  transfers between devices with their start and end apart: 21 -> 0, of which waited for: 12 -> 0; matrix products, arithmetic and copies ran while one was open for 34% -> 0% of each run, Pallas kernels for 0% -> 0%
where the time goes in v1:
time: 340 us
  Pallas kernels  292 us (86%)
  local copies, waits for them, and re-layouts  36.6 us (11%)
  matrix products  6.3 us (2%)
    pallas_call x1, Pallas kernels, compute_call(): pl.pallas_call(compute_kernel, out_shape=(jax.ShapeDtypeStruct(x.shape, F...  127 us
    pallas_call x1, Pallas kernels, gather_call(): pl.pallas_call(functools.partial(gather_kernel, n_fsdp, n_tensor, half),...  87.6 us
    pallas_call x1, Pallas kernels, reduce_call(): pl.pallas_call(functools.partial(reduce_kernel, n_fsdp, n_tensor, half),...  78.2 us
    unnamed x112, local copies, waits for them, and re-layouts  28.1 us

profile of v1, /device:TPU:0, one launch (start us, length us, event | category | flops | bytes accessed | tf_op | source)
XLA Modules:
  0.0 339.8 jit_solution(8152373611593649012)
XLA Ops:
  0.7 1.7 convolution_bitcast_fusion
  3.1 0.8 fusion.1.side
  4.0 0.8 pad_maximum_fusion.own
  4.8 87.6 %shard_map.554 = (bf16[2,2,2,4,2,64,1536]{6,5,4,3,2,1,0:T(8,128)(2,1)}, f32[4,136,512]{2,1,0:T(8,128)}) custom-call(bf16[2,64,1536]{2,1,0:T(8,128)(2,1)} %pad_maximum_fusion.own, f32[136,512]{1,0:T(8,128)} %fusion.1.side), custom_call_target="tpu_custom_call" | custom-call | tf_op jit(solution)/shard_map/pallas_call | solution.py:603
  92.3 2.0 copy.114
  94.9 1.1 slice.12
  96.0 0.9 copy.140
  96.9 0.7 slice.13
  99.4 126.7 %shard_map.555 = (f32[3,196,512]{2,1,0:T(8,128)}, f32[3,196,512]{2,1,0:T(8,128)}, bf16[2,4,512,1536]{3,2,1,0:T(8,128)(2,1)}, f32[2,4,64,256]{3,2,1,0:T(8,128)}, f32[24,512]{1,0:T(8,128)}) custom-call(f32[3,196,512]{2,1,0:T(8,128)} %x_in.1, f32[3,196,512]{2,1,0:T(8,128)} %ct_in.1, f32[3]{0:T(128)} %compare_convert_fusion.live, ...), custom_call_target="tpu_custom_call" | custom-call | tf_op jit(solution)/shard_map/pallas_call | solution.py:420
  226.1 1.5 reshape.94
  228.1 4.6 %fusion.4 = f32[32,169]{1,0:T(8,128)S(1)} fusion(f32[32,4096]{1,0:T(8,128)S(1)} %reshape.95, f32[4096,169]{0,1:T(8,128)} %constant.24.clone), kind=kOutput, calls=%fused_computation.21 | convolution fusion | flops 265814016 | bytes 3314816 | tf_op jit(solution)/shard_map/dot_general | solution.py:912
  233.4 1.0 copy.122.refs_11_
  234.4 1.0 copy.123.refs_12_
  235.4 1.0 copy.124.refs_13_
  236.4 0.8 copy.116.refs_2_
  237.3 0.8 copy.117.refs_3_
  238.1 0.8 copy.118.refs_4_
  239.0 0.8 copy.119.refs_5_
  239.7 0.8 copy.120.refs_6_
  240.5 0.8 copy.121.refs_7_
  241.2 78.2 %shard_map.556 = (f32[2,64,3,128]{3,2,1,0:T(4,128)}, f32[2,64,3,128]{3,2,1,0:T(4,128)}, f32[2,64,3,128]{3,2,1,0:T(4,128)}, f32[2,128,64]{2,1,0:T(8,128)}, f32[2,...) custom-call(bf16[2,2,2,4,2,64,1536]{6,5,4,3,2,1,0:T(8,128)(2,1)} %bi, ...), custom_call_target="tpu_custom_call" | custom-call | tf_op jit(solution)/shard_map/pallas_call | solution.py:856
  319.4 2.0 copy.131
  321.5 2.0 copy.132
  323.5 0.9 copy.133
  (115 shorter events, 19.0 us)
Async XLA Ops:
  228.1 6.3 %copy-start.4 = (f32[2,512,64]{1,2,0:T(8,128)S(1)}, f32[2,512,64]{1,2,0:T(8,128)}, u32[]{:S(2)}) copy-start(f32[2,512,64]{1,2,0:T(8,128)} %param.48) | copy-start | bytes 786436
  234.4 5.3 %copy-start.18 = (f32[2,128,64]{1,2,0:T(8,128)S(1)}, f32[2,128,64]{1,2,0:T(8,128)}, u32[]{:S(2)}) copy-start(f32[2,128,64]{1,2,0:T(8,128)} %param.42) | copy-start | bytes 196612
  235.4 5.0 %copy-start.19 = (f32[2,128,64]{1,2,0:T(8,128)S(1)}, f32[2,128,64]{1,2,0:T(8,128)}, u32[]{:S(2)}) copy-start(f32[2,128,64]{1,2,0:T(8,128)} %param.43) | copy-start | bytes 196612
  319.4 5.6 %copy-start.7 = (f32[2,64,3,128]{3,2,1,0:T(4,128)S(1)}, f32[2,64,3,128]{3,2,1,0:T(4,128)}, u32[]{:S(2)}) copy-start(f32[2,64,3,128]{3,2,1,0:T(4,128)} %get-tuple-element.158) | copy-start | bytes 589828
  321.5 5.1 %copy-start.17 = (f32[2,128,64]{2,1,0:T(8,128)S(1)}, f32[2,128,64]{2,1,0:T(8,128)}, u32[]{:S(2)}) copy-start(f32[2,128,64]{2,1,0:T(8,128)} %get-tuple-element.160) | copy-start | bytes 196612
  321.5 5.8 %copy-start.16 = (f32[2,128,64]{2,1,0:T(8,128)S(1)}, f32[2,128,64]{2,1,0:T(8,128)}, u32[]{:S(2)}) copy-start(f32[2,128,64]{2,1,0:T(8,128)} %get-tuple-element.161) | copy-start | bytes 196612
  323.5 5.3 %copy-start.12 = (f32[2,64,512]{2,1,0:T(8,128)S(1)}, f32[2,64,512]{2,1,0:T(8,128)}, u32[]{:S(2)}) copy-start(f32[2,64,512]{2,1,0:T(8,128)} %get-tuple-element.221) | copy-start | bytes 786436
  324.3 5.1 %copy-start.11 = (f32[2,64,512]{2,1,0:T(8,128)S(1)}, f32[2,64,512]{2,1,0:T(8,128)}, u32[]{:S(2)}) copy-start(f32[2,64,512]{2,1,0:T(8,128)} %get-tuple-element.222) | copy-start | bytes 786436
  324.4 5.8 %copy-start.10 = (f32[2,64,512]{2,1,0:T(8,128)S(1)}, f32[2,64,512]{2,1,0:T(8,128)}, u32[]{:S(2)}) copy-start(f32[2,64,512]{2,1,0:T(8,128)} %get-tuple-element.223) | copy-start | bytes 786436
  325.7 5.1 %copy-start.31 = (f32[2,4,169]{2,1,0:T(4,128)S(1)}, f32[2,4,169]{2,1,0:T(4,128)}, u32[]{:S(2)}) copy-start(f32[2,4,169]{2,1,0:T(4,128)} %get-tuple-element.227) | copy-start | bytes 16228
  325.7 5.7 %copy-start.30 = (f32[2,4,169]{2,1,0:T(4,128)S(1)}, f32[2,4,169]{2,1,0:T(4,128)}, u32[]{:S(2)}) copy-start(f32[2,4,169]{2,1,0:T(4,128)} %get-tuple-element.228) | copy-start | bytes 16228
  325.7 6.3 %copy-start.29 = (f32[2,4,169]{2,1,0:T(4,128)S(1)}, f32[2,4,169]{2,1,0:T(4,128)}, u32[]{:S(2)}) copy-start(f32[2,4,169]{2,1,0:T(4,128)} %get-tuple-element.229) | copy-start | bytes 16228
  325.7 6.9 %copy-start.37 = (f32[2,2,128]{2,1,0:T(2,128)S(1)}, f32[2,2,128]{2,1,0:T(2,128)}, u32[]{:S(2)}) copy-start(f32[2,2,128]{2,1,0:T(2,128)} %get-tuple-element.230) | copy-start | bytes 6148
  325.7 7.5 %copy-start.36 = (f32[2,2,128]{2,1,0:T(2,128)S(1)}, f32[2,2,128]{2,1,0:T(2,128)}, u32[]{:S(2)}) copy-start(f32[2,2,128]{2,1,0:T(2,128)} %get-tuple-element.231) | copy-start | bytes 6148
  325.8 8.0 %copy-start.35 = (f32[2,2,128]{2,1,0:T(2,128)S(1)}, f32[2,2,128]{2,1,0:T(2,128)}, u32[]{:S(2)}) copy-start(f32[2,2,128]{2,1,0:T(2,128)} %get-tuple-element.232) | copy-start | bytes 6148
  325.8 8.6 %copy-start.34 = (f32[2,512]{1,0:T(2,128)S(1)}, f32[2,512]{1,0:T(2,128)}, u32[]{:S(2)}) copy-start(f32[2,512]{1,0:T(2,128)} %get-tuple-element.233) | copy-start | bytes 12292
  325.8 9.2 %copy-start.33 = (f32[2,512]{1,0:T(2,128)S(1)}, f32[2,512]{1,0:T(2,128)}, u32[]{:S(2)}) copy-start(f32[2,512]{1,0:T(2,128)} %get-tuple-element.234) | copy-start | bytes 12292
  325.8 9.8 %copy-start.32 = (f32[2,512]{1,0:T(2,128)S(1)}, f32[2,512]{1,0:T(2,128)}, u32[]{:S(2)}) copy-start(f32[2,512]{1,0:T(2,128)} %get-tuple-element.235) | copy-start | bytes 12292
  325.8 10.4 %copy-start.28 = (f32[2,2,512]{2,1,0:T(2,128)S(1)}, f32[2,2,512]{2,1,0:T(2,128)}, u32[]{:S(2)}) copy-start(f32[2,2,512]{2,1,0:T(2,128)} %get-tuple-element.236) | copy-start | bytes 24580
  325.8 11.0 %copy-start.27 = (f32[2,2,512]{2,1,0:T(2,128)S(1)}, f32[2,2,512]{2,1,0:T(2,128)}, u32[]{:S(2)}) copy-start(f32[2,2,512]{2,1,0:T(2,128)} %get-tuple-element.237) | copy-start | bytes 24580
  325.8 11.5 %copy-start.26 = (f32[2,2,512]{2,1,0:T(2,128)S(1)}, f32[2,2,512]{2,1,0:T(2,128)}, u32[]{:S(2)}) copy-start(f32[2,2,512]{2,1,0:T(2,128)} %get-tuple-element.238) | copy-start | bytes 24580
  325.8 12.1 %copy-start.24 = (f32[2,4,512]{2,1,0:T(4,128)S(1)}, f32[2,4,512]{2,1,0:T(4,128)}, u32[]{:S(2)}) copy-start(f32[2,4,512]{2,1,0:T(4,128)} %get-tuple-element.239) | copy-start | bytes 49156
  325.8 12.7 %copy-start.23 = (f32[2,4,512]{2,1,0:T(4,128)S(1)}, f32[2,4,512]{2,1,0:T(4,128)}, u32[]{:S(2)}) copy-start(f32[2,4,512]{2,1,0:T(4,128)} %get-tuple-element.240) | copy-start | bytes 49156
  325.8 13.3 %copy-start.22 = (f32[2,4,512]{2,1,0:T(4,128)S(1)}, f32[2,4,512]{2,1,0:T(4,128)}, u32[]{:S(2)}) copy-start(f32[2,4,512]{2,1,0:T(4,128)} %get-tuple-element.241) | copy-start | bytes 49156
  (14 other events, 45.4 us)

commit v2 on v1

v2 whole, which is shorter than its diff:
```python
import functools
import numpy as np
import jax
import jax.numpy as jnp
from jax import lax
from jax.experimental import pallas as pl
from jax.experimental.pallas import tpu as pltpu
from jax.sharding import PartitionSpec as P
HEAD_DIM = 32
SIDE = 14
WIN = 7
SHIFT = 3
BLOCKS = 2
ADAM_STEP = 10
TOKENS = SIDE * SIDE
WINS = (SIDE // WIN) ** 2
SPAN = WIN * WIN
PAD = 64
IMG_PAD = WINS * PAD
IMG_ROWS = 208
GROUP = 4
NORM_EPS = 1e-05
BETA_ONE = 0.9
BETA_TWO = 0.999
MATRIX_RATE = 0.04
SMALL_RATE = 0.3
WEIGHT_DECAY = 0.05
ADAM_EPS = 1e-08
MASK_FILL = -100.0
KEY_FILL = -1e30
INV_ROOT = HEAD_DIM ** (-0.5)
MIB = 1024 * 1024
F32 = jnp.float32
BF16 = jnp.bfloat16
NT = (((1,), (1,)), ((), ()))
TN = (((0,), (0,)), ((), ()))


def window_source(shifted):
    out = np.zeros((WINS, SPAN), np.int64)
    step = SHIFT if shifted else 0
    per = SIDE // WIN
    for w in range(WINS):
        for p in range(SPAN):
            r = (w // per) * WIN + p // WIN
            c = (w % per) * WIN + p % WIN
            out[w, p] = ((r + step) % SIDE) * SIDE + (c + step) % SIDE
    return out


def image_base(i):
    return (i * TOKENS) // 16 * 16


def permutations(images):
    perm = np.zeros((BLOCKS, images, IMG_PAD, IMG_ROWS), np.float32)
    for b in range(BLOCKS):
        src = window_source(b % 2 == 1)
        for i in range(images):
            off = i * TOKENS - image_base(i)
            for w in range(WINS):
                for p in range(SPAN):
                    perm[b, i, w * PAD + p, off + src[w, p]] = 1.0
    return perm


def mask_table():
    out = np.zeros((BLOCKS, WINS, PAD, PAD), np.float32)
    coords = np.arange(SIDE)
    bands = (coords >= SIDE - WIN).astype(int) + (coords >= SIDE - SHIFT).astype(int)
    region = (bands[:, None] * 3 + bands[None, :]).reshape(-1)
    base = window_source(False)
    for b in range(BLOCKS):
        for w in range(WINS):
            if b % 2 == 1:
                lab = region[base[w]]
                out[b, w, :SPAN, :SPAN] = np.where(lab[:, None] == lab[None, :], 0.0, MASK_FILL)
            out[b, w, SPAN:, :] = KEY_FILL
    return out


def rel_onehot(rels):
    out = np.zeros((rels, PAD, PAD), np.float32)
    pos = np.arange(SPAN)
    row, col = pos // WIN, pos % WIN
    for q in range(SPAN):
        e = (row[q] - row + WIN - 1) * (2 * WIN - 1) + col[q] - col + WIN - 1
        out[e, np.arange(SPAN), q] = 1.0
    return out


def dot(a, b, dims=None):
    if dims is None:
        return jnp.dot(a, b, preferred_element_type=F32)
    return lax.dot_general(a, b, dims, preferred_element_type=F32)


def lane_heads(width):
    return lax.broadcasted_iota(jnp.int32, (1, width), 1) // HEAD_DIM


def spread(rows, heads):
    zero = jnp.zeros_like(rows)
    return jnp.concatenate([jnp.where(heads == h, rows, zero) for h in range(GROUP)], 0)


def gather_diag(prod, heads):
    out = prod[0:PAD]
    for h in range(1, GROUP):
        out = jnp.where(heads == h, prod[h * PAD : (h + 1) * PAD], out)
    return out


def gelu_pair(u):
    au = jnp.abs(u)
    t = 1.0 / (1.0 + (0.3275911 * 0.7071067811865476) * au)
    e = jnp.exp(-0.5 * u * u)
    q = 1.061405429 * 0.5
    q = q * t - 1.453152027 * 0.5
    q = q * t + 1.421413741 * 0.5
    q = q * t - 0.284496736 * 0.5
    q = q * t + 0.254829592 * 0.5
    q = q * t * e
    phi = jnp.where(u >= 0, 1.0 - q, q)
    return u * phi, phi + u * e * 0.3989422804014327


def chunks(rows, size):
    return [(r, min(size, rows - r)) for r in range(0, rows, size)]


def norm_rows(x):
    mean = jnp.mean(x, -1, keepdims=True)
    cen = x - mean
    inv = lax.rsqrt(jnp.mean(cen * cen, -1, keepdims=True) + NORM_EPS)
    return cen * inv, inv


def put_rows(ref, vals):
    images = len(vals)
    for i in range(images):
        base = image_base(i)
        lead = 0
        if i > 0:
            lead = image_base(i - 1) + IMG_ROWS - base
            mix = vals[i - 1][IMG_ROWS - lead :] + vals[i][:lead]
            ref[base : base + lead, :] = mix.astype(ref.dtype)
        end = image_base(i + 1) - base if i + 1 < images else IMG_ROWS
        ref[base + lead : base + end, :] = vals[i][lead:end].astype(ref.dtype)


def norm_into(src, dst, gain, off):
    for r, n in chunks(src.shape[0], 112):
        unit, _ = norm_rows(src[r : r + n, :])
        dst[r : r + n, :] = (unit * gain + off).astype(BF16)


def fold(val):
    rows, cols = val.shape
    return jnp.sum(val.reshape(rows // 8, 8, cols), 0)


def back_norm(src, grad, gain, dst):
    width = src.shape[1]
    sums = [jnp.zeros((8, width), F32) for _ in range(3)]
    for r, n in chunks(src.shape[0], 112):
        unit, inv = norm_rows(src[r : r + n, :])
        gr = grad[r : r + n, :]
        e = gr * gain
        res = dst[r : r + n, :] + inv * (
            e - jnp.mean(e, -1, keepdims=True) - unit * jnp.mean(e * unit, -1, keepdims=True)
        )
        dst[r : r + n, :] = res
        for j, val in enumerate((gr * unit, gr, res)):
            sums[j] = sums[j] + fold(val)
    return [jnp.sum(s, 0, keepdims=True) for s in sums]


def column_sum(ref):
    total = jnp.zeros((8, ref.shape[1]), F32)
    for r, n in chunks(ref.shape[0], 112):
        total = total + fold(ref[r : r + n, :])
    return jnp.sum(total, 0, keepdims=True)
GAIN_ROW = 0
BIAS_ROW = GAIN_ROW + 2 * BLOCKS
QV_ROW = BIAS_ROW + 4 * BLOCKS
HID_ROW = QV_ROW + 2 * BLOCKS
MESH = pl.DeviceIdType.MESH


class Digit:
    def __init__(self, name, axis, size, stride, dim):
        self.name, self.axis, self.size, self.stride, self.dim = name, axis, size, stride, dim

    def here(self):
        return lax.rem(lax.axis_index(self.axis) // self.stride, self.size)

    def peer(self, step):
        d = self.here()
        to = lax.rem(d + step, self.size)
        return to, {self.axis: lax.axis_index(self.axis) + (to - d) * self.stride}


def plan(n_fsdp, n_tensor):
    if (n_fsdp, n_tensor) == (8, 4):
        parts = [("x", "tensor", 2), ("core", "tensor", 2), ("z", "fsdp", 4), ("y", "fsdp", 2)]
    elif (n_fsdp, n_tensor) == (32, 4):
        parts = [("x", "tensor", 4), ("z", "fsdp", 4), ("y", "fsdp", 4), ("core", "fsdp", 2)]
    else:
        parts = [("x", "tensor", n_tensor), ("z", "fsdp", n_fsdp)]
    digits = {}
    for dim, (name, axis, size) in enumerate(parts):
        stride = 1
        for _, later_axis, later in parts[dim + 1 :]:
            if later_axis == axis:
                stride *= later
        digits[name] = Digit(name, axis, size, stride, dim)
    return digits


def orders(digits):
    one = [n for n in ("z", "x", "y", "core") if n in digits]
    two = [n for n in ("z", "y", "x", "core") if n in digits]
    return [[digits[n] for n in one], [digits[n] for n in two]]


def greet(peers):
    barrier = pltpu.get_barrier_semaphore()
    for device in peers:
        pl.semaphore_signal(barrier, inc=1, device_id=device, device_id_type=MESH)
    pl.semaphore_wait(barrier, len(peers))


def tensor_peers(n_tensor):
    t = lax.axis_index("tensor")
    return [{"tensor": lax.rem(t + s, n_tensor)} for s in range(1, n_tensor)]


def all_peers(digits, n_tensor):
    peers = [d.peer(s)[1] for d in digits.values() if d.axis == "fsdp" for s in range(1, d.size)]
    return peers + tensor_peers(n_tensor)


def pieces(cols, width):
    return [(c, min(width, cols - c)) for c in range(0, cols, width)]


def adam(weight, first, second, grad, rate, decay):
    first_new = BETA_ONE * first + (1.0 - BETA_ONE) * grad
    second_new = BETA_TWO * second + (1.0 - BETA_TWO) * grad * grad
    first_hat = first_new * (1.0 / (1.0 - BETA_ONE**ADAM_STEP))
    second_hat = second_new * (1.0 / (1.0 - BETA_TWO**ADAM_STEP))
    step = first_hat / (jnp.sqrt(second_hat) + ADAM_EPS)
    if decay:
        step = step + decay * weight
    return weight - rate * step, first_new, second_new


def pick(index, values):
    out = values[0]
    for i in range(1, len(values)):
        out = jnp.where(index == i, values[i], out)
    return out


def rel_row(groups):
    return HID_ROW + BLOCKS * groups


def solution(mesh):
    n_fsdp, n_tensor = mesh.shape["fsdp"], mesh.shape["tensor"]
    tokens = P(("fsdp", "tensor"), None, None)
    kinds = (
        P(None, "fsdp", None, "tensor"), P(None, "tensor", "fsdp"), P(None, "fsdp", "tensor"),
        P(None, "tensor", "fsdp"), P(None, "tensor", None), P(None, None, "tensor"),
        P(None, "tensor"), P(), P(),
    )
    thrice = tuple(k for k in kinds for _ in range(3))
    return jax.shard_map(
        functools.partial(shards, n_fsdp, n_tensor),
        mesh=mesh,
        in_specs=(tokens, tokens, P("fsdp")) + thrice,
        out_specs=(tokens, tokens) + thrice,
        check_vma=False,
    )
PART = 512
HALF = 256
REL_LANES = 256


def rel_consts():
    side = 2 * WIN - 1
    top = side * (WIN - 1) + WIN - 1
    down = np.zeros((96, PAD), np.float32)
    across = np.zeros((GROUP * PAD, GROUP * REL_LANES), np.float32)
    for i in range(SPAN):
        place = side * (i // WIN) + i % WIN
        down[top - place, i] = 1.0
        for h in range(GROUP):
            across[h * PAD + i, h * REL_LANES + place] = 1.0
    return down, across


def block_kernel(
    n_fsdp, n_tensor,
    x_hbm, ct_hbm, live, own, rel, side, mask, gains, offs, perm, perm_t, rel_down, rel_across,
    xo_hbm, dxo_hbm, gsum, total, keep_gl, keep_gp, keep_qkv, keep_pts,
    wt, dgr, rels, sides, io, xs, ms, aw, qkv, pts, ow, osb, a2, gl, gp, ubuf, acc, dx, cut, awt, dwin, dsum, small,
    *rest,
):
    digits = plan(n_fsdp, n_tensor)
    dims = sorted(digits.values(), key=lambda d: d.dim)
    ways = orders(digits)
    backs = [w[::-1] for w in ways]
    phases = len(dims)
    stage = [rest[j * phases : (j + 1) * phases] for j in range(2)]
    small_slots = rest[2 * phases : 3 * phases]
    (io_sem, own_sem, keep_sem, rel_send, rel_recv, side_send, side_recv, ag_send, ag_recv, rs_send, rs_recv,
     sm_send, sm_recv) = rest[3 * phases :]
    images = io.shape[0]
    groups = n_tensor
    rows, width = xs.shape[1:]
    lanes = GROUP * HEAD_DIM
    hid = gl.shape[2]
    cols = wt.shape[-1]
    parts = cols // PART
    c_out, c_up, c_down = 3 * lanes, 4 * lanes, 4 * lanes + hid
    heads = lane_heads(lanes)
    tdims = [d for d in dims if d.axis == "tensor"]
    fdims = [d for d in dims if d.axis == "fsdp"]
    per = wt.shape[-2]
    fshape = tuple(d.size for d in fdims) + (per,)
    t_here = lax.axis_index("tensor")

    def tplace(t):
        return tuple(lax.rem(t // d.stride, d.size) for d in tdims)

    def weight(b, t, lo, hi):
        index = (b,) + tplace(t) + (slice(None),) * len(fshape) + (slice(lo, hi),)
        return wt[index].reshape(width, hi - lo)

    def grad_ref(b):
        return dgr if b == BLOCKS - 1 else wt.at[BLOCKS - 1]

    def put_grad(b, t, lo, hi, value):
        index = tplace(t) + (slice(None),) * len(fshape) + (slice(lo, hi),)
        grad_ref(b)[index] = value.astype(BF16).reshape(fshape + (hi - lo,))

    def ag_copies(p, phase):
        b, c = p // parts, (p % parts) * PART
        out = []
        for h in range(2):
            order = ways[h]
            digit = order[phase]
            at = pl.ds(c + h * HALF, HALF)
            index = tuple(slice(None) if d in order[:phase] else d.here() for d in dims)
            dst = wt.at[(b,) + index + (slice(None), at)]
            src = own.at[b, :, at] if phase == 0 else dst
            for s in range(1, digit.size):
                sem = (p, h, phase, s - 1)
                out.append(pltpu.make_async_remote_copy(
                    src_ref=src, dst_ref=dst, send_sem=ag_send.at[sem], recv_sem=ag_recv.at[sem],
                    device_id=digit.peer(s)[1], device_id_type=MESH))
        return out

    def start(copies):
        for cp in copies:
            cp.start()

    def arrive(copies):
        for cp in copies:
            cp.wait_recv()

    def sent(copies):
        for cp in copies:
            cp.wait_send()

    pairs = BLOCKS * parts

    def ag_step(p, phase):
        if 0 <= p < pairs:
            arrive(ag_copies(p, phase - 1))
            start(ag_copies(p, phase))

    def pump(i):
        ag_step(i + 2, 1)
        ag_step(i + 1, 2)
        ag_step(i, 3)

    def need(p):
        arrive(ag_copies(p, phases - 1))

    def rs_copies(b, part, phase):
        out = []
        for h in range(2):
            order = backs[h]
            digit = order[phase]
            at = pl.ds(part * PART + h * HALF, HALF)
            for s in range(1, digit.size):
                to, device = digit.peer(s)
                index = tuple(
                    to if d is digit else d.here() if d in order[:phase] else slice(None) for d in dims
                )
                sem = (b, part, h, phase, s - 1)
                out.append(pltpu.make_async_remote_copy(
                    src_ref=grad_ref(b).at[index + (slice(None), at)],
                    dst_ref=stage[h][phase].at[b, part, s - 1],
                    send_sem=rs_send.at[sem], recv_sem=rs_recv.at[sem],
                    device_id=device, device_id_type=MESH))
        return out

    def rs_absorb(b, part, phase):
        grad = grad_ref(b)
        for h in range(2):
            order = backs[h]
            digit = order[phase]
            at = slice(part * PART + h * HALF, part * PART + (h + 1) * HALF)
            left = [d for d in dims if d not in order[: phase + 1]]
            land = stage[h][phase]
            steps = int(np.prod([d.size for d in left]))

            def one(i, carry):
                place = {}
                more = i
                for d in reversed(left):
                    place[d.name] = lax.rem(more, d.size)
                    more = more // d.size
                index = tuple(place[d.name] if d in left else d.here() for d in dims)
                value = grad[index + (slice(None), at)]
                for s in range(digit.size - 1):
                    value = value + land[(b, part, s) + tuple(place[d.name] for d in left)]
                grad[index + (slice(None), at)] = value
                return carry

            lax.fori_loop(0, steps, one, 0)

    def rs_step(b, part, phase):
        arrive(rs_copies(b, part, phase - 1))
        rs_absorb(b, part, phase - 1)
        start(rs_copies(b, part, phase))

    def rs_finish(b, part):
        arrive(rs_copies(b, part, phases - 1))
        for h in range(2):
            digit = backs[h][-1]
            at = slice(part * PART + h * HALF, part * PART + (h + 1) * HALF)
            index = tuple(d.here() for d in dims)
            value = grad_ref(b)[index + (slice(None), at)].astype(F32)
            for s in range(digit.size - 1):
                value = value + stage[h][phases - 1][b, part, s].astype(F32)
            gsum[b, :, at] = value

    small_order = [digits[n] for n in ("core", "y", "x", "z")]

    def small_copies(phase):
        digit = small_order[phase]
        place = small_slots[phase].at[digit.here()]
        return [
            pltpu.make_async_remote_copy(
                src_ref=place, dst_ref=place, send_sem=sm_send.at[phase, s - 1],
                recv_sem=sm_recv.at[phase, s - 1], device_id=digit.peer(s)[1], device_id_type=MESH)
            for s in range(1, digit.size)
        ]

    def small_step(phase):
        if phase == 0:
            value = small[...]
        else:
            arrive(small_copies(phase - 1))
            value = small_slots[phase - 1][0]
            for s in range(1, small_order[phase - 1].size):
                value = value + small_slots[phase - 1][s]
        if phase < phases:
            small_slots[phase][small_order[phase].here()] = value
            start(small_copies(phase))
        else:
            total[...] = value

    loads = [
        pltpu.make_async_copy(x_hbm, io, io_sem.at[0]),
        pltpu.make_async_copy(ct_hbm, io, io_sem.at[1]),
    ]
    loads[0].start()
    mine = tuple(d.here() for d in dims)
    own_copies = [
        pltpu.make_async_copy(own.at[b], wt.at[(b,) + mine], own_sem.at[b]) for b in range(BLOCKS)
    ]
    own_copies.append(pltpu.make_async_copy(side, sides.at[t_here], own_sem.at[BLOCKS]))
    own_copies.append(pltpu.make_async_copy(rel, rels.at[t_here], own_sem.at[BLOCKS + 1]))
    start(own_copies)
    greet(all_peers(digits, n_tensor))
    side_copies = [
        pltpu.make_async_remote_copy(
            src_ref=src, dst_ref=dst.at[t_here], send_sem=ssem.at[j], recv_sem=rsem.at[j],
            device_id=device, device_id_type=MESH)
        for src, dst, ssem, rsem in (
            (rel, rels, rel_send, rel_recv), (side, sides, side_send, side_recv)
        )
        for j, device in enumerate(tensor_peers(n_tensor))
    ]
    start(ag_copies(0, 0))
    start(side_copies)
    for p in range(1, pairs):
        start(ag_copies(p, 0))

    used = images * TOKENS
    floor = used // 8 * 8
    loads[0].wait()
    xs[0, floor:rows, :] = jnp.zeros((rows - floor, width), F32)
    for i in range(images):
        xs[0, i * TOKENS : (i + 1) * TOKENS, :] = io[i]
    loads[1].start()

    def first_norm(b):
        norm_into(xs.at[b], cut, gains[b, 0:1, :], offs[b, 0:1, :])
        for i in range(images):
            base = image_base(i)
            aw[b, i * IMG_PAD : (i + 1) * IMG_PAD, :] = dot(
                perm[b, i], cut[base : base + IMG_ROWS, :]
            ).astype(BF16)

    first_norm(0)
    loads[1].wait()
    dx[floor:rows, :] = jnp.zeros((rows - floor, width), F32)
    for i in range(images):
        dx[i * TOKENS : (i + 1) * TOKENS, :] = io[i] * live[i]
    for cp in own_copies:
        cp.wait()
    ag_step(0, 1)
    ag_step(1, 1)
    ag_step(0, 2)
    pump(0)
    for cp in side_copies:
        cp.wait()

    def hooks(t, table):
        for at, calls in table.items():

            @pl.when(t == at)
            def _():
                for call in calls:
                    call()

    fwd_hooks = {
        (0, "attend"): {1: [lambda: pump(1)], 3: [lambda: pump(2)]},
        (0, "mlp"): {2: [lambda: pump(3)]},
        (1, "attend"): {1: [lambda: pump(4)], 3: [lambda: pump(5)]},
    }

    att_keeps = [
        pltpu.make_async_copy(qkv, keep_qkv, keep_sem.at[0]),
        pltpu.make_async_copy(pts, keep_pts, keep_sem.at[1]),
    ]
    mlp_keeps = [
        pltpu.make_async_copy(gl, keep_gl, keep_sem.at[2]),
        pltpu.make_async_copy(gp, keep_gp, keep_sem.at[3]),
    ]
    bias_at = 0
    for b in range(BLOCKS):
        off2, off3 = (offs[b, j : j + 1, :].astype(BF16).astype(F32) for j in (2, 3))
        if b > 0:
            first_norm(b)
            for cp in att_keeps:
                cp.wait()
        need(b * parts)

        def attend(t, carry):
            hooks(t, fwd_hooks.get((b, "attend"), {}))
            rows_qkv = dot(aw[b], weight(b, t, 0, c_out))
            for j in range(3):
                part = rows_qkv[:, j * lanes : (j + 1) * lanes]
                if j != 1:
                    at = bias_at + 2 * b + j // 2
                    part = part + sides[t, at : at + 1, 0:lanes].astype(BF16).astype(F32)
                qkv[t, :, j * lanes : (j + 1) * lanes] = part.astype(BF16)

            def window(w, c2):
                r = pl.multiple_of(w * PAD, PAD)
                q = qkv[t, pl.ds(r, PAD), 0:lanes]
                k = qkv[t, pl.ds(r, PAD), lanes : 2 * lanes]
                v = qkv[t, pl.ds(r, PAD), 2 * lanes : 3 * lanes]
                s = dot(k, spread(q, heads), NT) * INV_ROOT
                s = s + rels[t, b].astype(F32)
                s = s + mask[b, lax.rem(w, WINS)].astype(F32)
                e = jnp.exp(s - jnp.max(s, 0, keepdims=True))
                p = (e * (1.0 / jnp.sum(e, 0, keepdims=True))).astype(BF16)
                pts[t, w] = p
                ow[pl.ds(r, PAD), :] = gather_diag(dot(p, v, TN), heads).astype(BF16)
                return c2

            lax.fori_loop(0, images * WINS, window, 0, unroll=2)
            put_rows(
                osb.at[b, t],
                [dot(perm_t[b, i], ow[i * IMG_PAD : (i + 1) * IMG_PAD, :]) for i in range(images)],
            )
            return carry

        lax.fori_loop(0, groups, attend, 0)
        if b + 1 < BLOCKS:
            start(att_keeps)
        y = dot(osb[b, 0], weight(b, 0, c_out, c_up), NT)
        for t in range(1, groups):
            y = y + dot(osb[b, t], weight(b, t, c_out, c_up), NT)
        ms[b] = xs[b] + y + off2
        norm_into(ms.at[b], a2.at[b], gains[b, 1:2, :], offs[b, 1:2, :])
        acc[...] = ms[b] + off3
        if b > 0:
            for cp in mlp_keeps:
                cp.wait()
        need(b * parts + 1)
        need(b * parts + 2)

        def mlp(t, carry):
            hooks(t, fwd_hooks.get((b, "mlp"), {}))
            ubuf[0:rows, :] = dot(a2[b], weight(b, t, c_up, c_down))
            at = bias_at + 2 * BLOCKS + b
            hbias = sides[t, at : at + 1, :].astype(BF16).astype(F32)
            for r, n in chunks(rows, 32):
                g, d = gelu_pair(ubuf[r : r + n, :] + hbias)
                gl[t, r : r + n, :] = g.astype(BF16)
                gp[t, r : r + n, :] = d.astype(BF16)
            acc[...] += dot(gl[t], weight(b, t, c_down, cols), NT)
            return carry

        lax.fori_loop(0, groups, mlp, 0)
        if b + 1 < BLOCKS:
            start(mlp_keeps)
            xs[b + 1] = acc[...]
    for i in range(images):
        io[i] = acc[i * TOKENS : (i + 1) * TOKENS, :]
    x_store = pltpu.make_async_copy(io, xo_hbm, io_sem.at[0])
    x_store.start()

    last = BLOCKS - 1
    back_hooks = {
        (1, "attend"): {
            0: [lambda: rs_step(1, 2, 1)],
            1: [lambda: rs_step(1, 1, 1)],
            2: [lambda: rs_step(1, 2, 2)],
            3: [lambda: rs_step(1, 1, 2)],
        },
        (0, "mlp"): {
            0: [lambda: rs_step(1, 0, 1)],
            1: [lambda: rs_step(1, 2, 3)],
            2: [lambda: rs_step(1, 1, 3)],
            3: [lambda: rs_step(1, 0, 2)],
        },
        (0, "attend"): {
            0: [lambda: rs_step(0, 2, 1), lambda: rs_finish(1, 2)],
            1: [lambda: rs_step(0, 1, 1), lambda: rs_finish(1, 1)],
            2: [lambda: rs_step(0, 2, 2), lambda: rs_step(1, 0, 3)],
            3: [lambda: rs_step(0, 1, 2), lambda: rs_finish(1, 0)],
        },
    }
    mlp_loads = [
        pltpu.make_async_copy(keep_gl, gl, keep_sem.at[2]),
        pltpu.make_async_copy(keep_gp, gp, keep_sem.at[3]),
    ]
    att_loads = [
        pltpu.make_async_copy(keep_qkv, qkv, keep_sem.at[0]),
        pltpu.make_async_copy(keep_pts, pts, keep_sem.at[1]),
    ]
    for b in range(BLOCKS - 1, -1, -1):
        bias_row = BIAS_ROW + 4 * b
        small[bias_row + 3 : bias_row + 4, :] = column_sum(dx)
        cut[...] = dx[...].astype(BF16)
        dxt = jnp.transpose(cut[...])
        a_t = jnp.transpose(a2[b])
        acc[...] = jnp.zeros_like(acc)
        if b < last:
            for p in range(last * parts, (last + 1) * parts):
                for phase in range(phases):
                    sent(ag_copies(p, phase))
            for cp in mlp_loads:
                cp.wait()

        def mlp_back(t, carry):
            hooks(t, back_hooks.get((b, "mlp"), {}))
            put_grad(b, t, c_down, cols, dot(dxt, gl[t]))
            dh = dot(cut[...], weight(b, t, c_down, cols))
            du = (dh * gp[t].astype(F32)).astype(BF16)
            gp[t] = du
            small[pl.ds(HID_ROW + b * groups + t, 1), :] = jnp.sum(
                fold(du.astype(F32)), 0, keepdims=True
            )
            put_grad(b, t, c_up, c_down, dot(a_t, du))
            acc[...] += dot(du, weight(b, t, c_up, c_down), NT)
            return carry

        lax.fori_loop(0, groups, mlp_back, 0)
        start(rs_copies(b, 2, 0))
        start(rs_copies(b, 1, 0))
        if b == last:
            start(mlp_loads)
        sums = back_norm(ms.at[b], acc, gains[b, 1:2, :], dx)
        small[GAIN_ROW + 2 * b + 1 : GAIN_ROW + 2 * b + 2, :] = sums[0]
        small[bias_row + 1 : bias_row + 2, :] = sums[1]
        small[bias_row + 2 : bias_row + 3, :] = sums[2]
        cut[...] = dx[...].astype(BF16)
        dmt = jnp.transpose(cut[...])
        awt[...] = jnp.transpose(aw[b])
        da = ubuf
        da[...] = jnp.zeros_like(da)
        for t in range(groups):
            put_grad(b, t, c_out, c_up, dot(dmt, osb[b, t]))
        if b < last:
            for cp in att_loads:
                cp.wait()

        def attend_back(t, carry):
            hooks(t, back_hooks.get((b, "attend"), {}))
            do_t = dot(cut[...], weight(b, t, c_out, c_up)).astype(BF16)
            for i in range(images):
                base = image_base(i)
                ow[i * IMG_PAD : (i + 1) * IMG_PAD, :] = dot(
                    perm[b, i], do_t[base : base + IMG_ROWS]
                ).astype(BF16)
            dsum[...] = jnp.zeros_like(dsum)

            def window(w, c2):
                r = pl.multiple_of(w * PAD, PAD)
                q = qkv[t, pl.ds(r, PAD), 0:lanes]
                k = qkv[t, pl.ds(r, PAD), lanes : 2 * lanes]
                v = qkv[t, pl.ds(r, PAD), 2 * lanes : 3 * lanes]
                p = pts[t, w]
                dob = spread(ow[pl.ds(r, PAD), :], heads)
                dp = dot(v, dob, NT)
                pf = p.astype(F32)
                ds = (pf * (dp - jnp.sum(pf * dp, 0, keepdims=True))).astype(BF16)
                dsum[...] += ds.astype(F32)
                dv = dot(p, dob)
                dk = dot(ds, spread(q, heads)) * INV_ROOT
                dq = gather_diag(dot(ds, k, TN), heads) * INV_ROOT
                dwin[pl.ds(r, PAD), 0:lanes] = dq.astype(BF16)
                dwin[pl.ds(r, PAD), lanes : 2 * lanes] = dk.astype(BF16)
                dwin[pl.ds(r, PAD), 2 * lanes : 3 * lanes] = dv.astype(BF16)
                return c2

            lax.fori_loop(0, images * WINS, window, 0, unroll=2)
            col = pl.ds(pl.multiple_of(t * lanes, lanes), lanes)
            for j in range(2):
                val = dwin[:, 2 * j * lanes : (2 * j + 1) * lanes].astype(F32)
                row = QV_ROW + 2 * b + j
                small[row : row + 1, col] = jnp.sum(fold(val), 0, keepdims=True)
            ds_all = dsum[...]
            high = ds_all.astype(BF16)
            rest_low = (ds_all - high.astype(F32)).astype(BF16)
            wide = sum(
                dot(dot(rel_down[...], piece).astype(BF16), rel_across[...])
                for piece in (high, rest_low)
            )
            skew = wide[0:8]
            for a in range(1, wide.shape[0] // 8):
                skew = skew + pltpu.roll(wide[8 * a : 8 * a + 8], 8 * a, 1)
            row_id = lax.broadcasted_iota(jnp.int32, skew.shape, 0)
            for bit in (1, 2, 4):
                skew = jnp.where((row_id & bit) != 0, pltpu.roll(skew, bit, 1), skew)
            skew = jnp.sum(skew, 0, keepdims=True)
            for h in range(GROUP):
                small[pl.ds(rel_row(groups) + (b * groups + t) * GROUP + h, 1), 0:REL_LANES] = skew[
                    :, h * REL_LANES : (h + 1) * REL_LANES
                ]
            put_grad(b, t, 0, c_out, dot(awt[...], dwin[...]))
            da[...] += dot(dwin[...], weight(b, t, 0, c_out), NT)
            return carry

        lax.fori_loop(0, groups, attend_back, 0)
        start(rs_copies(b, 0, 0))
        if b == last:
            start(att_loads)
        vals = []
        for i in range(images):
            part = da[i * IMG_PAD : (i + 1) * IMG_PAD, :]
            high = part.astype(BF16)
            rest_low = (part - high.astype(F32)).astype(BF16)
            vals.append(dot(perm_t[b, i], high) + dot(perm_t[b, i], rest_low))
        put_rows(acc, vals)
        sums = back_norm(xs.at[b], acc, gains[b, 0:1, :], dx)
        small[GAIN_ROW + 2 * b : GAIN_ROW + 2 * b + 1, :] = sums[0]
        small[bias_row : bias_row + 1, :] = sums[1]
    small_step(0)
    rs_step(0, 0, 1)
    x_store.wait()
    for i in range(images):
        io[i] = dx[i * TOKENS : (i + 1) * TOKENS, :]
    dx_store = pltpu.make_async_copy(io, dxo_hbm, io_sem.at[1])
    dx_store.start()
    small_step(1)
    rs_step(0, 2, 3)
    rs_step(0, 0, 2)
    small_step(2)
    rs_step(0, 1, 3)
    rs_finish(0, 2)
    small_step(3)
    rs_step(0, 0, 3)
    rs_finish(0, 1)
    small_step(4)
    rs_finish(0, 0)
    dx_store.wait()
    for p in range(last * parts):
        for phase in range(phases):
            sent(ag_copies(p, phase))
    for b in range(BLOCKS):
        for part in range(parts):
            for phase in range(phases):
                sent(rs_copies(b, part, phase))
    for phase in range(phases):
        sent(small_copies(phase))


def block_call(x, ct, live, own, rel, side, gains, offs, n_fsdp, n_tensor):
    images, _, width = x.shape
    cols = own.shape[2]
    per = own.shape[1]
    lanes = GROUP * HEAD_DIM
    hid = (cols - 4 * lanes) // 2
    parts = cols // PART
    rows = -(-images * TOKENS // 16) * 16
    wrows = images * IMG_PAD
    digits = plan(n_fsdp, n_tensor)
    dims = sorted(digits.values(), key=lambda d: d.dim)
    sizes = tuple(d.size for d in dims)
    most = max(sizes) - 1
    phases = len(dims)
    perm = permutations(images)
    down, across = rel_consts()
    consts = (
        jnp.asarray(np.tile(mask_table(), (1, 1, 1, GROUP)), BF16),
        jnp.asarray(perm, BF16),
        jnp.asarray(np.swapaxes(perm, 2, 3), BF16),
        jnp.asarray(down, BF16),
        jnp.asarray(across, BF16),
    )
    small_rows = rel_row(n_tensor) + BLOCKS * n_tensor * GROUP
    stages = []
    for order in orders(digits):
        order = order[::-1]
        for phase, digit in enumerate(order):
            left = tuple(d.size for d in dims if d not in order[: phase + 1])
            stages.append(pltpu.VMEM((BLOCKS, parts, digit.size - 1) + left + (per, HALF), BF16))
    small_order = [digits[n] for n in ("core", "y", "x", "z")]
    vmem = pl.BlockSpec(memory_space=pltpu.VMEM)
    anyspace = pl.BlockSpec(memory_space=pl.ANY)
    keep = [
        (n_tensor, rows, hid), (n_tensor, rows, hid), (n_tensor, wrows, 3 * lanes),
        (n_tensor, images * WINS, PAD, GROUP * PAD),
    ]
    dma = pltpu.SemaphoreType.DMA
    out = pl.pallas_call(
        functools.partial(block_kernel, n_fsdp, n_tensor),
        out_shape=(
            jax.ShapeDtypeStruct(x.shape, F32),
            jax.ShapeDtypeStruct(x.shape, F32),
            jax.ShapeDtypeStruct((BLOCKS, per, cols), F32),
            jax.ShapeDtypeStruct((small_rows, width), F32),
        ) + tuple(jax.ShapeDtypeStruct(s, BF16) for s in keep),
        in_specs=[
            anyspace, anyspace, pl.BlockSpec(memory_space=pltpu.SMEM), anyspace, anyspace, anyspace,
        ] + [vmem] * 7,
        out_specs=(anyspace, anyspace, vmem, vmem) + (anyspace,) * 4,
        scratch_shapes=[
            pltpu.VMEM((BLOCKS,) + sizes + (per, cols), BF16),
            pltpu.VMEM(sizes + (per, cols), BF16),
            pltpu.VMEM((n_tensor,) + rel.shape, BF16),
            pltpu.VMEM((n_tensor,) + side.shape, F32),
            pltpu.VMEM(x.shape, F32),
            pltpu.VMEM((BLOCKS, rows, width), F32),
            pltpu.VMEM((BLOCKS, rows, width), F32),
            pltpu.VMEM((BLOCKS, wrows, width), BF16),
            pltpu.VMEM(keep[2], BF16),
            pltpu.VMEM(keep[3], BF16),
            pltpu.VMEM((wrows, lanes), BF16),
            pltpu.VMEM((BLOCKS, n_tensor, rows, lanes), BF16),
            pltpu.VMEM((BLOCKS, rows, width), BF16),
            pltpu.VMEM(keep[0], BF16),
            pltpu.VMEM(keep[1], BF16),
            pltpu.VMEM((wrows, width), F32),
            pltpu.VMEM((rows, width), F32),
            pltpu.VMEM((rows, width), F32),
            pltpu.VMEM((rows, width), BF16),
            pltpu.VMEM((width, wrows), BF16),
            pltpu.VMEM((wrows, 3 * lanes), BF16),
            pltpu.VMEM((PAD, GROUP * PAD), F32),
            pltpu.VMEM((small_rows, width), F32),
        ]
        + stages
        + [pltpu.VMEM((d.size, small_rows, width), F32) for d in small_order]
        + [
            dma((2,)), dma((BLOCKS + 2,)), dma((4,)),
            dma((n_tensor - 1,)), dma((n_tensor - 1,)), dma((n_tensor - 1,)), dma((n_tensor - 1,)),
            dma((BLOCKS * parts, 2, phases, most)), dma((BLOCKS * parts, 2, phases, most)),
            dma((BLOCKS, parts, 2, phases, most)), dma((BLOCKS, parts, 2, phases, most)),
            dma((phases, most)), dma((phases, most)),
        ],
        compiler_params=pltpu.CompilerParams(
            collective_id=0, has_side_effects=True, vmem_limit_bytes=127 * MIB // 2
        ),
    )(x, ct, live, own, rel, side, consts[0], gains, offs, *consts[1:])
    return out[:4]


def adam_kernel(groups, gsum, total, slot, *refs):
    params = [refs[3 * j : 3 * j + 3] for j in range(9)]
    outs = [refs[27 + 3 * j : 30 + 3 * j] for j in range(9)]
    lanes = GROUP * HEAD_DIM
    hid = params[2][0].shape[2]
    t = slot[0]

    def update(kind, place, grad, rate, decay):
        new = adam(*(p[place] for p in params[kind]), grad, rate, decay)
        for ref, val in zip(outs[kind], new):
            ref[place] = val

    for b in range(BLOCKS):
        for j in range(3):
            update(0, (b, j), gsum[b, :, j * lanes : (j + 1) * lanes], MATRIX_RATE, WEIGHT_DECAY)
        update(1, (b,), gsum[b, :, 3 * lanes : 4 * lanes], MATRIX_RATE, WEIGHT_DECAY)
        update(2, (b,), gsum[b, :, 4 * lanes : 4 * lanes + hid], MATRIX_RATE, WEIGHT_DECAY)
        update(3, (b,), gsum[b, :, 4 * lanes + hid :], MATRIX_RATE, WEIGHT_DECAY)
        heads, rels = params[4][0].shape[1:]
        at = rel_row(groups) + b * groups * heads
        hid_at = HID_ROW + b * groups
        rel = pick(t, [total[at + i * heads : at + (i + 1) * heads, 0:rels] for i in range(groups)])
        qv = pick(t, [total[QV_ROW + 2 * b : QV_ROW + 2 * b + 2, i * lanes : (i + 1) * lanes] for i in range(groups)])
        hidden = pick(t, [total[hid_at + i : hid_at + i + 1, :] for i in range(groups)])
        update(4, (b,), rel, SMALL_RATE, 0.0)
        update(5, (b,), qv, SMALL_RATE, 0.0)
        update(6, (slice(b, b + 1),), hidden, SMALL_RATE, 0.0)
        update(7, (b,), total[GAIN_ROW + 2 * b : GAIN_ROW + 2 * b + 2, :], SMALL_RATE, 0.0)
        update(8, (b,), total[BIAS_ROW + 4 * b : BIAS_ROW + 4 * b + 4, :], SMALL_RATE, 0.0)


def adam_call(gsum, total, params, n_tensor):
    vmem = pl.BlockSpec(memory_space=pltpu.VMEM)
    flat = [p for group in params for p in group]
    slot = lax.axis_index("tensor").astype(jnp.int32).reshape(1)
    return pl.pallas_call(
        functools.partial(adam_kernel, n_tensor),
        out_shape=tuple(jax.ShapeDtypeStruct(p.shape, p.dtype) for p in flat),
        in_specs=[vmem, vmem, pl.BlockSpec(memory_space=pltpu.SMEM)] + [vmem] * len(flat),
        out_specs=tuple(vmem for _ in flat),
        compiler_params=pltpu.CompilerParams(vmem_limit_bytes=32 * MIB),
    )(gsum, total, slot, *flat)


def shards(n_fsdp, n_tensor, *args):
    image_rows, cotangent, live_counts = args[:3]
    qkv, out, up, down, rel, qv, hidden, gain, bias = [args[3 + 3 * j : 6 + 3 * j] for j in range(9)]
    qkv = tuple(p.transpose(0, 2, 1, 3) for p in qkv)
    out = tuple(p.swapaxes(1, 2) for p in out)
    down = tuple(p.swapaxes(1, 2) for p in down)
    images = image_rows.shape[0]
    slots = lax.axis_index("tensor") * images + jnp.arange(images, dtype=jnp.int32)
    live = (slots < live_counts[0]).astype(F32)
    own = jnp.concatenate([qkv[0][:, j] for j in range(3)] + [out[0], up[0], down[0]], 2).astype(BF16)
    heads, rels = rel[0].shape[1:]
    onehot = jnp.asarray(rel_onehot(rels).reshape(rels, -1), BF16)
    rel_own = lax.dot_general(
        rel[0].astype(BF16), onehot, (((2,), (0,)), ((), ())), preferred_element_type=F32
    )
    rel_own = rel_own.astype(BF16).reshape(BLOCKS, heads, PAD, PAD)
    rel_own = rel_own.swapaxes(1, 2).reshape(BLOCKS, PAD, heads * PAD)
    hid = hidden[0].shape[1]
    side = jnp.concatenate(
        [jnp.pad(qv[0].reshape(2 * BLOCKS, -1), ((0, 0), (0, hid - qv[0].shape[2]))), hidden[0],
         jnp.zeros((8 - 3 * BLOCKS, hid), F32)], 0)
    x_out, dx_out, gsum, total = block_call(
        image_rows, cotangent, live, own, rel_own, side, gain[0], bias[0], n_fsdp, n_tensor
    )
    new = adam_call(gsum, total, (qkv, out, up, down, rel, qv, hidden, gain, bias), n_tensor)
    new = [list(new[3 * j : 3 * j + 3]) for j in range(9)]
    new[0] = [p.transpose(0, 2, 1, 3) for p in new[0]]
    new[1] = [p.swapaxes(1, 2) for p in new[1]]
    new[3] = [p.swapaxes(1, 2) for p in new[3]]
    return (x_out, dx_out) + tuple(p for group in new for p in group)
```

time: 340 us -> 249 us (0.73)
  Pallas kernels: 292 us -> 213 us
  local copies, waits for them, and re-layouts: 36.6 us -> 27.3 us
  matrix products: 6.3 us -> 1.71 us
    pallas_call x3 -> x2, Pallas kernels: 292 us -> 213 us  [the longest x1 211 us: block_call(): pl.pallas_call(functools.partial(block_kernel, n_fsdp, n_tensor), out_sha...]
    dot_general x1 -> x0, matrix products: 4.59 us -> none  [shards(): jnp.dot(table.reshape(BLOCKS * n_tensor * heads, PAD * PAD), jnp.asarray(...]
    unnamed x112 -> x72, local copies, waits for them, and re-layouts: 28.1 us -> 26.2 us
where the time goes in v2:
time: 249 us; the launch traced here: 248 us
  Pallas kernels  213 us (86%)
  local copies, waits for them, and re-layouts  27.3 us (11%)
  other arithmetic  3.87 us (2%)
    pallas_call x1, Pallas kernels, block_call(): pl.pallas_call(functools.partial(block_kernel, n_fsdp, n_tensor), out_sha...  211 us
    unnamed x72, local copies, waits for them, and re-layouts  26.2 us

profile of v2, /device:TPU:0, one launch (start us, length us, event | category | flops | bytes accessed | tf_op | source)
XLA Modules:
  0.0 247.7 jit_solution(1399674182142603969)
XLA Ops:
  2.0 1.4 fusion.4.side
  3.4 1.7 fusion
  5.4 0.8 reshape.71.rel
  10.0 211.3 %shard_map.563 = (f32[3,196,512]{2,1,0:T(8,128)}, f32[3,196,512]{2,1,0:T(8,128)}, f32[2,64,1536]{2,1,0:T(8,128)}, f32[56,512]{1,0:T(8,128)}, bf16[4,592,512]{2,1...) custom-call(f32[3,196,512]{2,1,0:T(8,128)} %x_hbm.1, ...), custom_call_target="tpu_custom_call" | custom-call | tf_op jit(solution)/shard_map/pallas_call | solution.py:849
  221.4 0.9 copy-done.2
  222.3 1.1 copy-done.4
  223.5 0.9 copy-done.5
  224.4 0.9 copy-done.6
  225.4 0.9 copy-done.7
  226.3 0.9 copy-done.8
  227.3 0.8 copy-done.10
  228.1 0.9 copy-done.11
  229.0 0.9 copy-done.12
  230.0 0.9 copy-done.13
  230.9 0.7 copy-done.14
  231.6 0.8 copy-done.15
  232.4 0.8 copy-done.16
  233.9 0.7 copy-done.18
  234.6 0.7 copy-done.19
  235.4 0.7 copy-done.20
  236.8 0.7 copy-done.22
  243.0 1.9 shard_map.564
  244.9 1.0 copy.81
  246.7 1.0 copy.82
  (61 shorter events, 12.3 us)
Async XLA Ops:
  0.7 8.0 %copy-start = (f32[2,64,512]{2,1,0:T(8,128)S(1)}, f32[2,64,512]{2,1,0:T(8,128)}, u32[]{:S(2)}) copy-start(f32[2,64,512]{2,1,0:T(8,128)} %refs_6_.1) | copy-start | bytes 786436
  0.7 7.4 %copy-start.9 = (f32[2,128,64]{1,2,0:T(8,128)S(1)}, f32[2,128,64]{1,2,0:T(8,128)}, u32[]{:S(2)}) copy-start(f32[2,128,64]{1,2,0:T(8,128)} %param.42) | copy-start | bytes 196612
  0.7 5.5 %copy-start.3 = (f32[2,64,3,128]{3,1,2,0:T(8,128)S(1)}, f32[2,64,3,128]{3,1,2,0:T(8,128)}, u32[]{:S(2)}) copy-start(f32[2,64,3,128]{3,1,2,0:T(8,128)} %param.39) | copy-start | bytes 589828
  3.4 5.9 %copy-start.1 = (f32[2,512,64]{1,2,0:T(8,128)S(1)}, f32[2,512,64]{1,2,0:T(8,128)}, u32[]{:S(2)}) copy-start(f32[2,512,64]{1,2,0:T(8,128)} %param.48) | copy-start | bytes 786436
  221.4 1.0 copy-start.2
  222.3 1.1 copy-start.4
  223.5 0.9 copy-start.5
  224.4 0.9 copy-start.6
  225.4 0.9 copy-start.7
  226.3 0.9 copy-start.8
  227.3 0.8 copy-start.10
  228.1 0.9 copy-start.11
  229.0 0.9 copy-start.12
  230.0 0.9 copy-start.13
  230.8 0.7 copy-start.14
  231.6 0.8 copy-start.15
  232.4 0.8 copy-start.16
  233.2 0.7 copy-start.17
  233.9 0.7 copy-start.18
  234.6 0.7 copy-start.19
  235.4 0.7 copy-start.20
  236.8 0.7 copy-start.22
  243.0 2.0 copy-start.32
  244.9 1.7 copy-start.31
  (9 other events, 6.2 us)

commit v3 on v2

--- a/solution.py
+++ b/solution.py
@@ -79,16 +79,6 @@
     return out
 
 
-def rel_onehot(rels):
-    out = np.zeros((rels, PAD, PAD), np.float32)
-    pos = np.arange(SPAN)
-    row, col = pos // WIN, pos % WIN
-    for q in range(SPAN):
-        e = (row[q] - row + WIN - 1) * (2 * WIN - 1) + col[q] - col + WIN - 1
-        out[e, np.arange(SPAN), q] = 1.0
-    return out
-
-
 def dot(a, b, dims=None):
     if dims is None:
         return jnp.dot(a, b, preferred_element_type=F32)
@@ -286,6 +276,12 @@
 PART = 512
 HALF = 256
 REL_LANES = 256
+Z_FIRST = (("z", "x", "y", "core"), ("z", "y", "x", "core"))
+Z_LATE = (("x", "y", "z", "core"), ("y", "x", "z", "core"))
+GATHER_LATE = ((1, 2),)
+REDUCE_LATE = ((1, 2), (0, 2))
+BATCH = 12
+LOG2E = 1.4426950408889634
 
 
 def rel_consts():
@@ -301,29 +297,49 @@
     return down, across
 
 
+def stage_keys(parts, phases):
+    return [
+        (b, part, h, phase)
+        for b in range(BLOCKS)
+        for part in range(parts)
+        for h in range(2)
+        for phase in range(phases)
+    ]
+
+
+def gather_order(digits, b, part, half):
+    return [digits[n] for n in (Z_LATE if (b, part) in GATHER_LATE else Z_FIRST)[half]]
+
+
+def reduce_order(digits, b, part, half):
+    return [digits[n] for n in (Z_LATE if (b, part) in REDUCE_LATE else Z_FIRST)[half]][::-1]
+
+
 def block_kernel(
     n_fsdp, n_tensor,
-    x_hbm, ct_hbm, live, own, rel, side, mask, gains, offs, perm, perm_t, rel_down, rel_across,
+    x_hbm, ct_hbm, counts, qkv_w, out_w, up_w, down_w, rel_w, qv_w, hid_w, mask, gains, offs, perm, perm_t, rel_down, rel_across,
     xo_hbm, dxo_hbm, gsum, total, keep_gl, keep_gp, keep_qkv, keep_pts,
-    wt, dgr, rels, sides, io, xs, ms, aw, qkv, pts, ow, osb, a2, gl, gp, ubuf, acc, dx, cut, awt, dwin, dsum, small,
+    wt, dgr, rels, sides, io, xs, ms, aw, qkv, pts, ow, osb, a2, gl, gp, ubuf, acc, dx, cut, awt, dwin, dsum, added, small,
     *rest,
 ):
     digits = plan(n_fsdp, n_tensor)
     dims = sorted(digits.values(), key=lambda d: d.dim)
-    ways = orders(digits)
-    backs = [w[::-1] for w in ways]
     phases = len(dims)
-    stage = [rest[j * phases : (j + 1) * phases] for j in range(2)]
-    small_slots = rest[2 * phases : 3 * phases]
+    parts = wt.shape[-1] // PART
+    pairs = BLOCKS * parts
+    stage = {}
+    for at, key in enumerate(stage_keys(parts, phases)):
+        stage[key] = rest[at]
+    rest = rest[len(stage) :]
+    small_slots = rest[:phases]
     (io_sem, own_sem, keep_sem, rel_send, rel_recv, side_send, side_recv, ag_send, ag_recv, rs_send, rs_recv,
-     sm_send, sm_recv) = rest[3 * phases :]
+     sm_send, sm_recv) = rest[phases:]
     images = io.shape[0]
     groups = n_tensor
     rows, width = xs.shape[1:]
     lanes = GROUP * HEAD_DIM
     hid = gl.shape[2]
     cols = wt.shape[-1]
-    parts = cols // PART
     c_out, c_up, c_down = 3 * lanes, 4 * lanes, 4 * lanes + hid
     heads = lane_heads(lanes)
     tdims = [d for d in dims if d.axis == "tensor"]
@@ -350,16 +366,15 @@
         b, c = p // parts, (p % parts) * PART
         out = []
         for h in range(2):
-            order = ways[h]
+            order = gather_order(digits, b, p % parts, h)
             digit = order[phase]
             at = pl.ds(c + h * HALF, HALF)
             index = tuple(slice(None) if d in order[:phase] else d.here() for d in dims)
             dst = wt.at[(b,) + index + (slice(None), at)]
-            src = own.at[b, :, at] if phase == 0 else dst
             for s in range(1, digit.size):
                 sem = (p, h, phase, s - 1)
                 out.append(pltpu.make_async_remote_copy(
-                    src_ref=src, dst_ref=dst, send_sem=ag_send.at[sem], recv_sem=ag_recv.at[sem],
+                    src_ref=dst, dst_ref=dst, send_sem=ag_send.at[sem], recv_sem=ag_recv.at[sem],
                     device_id=digit.peer(s)[1], device_id_type=MESH))
         return out
 
@@ -374,17 +389,21 @@
     def sent(copies):
         for cp in copies:
             cp.wait_send()
-
-    pairs = BLOCKS * parts
 
     def ag_step(p, phase):
         if 0 <= p < pairs:
             arrive(ag_copies(p, phase - 1))
             start(ag_copies(p, phase))
+            if phase == 1 and p + 2 < late:
+                start(ag_copies(p + 2, 0))
+
+    late = pairs - 1
 
     def pump(i):
-        ag_step(i + 2, 1)
-        ag_step(i + 1, 2)
+        if i + 2 < late:
+            ag_step(i + 2, 1)
+        if i + 1 < late:
+            ag_step(i + 1, 2)
         ag_step(i, 3)
 
     def need(p):
@@ -393,7 +412,7 @@
     def rs_copies(b, part, phase):
         out = []
         for h in range(2):
-            order = backs[h]
+            order = reduce_order(digits, b, part, h)
             digit = order[phase]
             at = pl.ds(part * PART + h * HALF, HALF)
             for s in range(1, digit.size):
@@ -404,7 +423,7 @@
                 sem = (b, part, h, phase, s - 1)
                 out.append(pltpu.make_async_remote_copy(
                     src_ref=grad_ref(b).at[index + (slice(None), at)],
-                    dst_ref=stage[h][phase].at[b, part, s - 1],
+                    dst_ref=stage[b, part, h, phase].at[s - 1],
                     send_sem=rs_send.at[sem], recv_sem=rs_recv.at[sem],
                     device_id=device, device_id_type=MESH))
         return out
@@ -412,11 +431,11 @@
     def rs_absorb(b, part, phase):
         grad = grad_ref(b)
         for h in range(2):
-            order = backs[h]
+            order = reduce_order(digits, b, part, h)
             digit = order[phase]
             at = slice(part * PART + h * HALF, part * PART + (h + 1) * HALF)
             left = [d for d in dims if d not in order[: phase + 1]]
-            land = stage[h][phase]
+            land = stage[b, part, h, phase]
             steps = int(np.prod([d.size for d in left]))
 
             def one(i, carry):
@@ -428,11 +447,11 @@
                 index = tuple(place[d.name] if d in left else d.here() for d in dims)
                 value = grad[index + (slice(None), at)]
                 for s in range(digit.size - 1):
-                    value = value + land[(b, part, s) + tuple(place[d.name] for d in left)]
+                    value = value + land[(s,) + tuple(place[d.name] for d in left)]
                 grad[index + (slice(None), at)] = value
                 return carry
 
-            lax.fori_loop(0, steps, one, 0)
+            lax.fori_loop(0, steps, one, 0, unroll=min(steps, 4))
 
     def rs_step(b, part, phase):
         arrive(rs_copies(b, part, phase - 1))
@@ -442,12 +461,12 @@
     def rs_finish(b, part):
         arrive(rs_copies(b, part, phases - 1))
         for h in range(2):
-            digit = backs[h][-1]
+            digit = reduce_order(digits, b, part, h)[-1]
             at = slice(part * PART + h * HALF, part * PART + (h + 1) * HALF)
             index = tuple(d.here() for d in dims)
             value = grad_ref(b)[index + (slice(None), at)].astype(F32)
             for s in range(digit.size - 1):
-                value = value + stage[h][phases - 1][b, part, s].astype(F32)
+                value = value + stage[b, part, h, phases - 1][s].astype(F32)
             gsum[b, :, at] = value
 
     small_order = [digits[n] for n in ("core", "y", "x", "z")]
@@ -480,28 +499,60 @@
         pltpu.make_async_copy(x_hbm, io, io_sem.at[0]),
         pltpu.make_async_copy(ct_hbm, io, io_sem.at[1]),
     ]
+    own_copies = []
+    for b in range(BLOCKS):
+        rows_of = [pl.ds((3 * b + j) * per, per) for j in range(3)]
+        pieces_of = [(qkv_w.at[b, j], ubuf.at[rows_of[0], pl.ds(j * lanes, lanes)]) for j in range(3)]
+        pieces_of.append((out_w.at[b], ubuf.at[rows_of[0], pl.ds(3 * lanes, lanes)]))
+        pieces_of.append((up_w.at[b], ubuf.at[rows_of[1], :]))
+        pieces_of.append((down_w.at[b], ubuf.at[rows_of[2], :]))
+        own_copies.append([
+            pltpu.make_async_copy(src, dst, own_sem.at[b, j]) for j, (src, dst) in enumerate(pieces_of)
+        ])
+        for cp in own_copies[b]:
+            cp.start()
     loads[0].start()
+    greet(all_peers(digits, n_tensor))
     mine = tuple(d.here() for d in dims)
-    own_copies = [
-        pltpu.make_async_copy(own.at[b], wt.at[(b,) + mine], own_sem.at[b]) for b in range(BLOCKS)
-    ]
-    own_copies.append(pltpu.make_async_copy(side, sides.at[t_here], own_sem.at[BLOCKS]))
-    own_copies.append(pltpu.make_async_copy(rel, rels.at[t_here], own_sem.at[BLOCKS + 1]))
-    start(own_copies)
-    greet(all_peers(digits, n_tensor))
+    for b in range(BLOCKS):
+        for cp in own_copies[b]:
+            cp.wait()
+        for j in range(parts):
+            row = (3 * b + j) * per
+            wt[(b,) + mine + (slice(None), slice(j * PART, (j + 1) * PART))] = ubuf[
+                row : row + per, :
+            ].astype(BF16)
+            if b * parts + j in (0, 1, late):
+                start(ag_copies(b * parts + j, 0))
+
+    rel_count = rel_w.shape[2]
+    added[0, 0:8, :] = jnp.zeros((8, GROUP * PAD), F32)
+    for b in range(BLOCKS):
+        added[0, GROUP * b : GROUP * (b + 1), 0:rel_count] = rel_w[b]
+        row = jnp.concatenate(
+            [added[0, GROUP * b + h : GROUP * b + h + 1, :] for h in range(GROUP)], 1
+        )
+        skew = jnp.broadcast_to(row, (8, row.shape[1]))
+        row_id = lax.broadcasted_iota(jnp.int32, skew.shape, 0)
+        for bit in (1, 2, 4):
+            skew = jnp.where((row_id & bit) != 0, pltpu.roll(skew, skew.shape[1] - bit, 1), skew)
+        wide = jnp.concatenate(
+            [skew]
+            + [pltpu.roll(skew, skew.shape[1] - 8 * a, 1) for a in range(1, rel_down.shape[0] // 8)], 0
+        )
+        wide = dot(rel_down[...], wide.astype(BF16), TN).astype(BF16)
+        rels[t_here, b] = dot(wide, rel_across[...], NT).astype(BF16)
+        sides[t_here, 2 * b : 2 * b + 2, 0:lanes] = qv_w[b]
+    sides[t_here, 2 * BLOCKS : 3 * BLOCKS, :] = hid_w[...]
     side_copies = [
         pltpu.make_async_remote_copy(
-            src_ref=src, dst_ref=dst.at[t_here], send_sem=ssem.at[j], recv_sem=rsem.at[j],
+            src_ref=ref.at[t_here], dst_ref=ref.at[t_here], send_sem=ssem.at[j], recv_sem=rsem.at[j],
             device_id=device, device_id_type=MESH)
-        for src, dst, ssem, rsem in (
-            (rel, rels, rel_send, rel_recv), (side, sides, side_send, side_recv)
-        )
+        for ref, ssem, rsem in ((rels, rel_send, rel_recv), (sides, side_send, side_recv))
         for j, device in enumerate(tensor_peers(n_tensor))
     ]
-    start(ag_copies(0, 0))
     start(side_copies)
-    for p in range(1, pairs):
-        start(ag_copies(p, 0))
+    ag_step(0, 1)
 
     used = images * TOKENS
     floor = used // 8 * 8
@@ -520,15 +571,14 @@
             ).astype(BF16)
 
     first_norm(0)
+    ag_step(late, 1)
+    ag_step(1, 1)
+    ag_step(0, 2)
     loads[1].wait()
     dx[floor:rows, :] = jnp.zeros((rows - floor, width), F32)
     for i in range(images):
-        dx[i * TOKENS : (i + 1) * TOKENS, :] = io[i] * live[i]
-    for cp in own_copies:
-        cp.wait()
-    ag_step(0, 1)
-    ag_step(1, 1)
-    ag_step(0, 2)
+        live = (t_here * images + i < counts[0]).astype(F32)
+        dx[i * TOKENS : (i + 1) * TOKENS, :] = io[i] * live
     pump(0)
     for cp in side_copies:
         cp.wait()
@@ -542,9 +592,13 @@
                     call()
 
     fwd_hooks = {
-        (0, "attend"): {1: [lambda: pump(1)], 3: [lambda: pump(2)]},
-        (0, "mlp"): {2: [lambda: pump(3)]},
-        (1, "attend"): {1: [lambda: pump(4)], 3: [lambda: pump(5)]},
+        (0, "attend"): {
+            0: [lambda: ag_step(3, 1)],
+            2: [lambda: ag_step(2, 2)],
+            3: [lambda: ag_step(1, 3), lambda: ag_step(late, 2)],
+        },
+        (0, "up"): {1: [lambda: ag_step(4, 1)], 3: [lambda: ag_step(3, 2)]},
+        (1, "attend"): {2: [lambda: ag_step(4, 2)]},
     }
 
     att_keeps = [
@@ -574,21 +628,29 @@
                     part = part + sides[t, at : at + 1, 0:lanes].astype(BF16).astype(F32)
                 qkv[t, :, j * lanes : (j + 1) * lanes] = part.astype(BF16)
 
-            def window(w, c2):
-                r = pl.multiple_of(w * PAD, PAD)
-                q = qkv[t, pl.ds(r, PAD), 0:lanes]
-                k = qkv[t, pl.ds(r, PAD), lanes : 2 * lanes]
-                v = qkv[t, pl.ds(r, PAD), 2 * lanes : 3 * lanes]
-                s = dot(k, spread(q, heads), NT) * INV_ROOT
-                s = s + rels[t, b].astype(F32)
-                s = s + mask[b, lax.rem(w, WINS)].astype(F32)
-                e = jnp.exp(s - jnp.max(s, 0, keepdims=True))
-                p = (e * (1.0 / jnp.sum(e, 0, keepdims=True))).astype(BF16)
-                pts[t, w] = p
-                ow[pl.ds(r, PAD), :] = gather_diag(dot(p, v, TN), heads).astype(BF16)
+            for w in range(WINS):
+                add = rels[t, b].astype(F32) + mask[b, w].astype(F32)
+                added[w] = add * LOG2E
+
+            def window(g, c2):
+                spots = [pl.ds(pl.multiple_of((g * BATCH + j) * PAD, PAD), PAD) for j in range(BATCH)]
+                s = []
+                for spot in spots:
+                    q = qkv[t, spot, 0:lanes]
+                    k = qkv[t, spot, lanes : 2 * lanes]
+                    s.append(dot(k, spread(q, heads), NT))
+                p = []
+                for j in range(BATCH):
+                    sj = s[j] * (INV_ROOT * LOG2E) + added[lax.rem(g * BATCH + j, WINS)]
+                    e = jnp.exp2(sj - jnp.max(sj, 0, keepdims=True))
+                    p.append((e * (1.0 / jnp.sum(e, 0, keepdims=True))).astype(BF16))
+                    pts[t, g * BATCH + j] = p[j]
+                for j in range(BATCH):
+                    v = qkv[t, spots[j], 2 * lanes : 3 * lanes]
+                    ow[spots[j], :] = gather_diag(dot(p[j], v, TN), heads).astype(BF16)
                 return c2
 
-            lax.fori_loop(0, images * WINS, window, 0, unroll=2)
+            lax.fori_loop(0, images * WINS // BATCH, window, 0)
             put_rows(
                 osb.at[b, t],
                 [dot(perm_t[b, i], ow[i * IMG_PAD : (i + 1) * IMG_PAD, :]) for i in range(images)],
@@ -603,15 +665,17 @@
             y = y + dot(osb[b, t], weight(b, t, c_out, c_up), NT)
         ms[b] = xs[b] + y + off2
         norm_into(ms.at[b], a2.at[b], gains[b, 1:2, :], offs[b, 1:2, :])
-        acc[...] = ms[b] + off3
+        if b + 1 < BLOCKS:
+            acc[...] = ms[b] + off3
         if b > 0:
             for cp in mlp_keeps:
                 cp.wait()
+        if b > 0:
+            ag_step(b * parts + 1, 3)
         need(b * parts + 1)
-        need(b * parts + 2)
-
-        def mlp(t, carry):
-            hooks(t, fwd_hooks.get((b, "mlp"), {}))
+
+        def up(t, carry):
+            hooks(t, fwd_hooks.get((b, "up"), {}))
             ubuf[0:rows, :] = dot(a2[b], weight(b, t, c_up, c_down))
             at = bias_at + 2 * BLOCKS + b
             hbias = sides[t, at : at + 1, :].astype(BF16).astype(F32)
@@ -619,37 +683,33 @@
                 g, d = gelu_pair(ubuf[r : r + n, :] + hbias)
                 gl[t, r : r + n, :] = g.astype(BF16)
                 gp[t, r : r + n, :] = d.astype(BF16)
+            return carry
+
+        lax.fori_loop(0, groups, up, 0)
+        if b + 1 == BLOCKS:
+            break
+        ag_step(2, 3)
+        need(b * parts + 2)
+
+        def down(t, carry):
             acc[...] += dot(gl[t], weight(b, t, c_down, cols), NT)
             return carry
 
-        lax.fori_loop(0, groups, mlp, 0)
-        if b + 1 < BLOCKS:
-            start(mlp_keeps)
-            xs[b + 1] = acc[...]
-    for i in range(images):
-        io[i] = acc[i * TOKENS : (i + 1) * TOKENS, :]
-    x_store = pltpu.make_async_copy(io, xo_hbm, io_sem.at[0])
-    x_store.start()
+        lax.fori_loop(0, groups, down, 0)
+        start(mlp_keeps)
+        xs[b + 1] = acc[...]
+        ag_step(3, 3)
 
     last = BLOCKS - 1
     back_hooks = {
-        (1, "attend"): {
-            0: [lambda: rs_step(1, 2, 1)],
-            1: [lambda: rs_step(1, 1, 1)],
-            2: [lambda: rs_step(1, 2, 2)],
-            3: [lambda: rs_step(1, 1, 2)],
-        },
-        (0, "mlp"): {
-            0: [lambda: rs_step(1, 0, 1)],
-            1: [lambda: rs_step(1, 2, 3)],
-            2: [lambda: rs_step(1, 1, 3)],
-            3: [lambda: rs_step(1, 0, 2)],
-        },
+        (1, "mlp"): {3: [lambda: rs_step(1, 2, 1)]},
+        (1, "attend"): {2: [lambda: rs_step(1, 1, 2)]},
+        (0, "mlp"): {0: [lambda: rs_step(1, 0, 1)], 3: [lambda: rs_step(1, 2, 2)]},
         (0, "attend"): {
-            0: [lambda: rs_step(0, 2, 1), lambda: rs_finish(1, 2)],
-            1: [lambda: rs_step(0, 1, 1), lambda: rs_finish(1, 1)],
-            2: [lambda: rs_step(0, 2, 2), lambda: rs_step(1, 0, 3)],
-            3: [lambda: rs_step(0, 1, 2), lambda: rs_finish(1, 0)],
+            0: [lambda: rs_step(1, 2, 3)],
+            1: [lambda: rs_finish(1, 1), lambda: rs_step(1, 0, 3)],
+            2: [lambda: rs_step(0, 1, 2)],
+            3: [lambda: rs_finish(1, 2)],
         },
     }
     mlp_loads = [
@@ -666,7 +726,6 @@
         cut[...] = dx[...].astype(BF16)
         dxt = jnp.transpose(cut[...])
         a_t = jnp.transpose(a2[b])
-        acc[...] = jnp.zeros_like(acc)
         if b < last:
             for p in range(last * parts, (last + 1) * parts):
                 for phase in range(phases):
@@ -674,9 +733,19 @@
             for cp in mlp_loads:
                 cp.wait()
 
+        def down_back(t, carry):
+            put_grad(b, t, c_down, cols, dot(dxt, gl[t]))
+            return carry
+
+        lax.fori_loop(0, groups, down_back, 0)
+        start(rs_copies(b, 2, 0))
+        if b == last:
+            ag_step(late, 3)
+            need(late)
+        acc[...] = jnp.zeros_like(acc)
+
         def mlp_back(t, carry):
             hooks(t, back_hooks.get((b, "mlp"), {}))
-            put_grad(b, t, c_down, cols, dot(dxt, gl[t]))
             dh = dot(cut[...], weight(b, t, c_down, cols))
             du = (dh * gp[t].astype(F32)).astype(BF16)
             gp[t] = du
@@ -688,10 +757,27 @@
             return carry
 
         lax.fori_loop(0, groups, mlp_back, 0)
-        start(rs_copies(b, 2, 0))
         start(rs_copies(b, 1, 0))
         if b == last:
+            result = ubuf
+            off3 = offs[b, 3:4, :].astype(BF16).astype(F32)
+            result[0:rows, :] = ms[b] + off3
+
+            def down(t, carry):
+                result[0:rows, :] += dot(gl[t], weight(b, t, c_down, cols), NT)
+                return carry
+
+            lax.fori_loop(0, groups, down, 0)
+            for i in range(images):
+                io[i] = result[i * TOKENS : (i + 1) * TOKENS, :]
+            x_store = pltpu.make_async_copy(io, xo_hbm, io_sem.at[0])
+            x_store.start()
             start(mlp_loads)
+            rs_step(1, 1, 1)
+        else:
+            rs_step(1, 0, 2)
+            rs_step(0, 2, 1)
+            rs_step(0, 1, 1)
         sums = back_norm(ms.at[b], acc, gains[b, 1:2, :], dx)
         small[GAIN_ROW + 2 * b + 1 : GAIN_ROW + 2 * b + 2, :] = sums[0]
         small[bias_row + 1 : bias_row + 2, :] = sums[1]
@@ -717,26 +803,28 @@
                 ).astype(BF16)
             dsum[...] = jnp.zeros_like(dsum)
 
-            def window(w, c2):
-                r = pl.multiple_of(w * PAD, PAD)
-                q = qkv[t, pl.ds(r, PAD), 0:lanes]
-                k = qkv[t, pl.ds(r, PAD), lanes : 2 * lanes]
-                v = qkv[t, pl.ds(r, PAD), 2 * lanes : 3 * lanes]
-                p = pts[t, w]
-                dob = spread(ow[pl.ds(r, PAD), :], heads)
-                dp = dot(v, dob, NT)
-                pf = p.astype(F32)
-                ds = (pf * (dp - jnp.sum(pf * dp, 0, keepdims=True))).astype(BF16)
-                dsum[...] += ds.astype(F32)
-                dv = dot(p, dob)
-                dk = dot(ds, spread(q, heads)) * INV_ROOT
-                dq = gather_diag(dot(ds, k, TN), heads) * INV_ROOT
-                dwin[pl.ds(r, PAD), 0:lanes] = dq.astype(BF16)
-                dwin[pl.ds(r, PAD), lanes : 2 * lanes] = dk.astype(BF16)
-                dwin[pl.ds(r, PAD), 2 * lanes : 3 * lanes] = dv.astype(BF16)
+            def window(g, c2):
+                spots = [pl.ds(pl.multiple_of((g * BATCH + j) * PAD, PAD), PAD) for j in range(BATCH)]
+                dob = [spread(ow[spot, :], heads) for spot in spots]
+                dp = [dot(qkv[t, spots[j], 2 * lanes : 3 * lanes], dob[j], NT) for j in range(BATCH)]
+                ds = []
+                for j in range(BATCH):
+                    p = pts[t, g * BATCH + j]
+                    dv = dot(p, dob[j])
+                    dwin[spots[j], 2 * lanes : 3 * lanes] = dv.astype(BF16)
+                    pf = p.astype(F32)
+                    ds.append((pf * (dp[j] - jnp.sum(pf * dp[j], 0, keepdims=True))).astype(BF16))
+                dsum[...] += sum(d.astype(F32) for d in ds)
+                for j in range(BATCH):
+                    q = qkv[t, spots[j], 0:lanes]
+                    k = qkv[t, spots[j], lanes : 2 * lanes]
+                    dk = dot(ds[j], spread(q, heads)) * INV_ROOT
+                    dwin[spots[j], lanes : 2 * lanes] = dk.astype(BF16)
+                    dq = gather_diag(dot(ds[j], k, TN), heads) * INV_ROOT
+                    dwin[spots[j], 0:lanes] = dq.astype(BF16)
                 return c2
 
-            lax.fori_loop(0, images * WINS, window, 0, unroll=2)
+            lax.fori_loop(0, images * WINS // BATCH, window, 0)
             col = pl.ds(pl.multiple_of(t * lanes, lanes), lanes)
             for j in range(2):
                 val = dwin[:, 2 * j * lanes : (2 * j + 1) * lanes].astype(F32)
@@ -768,6 +856,7 @@
         start(rs_copies(b, 0, 0))
         if b == last:
             start(att_loads)
+            rs_step(1, 1, 3)
         vals = []
         for i in range(images):
             part = da[i * IMG_PAD : (i + 1) * IMG_PAD, :]
@@ -780,20 +869,22 @@
         small[bias_row : bias_row + 1, :] = sums[1]
     small_step(0)
     rs_step(0, 0, 1)
+    rs_finish(1, 0)
+    rs_step(0, 1, 3)
     x_store.wait()
     for i in range(images):
         io[i] = dx[i * TOKENS : (i + 1) * TOKENS, :]
     dx_store = pltpu.make_async_copy(io, dxo_hbm, io_sem.at[1])
     dx_store.start()
     small_step(1)
+    rs_step(0, 0, 2)
+    rs_step(0, 2, 2)
+    small_step(2)
+    rs_finish(0, 1)
+    rs_step(0, 0, 3)
     rs_step(0, 2, 3)
-    rs_step(0, 0, 2)
-    small_step(2)
-    rs_step(0, 1, 3)
+    small_step(3)
     rs_finish(0, 2)
-    small_step(3)
-    rs_step(0, 0, 3)
-    rs_finish(0, 1)
     small_step(4)
     rs_finish(0, 0)
     dx_store.wait()
@@ -808,12 +899,11 @@
         sent(small_copies(phase))
 
 
-def block_call(x, ct, live, own, rel, side, gains, offs, n_fsdp, n_tensor):
+def block_call(x, ct, counts, mats, rel, qv, hidden, gains, offs, n_fsdp, n_tensor):
     images, _, width = x.shape
-    cols = own.shape[2]
-    per = own.shape[1]
-    lanes = GROUP * HEAD_DIM
-    hid = (cols - 4 * lanes) // 2
+    per, lanes = mats[1].shape[1:]
+    hid = mats[2].shape[2]
+    cols = 4 * lanes + 2 * hid
     parts = cols // PART
     rows = -(-images * TOKENS // 16) * 16
     wrows = images * IMG_PAD
@@ -833,11 +923,10 @@
     )
     small_rows = rel_row(n_tensor) + BLOCKS * n_tensor * GROUP
     stages = []
-    for order in orders(digits):
-        order = order[::-1]
-        for phase, digit in enumerate(order):
-            left = tuple(d.size for d in dims if d not in order[: phase + 1])
-            stages.append(pltpu.VMEM((BLOCKS, parts, digit.size - 1) + left + (per, HALF), BF16))
+    for b, part, h, phase in stage_keys(parts, phases):
+        order = reduce_order(digits, b, part, h)
+        left = tuple(d.size for d in dims if d not in order[: phase + 1])
+        stages.append(pltpu.VMEM((order[phase].size - 1,) + left + (per, HALF), BF16))
     small_order = [digits[n] for n in ("core", "y", "x", "z")]
     vmem = pl.BlockSpec(memory_space=pltpu.VMEM)
     anyspace = pl.BlockSpec(memory_space=pl.ANY)
@@ -856,13 +945,14 @@
         ) + tuple(jax.ShapeDtypeStruct(s, BF16) for s in keep),
         in_specs=[
             anyspace, anyspace, pl.BlockSpec(memory_space=pltpu.SMEM), anyspace, anyspace, anyspace,
-        ] + [vmem] * 7,
+            anyspace,
+        ] + [vmem] * 10,
         out_specs=(anyspace, anyspace, vmem, vmem) + (anyspace,) * 4,
         scratch_shapes=[
             pltpu.VMEM((BLOCKS,) + sizes + (per, cols), BF16),
             pltpu.VMEM(sizes + (per, cols), BF16),
-            pltpu.VMEM((n_tensor,) + rel.shape, BF16),
-            pltpu.VMEM((n_tensor,) + side.shape, F32),
+            pltpu.VMEM((n_tensor, BLOCKS, PAD, GROUP * PAD), BF16),
+            pltpu.VMEM((n_tensor, 8, hid), F32),
             pltpu.VMEM(x.shape, F32),
             pltpu.VMEM((BLOCKS, rows, width), F32),
             pltpu.VMEM((BLOCKS, rows, width), F32),
@@ -881,34 +971,50 @@
             pltpu.VMEM((width, wrows), BF16),
             pltpu.VMEM((wrows, 3 * lanes), BF16),
             pltpu.VMEM((PAD, GROUP * PAD), F32),
+            pltpu.VMEM((WINS, PAD, GROUP * PAD), F32),
             pltpu.VMEM((small_rows, width), F32),
         ]
         + stages
         + [pltpu.VMEM((d.size, small_rows, width), F32) for d in small_order]
         + [
-            dma((2,)), dma((BLOCKS + 2,)), dma((4,)),
+            dma((2,)), dma((BLOCKS, 6)), dma((4,)),
             dma((n_tensor - 1,)), dma((n_tensor - 1,)), dma((n_tensor - 1,)), dma((n_tensor - 1,)),
             dma((BLOCKS * parts, 2, phases, most)), dma((BLOCKS * parts, 2, phases, most)),
             dma((BLOCKS, parts, 2, phases, most)), dma((BLOCKS, parts, 2, phases, most)),
             dma((phases, most)), dma((phases, most)),
         ],
         compiler_params=pltpu.CompilerParams(
-            collective_id=0, has_side_effects=True, vmem_limit_bytes=127 * MIB // 2
+            has_side_effects=True, vmem_limit_bytes=127 * MIB // 2,
+            collective_id=0,
         ),
-    )(x, ct, live, own, rel, side, consts[0], gains, offs, *consts[1:])
+    )(x, ct, counts, *mats, rel, qv, hidden, consts[0], gains, offs, *consts[1:])
     return out[:4]
 
 
-def adam_kernel(groups, gsum, total, slot, *refs):
-    params = [refs[3 * j : 3 * j + 3] for j in range(9)]
-    outs = [refs[27 + 3 * j : 30 + 3 * j] for j in range(9)]
+def adam_kernel(groups, slot, *refs):
+    count = 31
+    ins, outs = refs[:count], refs[count : 2 * count - 2]
+    held, sem = refs[2 * count - 2 : -1], refs[-1]
+    copies = [
+        pltpu.make_async_copy(src, dst, sem.at[j]) for j, (src, dst) in enumerate(zip(ins, held))
+    ]
+    for cp in copies:
+        cp.start()
+    for cp in copies:
+        cp.wait()
+    passed = [pltpu.make_async_copy(held[j], outs[j], sem.at[j]) for j in range(2)]
+    for cp in passed:
+        cp.start()
+    gsum, total = held[2:4]
+    params = [held[4 + 3 * j : 7 + 3 * j] for j in range(9)]
+    news = [outs[2 + 3 * j : 5 + 3 * j] for j in range(9)]
     lanes = GROUP * HEAD_DIM
     hid = params[2][0].shape[2]
     t = slot[0]
 
     def update(kind, place, grad, rate, decay):
         new = adam(*(p[place] for p in params[kind]), grad, rate, decay)
-        for ref, val in zip(outs[kind], new):
+        for ref, val in zip(news[kind], new):
             ref[place] = val
 
     for b in range(BLOCKS):
@@ -920,56 +1026,50 @@
         heads, rels = params[4][0].shape[1:]
         at = rel_row(groups) + b * groups * heads
         hid_at = HID_ROW + b * groups
+        qv_rows = slice(QV_ROW + 2 * b, QV_ROW + 2 * b + 2)
         rel = pick(t, [total[at + i * heads : at + (i + 1) * heads, 0:rels] for i in range(groups)])
-        qv = pick(t, [total[QV_ROW + 2 * b : QV_ROW + 2 * b + 2, i * lanes : (i + 1) * lanes] for i in range(groups)])
+        qv = pick(t, [total[qv_rows, i * lanes : (i + 1) * lanes] for i in range(groups)])
         hidden = pick(t, [total[hid_at + i : hid_at + i + 1, :] for i in range(groups)])
         update(4, (b,), rel, SMALL_RATE, 0.0)
         update(5, (b,), qv, SMALL_RATE, 0.0)
         update(6, (slice(b, b + 1),), hidden, SMALL_RATE, 0.0)
         update(7, (b,), total[GAIN_ROW + 2 * b : GAIN_ROW + 2 * b + 2, :], SMALL_RATE, 0.0)
         update(8, (b,), total[BIAS_ROW + 4 * b : BIAS_ROW + 4 * b + 4, :], SMALL_RATE, 0.0)
-
-
-def adam_call(gsum, total, params, n_tensor):
+    for cp in passed:
+        cp.wait()
+
+
+def adam_call(x, dx, gsum, total, params, n_tensor):
+    flat = [p for group in params for p in group]
+    ins = [x, dx, gsum, total] + flat
+    hbm = pl.BlockSpec(memory_space=pltpu.HBM)
     vmem = pl.BlockSpec(memory_space=pltpu.VMEM)
-    flat = [p for group in params for p in group]
     slot = lax.axis_index("tensor").astype(jnp.int32).reshape(1)
     return pl.pallas_call(
         functools.partial(adam_kernel, n_tensor),
-        out_shape=tuple(jax.ShapeDtypeStruct(p.shape, p.dtype) for p in flat),
-        in_specs=[vmem, vmem, pl.BlockSpec(memory_space=pltpu.SMEM)] + [vmem] * len(flat),
-        out_specs=tuple(vmem for _ in flat),
-        compiler_params=pltpu.CompilerParams(vmem_limit_bytes=32 * MIB),
-    )(gsum, total, slot, *flat)
+        out_shape=tuple(jax.ShapeDtypeStruct(p.shape, p.dtype) for p in [x, dx] + flat),
+        in_specs=[pl.BlockSpec(memory_space=pltpu.SMEM)] + [hbm] * len(ins),
+        out_specs=(hbm, hbm) + tuple(vmem for _ in flat),
+        scratch_shapes=[pltpu.VMEM(p.shape, p.dtype) for p in ins]
+        + [pltpu.SemaphoreType.DMA((len(ins),))],
+        compiler_params=pltpu.CompilerParams(vmem_limit_bytes=127 * MIB // 2),
+    )(slot, *ins)
 
 
 def shards(n_fsdp, n_tensor, *args):
     image_rows, cotangent, live_counts = args[:3]
-    qkv, out, up, down, rel, qv, hidden, gain, bias = [args[3 + 3 * j : 6 + 3 * j] for j in range(9)]
-    qkv = tuple(p.transpose(0, 2, 1, 3) for p in qkv)
-    out = tuple(p.swapaxes(1, 2) for p in out)
-    down = tuple(p.swapaxes(1, 2) for p in down)
-    images = image_rows.shape[0]
-    slots = lax.axis_index("tensor") * images + jnp.arange(images, dtype=jnp.int32)
-    live = (slots < live_counts[0]).astype(F32)
-    own = jnp.concatenate([qkv[0][:, j] for j in range(3)] + [out[0], up[0], down[0]], 2).astype(BF16)
-    heads, rels = rel[0].shape[1:]
-    onehot = jnp.asarray(rel_onehot(rels).reshape(rels, -1), BF16)
-    rel_own = lax.dot_general(
-        rel[0].astype(BF16), onehot, (((2,), (0,)), ((), ())), preferred_element_type=F32
+    groups = [args[3 + 3 * j : 6 + 3 * j] for j in range(9)]
+    turn = {0: lambda p: p.transpose(0, 2, 1, 3), 1: lambda p: p.swapaxes(1, 2), 3: lambda p: p.swapaxes(1, 2)}
+    for j, f in turn.items():
+        groups[j] = [f(p) for p in groups[j]]
+    mats = [g[0] for g in groups[:4]]
+    rel, qv, hidden, gain, bias = [g[0] for g in groups[4:]]
+    x, dx, gsum, total = block_call(
+        image_rows, cotangent, live_counts, mats, rel, qv, hidden, gain, bias, n_fsdp, n_tensor
     )
-    rel_own = rel_own.astype(BF16).reshape(BLOCKS, heads, PAD, PAD)
-    rel_own = rel_own.swapaxes(1, 2).reshape(BLOCKS, PAD, heads * PAD)
-    hid = hidden[0].shape[1]
-    side = jnp.concatenate(
-        [jnp.pad(qv[0].reshape(2 * BLOCKS, -1), ((0, 0), (0, hid - qv[0].shape[2]))), hidden[0],
-         jnp.zeros((8 - 3 * BLOCKS, hid), F32)], 0)
-    x_out, dx_out, gsum, total = block_call(
-        image_rows, cotangent, live, own, rel_own, side, gain[0], bias[0], n_fsdp, n_tensor
-    )
-    new = adam_call(gsum, total, (qkv, out, up, down, rel, qv, hidden, gain, bias), n_tensor)
-    new = [list(new[3 * j : 3 * j + 3]) for j in range(9)]
-    new[0] = [p.transpose(0, 2, 1, 3) for p in new[0]]
-    new[1] = [p.swapaxes(1, 2) for p in new[1]]
-    new[3] = [p.swapaxes(1, 2) for p in new[3]]
-    return (x_out, dx_out) + tuple(p for group in new for p in group)
+    new = adam_call(x, dx, gsum, total, groups, n_tensor)
+    x, dx = new[:2]
+    new = [list(new[2 + 3 * j : 5 + 3 * j]) for j in range(9)]
+    for j, f in turn.items():
+        new[j] = [f(p) for p in new[j]]
+    return (x, dx) + tuple(p for group in new for p in group)

time: 249 us -> 183 us (0.73)
  Pallas kernels: 213 us -> 181 us
  local copies, waits for them, and re-layouts: 27.3 us -> 0 us
  other arithmetic: 3.87 us -> 0 us
    pallas_call x1, Pallas kernels: 211 us -> 175 us  [block_call(): pl.pallas_call(functools.partial(block_kernel, n_fsdp, n_tensor), out_sha...]
    unnamed x72 -> x0, local copies, waits for them, and re-layouts: 26.2 us -> none
    pallas_call x1, Pallas kernels: 1.94 us -> 5.95 us  [adam_call(): pl.pallas_call(functools.partial(adam_kernel, n_tensor), out_shape=tuple(...]
where the time goes in v3:
time: 183 us; the launch traced here: 182 us
  Pallas kernels  181 us (99%)
    pallas_call x1, Pallas kernels, block_call(): pl.pallas_call(functools.partial(block_kernel, n_fsdp, n_tensor), out_sha...  175 us
    pallas_call x1, Pallas kernels, adam_call(): pl.pallas_call(functools.partial(adam_kernel, n_tensor), out_shape=tuple(...  5.95 us

profile of v3, /device:TPU:0, one launch (start us, length us, event | category | flops | bytes accessed | tf_op | source)
XLA Modules:
  0.0 182.4 jit_solution(17614240243901297018)
XLA Ops:
  1.3 174.9 %shard_map.554 = (f32[3,196,512]{2,1,0:T(8,128)}, f32[3,196,512]{2,1,0:T(8,128)}, f32[2,64,1536]{2,1,0:T(8,128)}, f32[56,512]{1,0:T(8,128)}, bf16[4,592,512]{2,1...) custom-call(f32[3,196,512]{2,1,0:T(8,128)} %x_hbm.1, ...), custom_call_target="tpu_custom_call" | custom-call | tf_op jit(solution)/shard_map/pallas_call | solution.py:938
  176.2 5.9 %shard_map.555 = (f32[3,196,512]{2,1,0:T(8,128)}, f32[3,196,512]{2,1,0:T(8,128)}, f32[2,3,64,128]{3,2,1,0:T(8,128)}, f32[2,3,64,128]{3,2,1,0:T(8,128)}, f32[2,3,...) custom-call(s32[1]{0:T(128)} %bitcast.slot, ...), custom_call_target="tpu_custom_call" | custom-call | tf_op jit(solution)/shard_map/pallas_call | solution.py:1048

commit v4 on v3

--- a/solution.py
+++ b/solution.py
@@ -276,12 +276,84 @@
 PART = 512
 HALF = 256
 REL_LANES = 256
+BATCH = 12
+LOG2E = 1.4426950408889634
 Z_FIRST = (("z", "x", "y", "core"), ("z", "y", "x", "core"))
 Z_LATE = (("x", "y", "z", "core"), ("y", "x", "z", "core"))
-GATHER_LATE = ((1, 2),)
-REDUCE_LATE = ((1, 2), (0, 2))
-BATCH = 12
-LOG2E = 1.4426950408889634
+Z_MID = (("x", "z", "y", "core"), ("y", "z", "x", "core"))
+GATHER = (
+    (0, 0, 256, Z_FIRST),
+    (0, 256, 256, Z_FIRST),
+    (0, 512, 256, Z_FIRST),
+    (0, 768, 256, Z_FIRST),
+    (0, 1024, 256, Z_FIRST),
+    (0, 1280, 256, Z_FIRST),
+    (1, 0, 256, Z_FIRST),
+    (1, 256, 256, Z_FIRST),
+    (1, 512, 256, Z_LATE),
+    (1, 768, 256, Z_FIRST),
+    (1, 1024, 256, Z_MID),
+    (1, 1280, 256, Z_LATE),
+)
+REDUCE = (
+    (1, 1024, 256, Z_FIRST),
+    (1, 1280, 256, Z_LATE),
+    (1, 512, 256, Z_FIRST),
+    (1, 768, 256, Z_FIRST),
+    (1, 0, 256, Z_MID),
+    (1, 256, 256, Z_LATE),
+    (0, 1024, 256, Z_FIRST),
+    (0, 1280, 256, Z_FIRST),
+    (0, 512, 256, Z_FIRST),
+    (0, 768, 256, Z_FIRST),
+    (0, 0, 256, Z_MID),
+    (0, 256, 256, Z_FIRST),
+)
+SCHEDULE = {
+    "start": (("ag", 0, 0), ("ag", 1, 0), ("ag", 8, 0), ("ag", 10, 0), ("ag", 11, 0)),
+    "x0": (("ag", 2, 0),),
+    "dx": (("ag", 3, 0), ("ag", 0, 1), ("ag", 8, 1), ("ag", 11, 1)),
+    "need0": (("ag", 4, 0), ("ag", 1, 1), ("ag", 0, 2), ("ag", 5, 0), ("ag", 2, 1), ("ag", 1, 2), ("ag", 6, 0), ("ag", 3, 1), ("ag", 0, 3), ("ag", 7, 0), ("ag", 2, 2), ("ag", 4, 1), ("ag", 8, 2), ("ag", 1, 3), ("ag", 5, 1), ("ag", 3, 2)),
+    ("attend0", 1): (("ag", 2, 3), ("ag", 6, 1)),
+    ("attend0", 2): (("ag", 4, 2),),
+    ("attend0", 3): (("ag", 5, 2),),
+    "need1": (("ag", 3, 3), ("ag", 7, 1), ("ag", 9, 0), ("ag", 6, 2)),
+    ("up0", 0): (("ag", 10, 1),),
+    ("up0", 1): (("ag", 4, 3),),
+    ("up0", 3): (("ag", 5, 3),),
+    "need2": (("ag", 8, 3), ("ag", 7, 2), ("ag", 11, 2)),
+    ("down0", 1): (("ag", 9, 1),),
+    ("down0", 2): (("ag", 6, 3),),
+    "need3": (("ag", 7, 3), ("ag", 9, 2), ("ag", 10, 2)),
+    ("attend1", 3): (("ag", 9, 3),),
+    "need4": (("ag", 10, 3),),
+    "dxt1": (("ag", 11, 3),),
+    "sent12": (("rs", 0, 0), ("rs", 1, 0)),
+    ("mlpb1", 2): (("rs", 0, 1), ("rs", 1, 1)),
+    "sent11": (("rs", 2, 0), ("rs", 3, 0)),
+    ("result1", 1): (("rs", 0, 2),),
+    ("result1", 3): (("rs", 2, 1),),
+    "lnb1": (("rs", 3, 1),),
+    ("attb1", 0): (("rs", 0, 3),),
+    ("attb1", 1): (("rs", 2, 2),),
+    ("attb1", 2): (("rs", 1, 2), ("rs", 3, 2)),
+    ("attb1", 3): (("fin", 0, 0), ("rs", 1, 3), ("rs", 2, 3)),
+    "sent10": (("fin", 1, 0), ("rs", 3, 3), ("rs", 4, 0), ("rs", 5, 0)),
+    ("downb0", 0): (("fin", 2, 0),),
+    ("downb0", 1): (("rs", 4, 1),),
+    ("downb0", 2): (("rs", 5, 1),),
+    "sent02": (("fin", 3, 0), ("rs", 6, 0), ("rs", 7, 0)),
+    ("mlpb0", 2): (("rs", 6, 1), ("rs", 7, 1)),
+    ("mlpb0", 3): (("rs", 4, 2),),
+    "sent01": (("rs", 8, 0), ("rs", 9, 0)),
+    ("attb0", 0): (("rs", 6, 2), ("rs", 8, 1), ("rs", 7, 2), ("rs", 9, 1)),
+    ("attb0", 2): (("rs", 5, 2), ("rs", 6, 3)),
+    ("attb0", 3): (("rs", 4, 3), ("rs", 7, 3), ("rs", 8, 2)),
+    "sent00": (("fin", 6, 0), ("rs", 9, 2), ("rs", 10, 0), ("rs", 11, 0)),
+    "ln1b0": (("fin", 4, 0), ("rs", 5, 3)),
+    "end0": (("small", 0, 0), ("fin", 7, 0), ("rs", 8, 3), ("rs", 10, 1), ("rs", 9, 3), ("fin", 5, 0), ("small", 0, 1), ("rs", 11, 1)),
+    "end": (("fin", 8, 0), ("rs", 10, 2), ("small", 0, 2), ("fin", 9, 0), ("rs", 11, 2), ("small", 0, 3), ("rs", 11, 3), ("rs", 10, 3), ("small", 0, 4), ("fin", 10, 0), ("fin", 11, 0)),
+}
 
 
 def rel_consts():
@@ -297,22 +369,8 @@
     return down, across
 
 
-def stage_keys(parts, phases):
-    return [
-        (b, part, h, phase)
-        for b in range(BLOCKS)
-        for part in range(parts)
-        for h in range(2)
-        for phase in range(phases)
-    ]
-
-
-def gather_order(digits, b, part, half):
-    return [digits[n] for n in (Z_LATE if (b, part) in GATHER_LATE else Z_FIRST)[half]]
-
-
-def reduce_order(digits, b, part, half):
-    return [digits[n] for n in (Z_LATE if (b, part) in REDUCE_LATE else Z_FIRST)[half]][::-1]
+def stage_keys(phases):
+    return [(q, h, phase) for q in range(len(REDUCE)) for h in range(2) for phase in range(phases)]
 
 
 def block_kernel(
@@ -326,9 +384,8 @@
     dims = sorted(digits.values(), key=lambda d: d.dim)
     phases = len(dims)
     parts = wt.shape[-1] // PART
-    pairs = BLOCKS * parts
     stage = {}
-    for at, key in enumerate(stage_keys(parts, phases)):
+    for at, key in enumerate(stage_keys(phases)):
         stage[key] = rest[at]
     rest = rest[len(stage) :]
     small_slots = rest[:phases]
@@ -363,80 +420,93 @@
         grad_ref(b)[index] = value.astype(BF16).reshape(fshape + (hi - lo,))
 
     def ag_copies(p, phase):
-        b, c = p // parts, (p % parts) * PART
+        b, c, n, names = GATHER[p]
         out = []
         for h in range(2):
-            order = gather_order(digits, b, p % parts, h)
+            order = [digits[name] for name in names[h]]
             digit = order[phase]
-            at = pl.ds(c + h * HALF, HALF)
+            at = pl.ds(c + h * (n // 2), n // 2)
             index = tuple(slice(None) if d in order[:phase] else d.here() for d in dims)
-            dst = wt.at[(b,) + index + (slice(None), at)]
+            place = wt.at[(b,) + index + (slice(None), at)]
             for s in range(1, digit.size):
-                sem = (p, h, phase, s - 1)
                 out.append(pltpu.make_async_remote_copy(
-                    src_ref=dst, dst_ref=dst, send_sem=ag_send.at[sem], recv_sem=ag_recv.at[sem],
-                    device_id=digit.peer(s)[1], device_id_type=MESH))
+                    src_ref=place, dst_ref=place, send_sem=ag_send.at[p, phase],
+                    recv_sem=ag_recv.at[p, phase], device_id=digit.peer(s)[1], device_id_type=MESH))
         return out
+
+    def span(ref, order, phase, full, at):
+        digit = order[phase]
+        index = tuple(
+            slice(0, digit.size - 1) if d is digit else slice(None) if d in full else d.here()
+            for d in dims
+        )
+        return ref.at[index + (slice(None), at)]
+
+    def ag_all(p, phase):
+        b, c, n, names = GATHER[p]
+        order = [digits[name] for name in names[0]]
+        place = span(wt.at[b], order, phase, order[:phase], pl.ds(c, n))
+        return pltpu.make_async_remote_copy(
+            src_ref=place, dst_ref=place, send_sem=ag_send.at[p, phase],
+            recv_sem=ag_recv.at[p, phase], device_id=order[phase].peer(1)[1], device_id_type=MESH)
 
     def start(copies):
         for cp in copies:
             cp.start()
 
-    def arrive(copies):
-        for cp in copies:
-            cp.wait_recv()
-
-    def sent(copies):
-        for cp in copies:
-            cp.wait_send()
+    def arrive(whole):
+        whole.wait_recv()
+
+    def sent(whole):
+        whole.wait_send()
 
     def ag_step(p, phase):
-        if 0 <= p < pairs:
-            arrive(ag_copies(p, phase - 1))
-            start(ag_copies(p, phase))
-            if phase == 1 and p + 2 < late:
-                start(ag_copies(p + 2, 0))
-
-    late = pairs - 1
-
-    def pump(i):
-        if i + 2 < late:
-            ag_step(i + 2, 1)
-        if i + 1 < late:
-            ag_step(i + 1, 2)
-        ag_step(i, 3)
-
-    def need(p):
-        arrive(ag_copies(p, phases - 1))
-
-    def rs_copies(b, part, phase):
+        if phase > 0:
+            arrive(ag_all(p, phase - 1))
+        start(ag_copies(p, phase))
+
+    def need(b, lo, hi):
+        for p, (block, c, n, _) in enumerate(GATHER):
+            if block == b and c < hi and lo < c + n:
+                arrive(ag_all(p, phases - 1))
+
+    def rs_copies(q, phase):
+        b, c, n, names = REDUCE[q]
         out = []
         for h in range(2):
-            order = reduce_order(digits, b, part, h)
+            order = [digits[name] for name in names[h]][::-1]
             digit = order[phase]
-            at = pl.ds(part * PART + h * HALF, HALF)
+            at = pl.ds(c + h * (n // 2), n // 2)
             for s in range(1, digit.size):
                 to, device = digit.peer(s)
                 index = tuple(
                     to if d is digit else d.here() if d in order[:phase] else slice(None) for d in dims
                 )
-                sem = (b, part, h, phase, s - 1)
                 out.append(pltpu.make_async_remote_copy(
                     src_ref=grad_ref(b).at[index + (slice(None), at)],
-                    dst_ref=stage[b, part, h, phase].at[s - 1],
-                    send_sem=rs_send.at[sem], recv_sem=rs_recv.at[sem],
+                    dst_ref=stage[q, h, phase].at[s - 1],
+                    send_sem=rs_send.at[q, phase], recv_sem=rs_recv.at[q, phase],
                     device_id=device, device_id_type=MESH))
         return out
 
-    def rs_absorb(b, part, phase):
+    def rs_all(q, phase):
+        b, c, n, names = REDUCE[q]
+        order = [digits[name] for name in names[0]][::-1]
+        place = span(grad_ref(b), order, phase, order[phase + 1 :], pl.ds(c, n))
+        return pltpu.make_async_remote_copy(
+            src_ref=place, dst_ref=place, send_sem=rs_send.at[q, phase],
+            recv_sem=rs_recv.at[q, phase], device_id=order[phase].peer(1)[1], device_id_type=MESH)
+
+    def rs_absorb(q, phase):
+        b, c, n, names = REDUCE[q]
         grad = grad_ref(b)
         for h in range(2):
-            order = reduce_order(digits, b, part, h)
+            order = [digits[name] for name in names[h]][::-1]
             digit = order[phase]
-            at = slice(part * PART + h * HALF, part * PART + (h + 1) * HALF)
+            at = slice(c + h * (n // 2), c + (h + 1) * (n // 2))
             left = [d for d in dims if d not in order[: phase + 1]]
-            land = stage[b, part, h, phase]
-            steps = int(np.prod([d.size for d in left]))
+            land = stage[q, h, phase]
+            steps = int(np.prod([d.size for d in left])) if left else 1
 
             def one(i, carry):
                 place = {}
@@ -453,21 +523,41 @@
 
             lax.fori_loop(0, steps, one, 0, unroll=min(steps, 4))
 
-    def rs_step(b, part, phase):
-        arrive(rs_copies(b, part, phase - 1))
-        rs_absorb(b, part, phase - 1)
-        start(rs_copies(b, part, phase))
-
-    def rs_finish(b, part):
-        arrive(rs_copies(b, part, phases - 1))
+    def rs_step(q, phase):
+        if phase > 0:
+            arrive(rs_all(q, phase - 1))
+            rs_absorb(q, phase - 1)
+        start(rs_copies(q, phase))
+
+    def rs_finish(q):
+        arrive(rs_all(q, phases - 1))
+        b, c, n, names = REDUCE[q]
         for h in range(2):
-            digit = reduce_order(digits, b, part, h)[-1]
-            at = slice(part * PART + h * HALF, part * PART + (h + 1) * HALF)
+            at = slice(c + h * (n // 2), c + (h + 1) * (n // 2))
             index = tuple(d.here() for d in dims)
             value = grad_ref(b)[index + (slice(None), at)].astype(F32)
-            for s in range(digit.size - 1):
-                value = value + stage[b, part, h, phases - 1][s].astype(F32)
+            for s in range(digits[names[h][0]].size - 1):
+                value = value + stage[q, h, phases - 1][s].astype(F32)
             gsum[b, :, at] = value
+
+    def slot(name):
+        for kind, item, phase in SCHEDULE.get(name, ()):
+            if kind == "ag":
+                ag_step(item, phase)
+            elif kind == "rs":
+                rs_step(item, phase)
+            elif kind == "fin":
+                rs_finish(item)
+            else:
+                small_step(phase)
+
+    def hooks(t, name):
+        for at in range(groups):
+            if (name, at) in SCHEDULE:
+
+                @pl.when(t == at)
+                def _():
+                    slot((name, at))
 
     small_order = [digits[n] for n in ("core", "y", "x", "z")]
 
@@ -476,16 +566,23 @@
         place = small_slots[phase].at[digit.here()]
         return [
             pltpu.make_async_remote_copy(
-                src_ref=place, dst_ref=place, send_sem=sm_send.at[phase, s - 1],
-                recv_sem=sm_recv.at[phase, s - 1], device_id=digit.peer(s)[1], device_id_type=MESH)
+                src_ref=place, dst_ref=place, send_sem=sm_send.at[phase], recv_sem=sm_recv.at[phase],
+                device_id=digit.peer(s)[1], device_id_type=MESH)
             for s in range(1, digit.size)
         ]
+
+    def small_all(phase):
+        digit = small_order[phase]
+        place = small_slots[phase].at[0 : digit.size - 1]
+        return pltpu.make_async_remote_copy(
+            src_ref=place, dst_ref=place, send_sem=sm_send.at[phase], recv_sem=sm_recv.at[phase],
+            device_id=digit.peer(1)[1], device_id_type=MESH)
 
     def small_step(phase):
         if phase == 0:
             value = small[...]
         else:
-            arrive(small_copies(phase - 1))
+            arrive(small_all(phase - 1))
             value = small_slots[phase - 1][0]
             for s in range(1, small_order[phase - 1].size):
                 value = value + small_slots[phase - 1][s]
@@ -522,8 +619,8 @@
             wt[(b,) + mine + (slice(None), slice(j * PART, (j + 1) * PART))] = ubuf[
                 row : row + per, :
             ].astype(BF16)
-            if b * parts + j in (0, 1, late):
-                start(ag_copies(b * parts + j, 0))
+
+    slot("start")
 
     rel_count = rel_w.shape[2]
     added[0, 0:8, :] = jnp.zeros((8, GROUP * PAD), F32)
@@ -552,7 +649,7 @@
         for j, device in enumerate(tensor_peers(n_tensor))
     ]
     start(side_copies)
-    ag_step(0, 1)
+    slot("x0")
 
     used = images * TOKENS
     floor = used // 8 * 8
@@ -571,35 +668,15 @@
             ).astype(BF16)
 
     first_norm(0)
-    ag_step(late, 1)
-    ag_step(1, 1)
-    ag_step(0, 2)
+    slot("dx")
     loads[1].wait()
     dx[floor:rows, :] = jnp.zeros((rows - floor, width), F32)
     for i in range(images):
         live = (t_here * images + i < counts[0]).astype(F32)
         dx[i * TOKENS : (i + 1) * TOKENS, :] = io[i] * live
-    pump(0)
+    slot("need0")
     for cp in side_copies:
         cp.wait()
-
-    def hooks(t, table):
-        for at, calls in table.items():
-
-            @pl.when(t == at)
-            def _():
-                for call in calls:
-                    call()
-
-    fwd_hooks = {
-        (0, "attend"): {
-            0: [lambda: ag_step(3, 1)],
-            2: [lambda: ag_step(2, 2)],
-            3: [lambda: ag_step(1, 3), lambda: ag_step(late, 2)],
-        },
-        (0, "up"): {1: [lambda: ag_step(4, 1)], 3: [lambda: ag_step(3, 2)]},
-        (1, "attend"): {2: [lambda: ag_step(4, 2)]},
-    }
 
     att_keeps = [
         pltpu.make_async_copy(qkv, keep_qkv, keep_sem.at[0]),
@@ -616,10 +693,12 @@
             first_norm(b)
             for cp in att_keeps:
                 cp.wait()
-        need(b * parts)
+        if b > 0:
+            slot("need3")
+        need(b, 0, c_up)
 
         def attend(t, carry):
-            hooks(t, fwd_hooks.get((b, "attend"), {}))
+            hooks(t, "attend%d" % b)
             rows_qkv = dot(aw[b], weight(b, t, 0, c_out))
             for j in range(3):
                 part = rows_qkv[:, j * lanes : (j + 1) * lanes]
@@ -660,6 +739,7 @@
         lax.fori_loop(0, groups, attend, 0)
         if b + 1 < BLOCKS:
             start(att_keeps)
+        slot("out%d" % b)
         y = dot(osb[b, 0], weight(b, 0, c_out, c_up), NT)
         for t in range(1, groups):
             y = y + dot(osb[b, t], weight(b, t, c_out, c_up), NT)
@@ -670,12 +750,11 @@
         if b > 0:
             for cp in mlp_keeps:
                 cp.wait()
-        if b > 0:
-            ag_step(b * parts + 1, 3)
-        need(b * parts + 1)
+        slot("need%d" % (1 + 3 * b))
+        need(b, c_up, c_down)
 
         def up(t, carry):
-            hooks(t, fwd_hooks.get((b, "up"), {}))
+            hooks(t, "up%d" % b)
             ubuf[0:rows, :] = dot(a2[b], weight(b, t, c_up, c_down))
             at = bias_at + 2 * BLOCKS + b
             hbias = sides[t, at : at + 1, :].astype(BF16).astype(F32)
@@ -688,30 +767,20 @@
         lax.fori_loop(0, groups, up, 0)
         if b + 1 == BLOCKS:
             break
-        ag_step(2, 3)
-        need(b * parts + 2)
+        slot("need2")
+        need(b, c_down, cols)
 
         def down(t, carry):
+            hooks(t, "down0")
             acc[...] += dot(gl[t], weight(b, t, c_down, cols), NT)
             return carry
 
         lax.fori_loop(0, groups, down, 0)
         start(mlp_keeps)
         xs[b + 1] = acc[...]
-        ag_step(3, 3)
+        slot("norm1")
 
     last = BLOCKS - 1
-    back_hooks = {
-        (1, "mlp"): {3: [lambda: rs_step(1, 2, 1)]},
-        (1, "attend"): {2: [lambda: rs_step(1, 1, 2)]},
-        (0, "mlp"): {0: [lambda: rs_step(1, 0, 1)], 3: [lambda: rs_step(1, 2, 2)]},
-        (0, "attend"): {
-            0: [lambda: rs_step(1, 2, 3)],
-            1: [lambda: rs_finish(1, 1), lambda: rs_step(1, 0, 3)],
-            2: [lambda: rs_step(0, 1, 2)],
-            3: [lambda: rs_finish(1, 2)],
-        },
-    }
     mlp_loads = [
         pltpu.make_async_copy(keep_gl, gl, keep_sem.at[2]),
         pltpu.make_async_copy(keep_gp, gp, keep_sem.at[3]),
@@ -724,28 +793,31 @@
         bias_row = BIAS_ROW + 4 * b
         small[bias_row + 3 : bias_row + 4, :] = column_sum(dx)
         cut[...] = dx[...].astype(BF16)
+        slot("dxt%d" % b)
         dxt = jnp.transpose(cut[...])
         a_t = jnp.transpose(a2[b])
         if b < last:
-            for p in range(last * parts, (last + 1) * parts):
-                for phase in range(phases):
-                    sent(ag_copies(p, phase))
+            for p in range(len(GATHER)):
+                if GATHER[p][0] == last:
+                    for phase in range(phases):
+                        sent(ag_all(p, phase))
             for cp in mlp_loads:
                 cp.wait()
 
         def down_back(t, carry):
+            hooks(t, "downb%d" % b)
             put_grad(b, t, c_down, cols, dot(dxt, gl[t]))
             return carry
 
         lax.fori_loop(0, groups, down_back, 0)
-        start(rs_copies(b, 2, 0))
+        slot("sent%d2" % b)
         if b == last:
-            ag_step(late, 3)
-            need(late)
+            slot("need5")
+            need(b, c_down, cols)
         acc[...] = jnp.zeros_like(acc)
 
         def mlp_back(t, carry):
-            hooks(t, back_hooks.get((b, "mlp"), {}))
+            hooks(t, "mlpb%d" % b)
             dh = dot(cut[...], weight(b, t, c_down, cols))
             du = (dh * gp[t].astype(F32)).astype(BF16)
             gp[t] = du
@@ -757,13 +829,15 @@
             return carry
 
         lax.fori_loop(0, groups, mlp_back, 0)
-        start(rs_copies(b, 1, 0))
+        slot("sent%d1" % b)
         if b == last:
+            slot("result")
             result = ubuf
             off3 = offs[b, 3:4, :].astype(BF16).astype(F32)
             result[0:rows, :] = ms[b] + off3
 
             def down(t, carry):
+                hooks(t, "result1")
                 result[0:rows, :] += dot(gl[t], weight(b, t, c_down, cols), NT)
                 return carry
 
@@ -773,11 +847,7 @@
             x_store = pltpu.make_async_copy(io, xo_hbm, io_sem.at[0])
             x_store.start()
             start(mlp_loads)
-            rs_step(1, 1, 1)
-        else:
-            rs_step(1, 0, 2)
-            rs_step(0, 2, 1)
-            rs_step(0, 1, 1)
+        slot("lnb%d" % b)
         sums = back_norm(ms.at[b], acc, gains[b, 1:2, :], dx)
         small[GAIN_ROW + 2 * b + 1 : GAIN_ROW + 2 * b + 2, :] = sums[0]
         small[bias_row + 1 : bias_row + 2, :] = sums[1]
@@ -794,7 +864,7 @@
                 cp.wait()
 
         def attend_back(t, carry):
-            hooks(t, back_hooks.get((b, "attend"), {}))
+            hooks(t, "attb%d" % b)
             do_t = dot(cut[...], weight(b, t, c_out, c_up)).astype(BF16)
             for i in range(images):
                 base = image_base(i)
@@ -853,10 +923,10 @@
             return carry
 
         lax.fori_loop(0, groups, attend_back, 0)
-        start(rs_copies(b, 0, 0))
+        slot("sent%d0" % b)
         if b == last:
             start(att_loads)
-            rs_step(1, 1, 3)
+        slot("ln1b%d" % b)
         vals = []
         for i in range(images):
             part = da[i * IMG_PAD : (i + 1) * IMG_PAD, :]
@@ -867,36 +937,23 @@
         sums = back_norm(xs.at[b], acc, gains[b, 0:1, :], dx)
         small[GAIN_ROW + 2 * b : GAIN_ROW + 2 * b + 1, :] = sums[0]
         small[bias_row : bias_row + 1, :] = sums[1]
-    small_step(0)
-    rs_step(0, 0, 1)
-    rs_finish(1, 0)
-    rs_step(0, 1, 3)
+    slot("end0")
     x_store.wait()
     for i in range(images):
         io[i] = dx[i * TOKENS : (i + 1) * TOKENS, :]
     dx_store = pltpu.make_async_copy(io, dxo_hbm, io_sem.at[1])
     dx_store.start()
-    small_step(1)
-    rs_step(0, 0, 2)
-    rs_step(0, 2, 2)
-    small_step(2)
-    rs_finish(0, 1)
-    rs_step(0, 0, 3)
-    rs_step(0, 2, 3)
-    small_step(3)
-    rs_finish(0, 2)
-    small_step(4)
-    rs_finish(0, 0)
+    slot("end")
     dx_store.wait()
-    for p in range(last * parts):
+    for p in range(len(GATHER)):
+        if GATHER[p][0] != last:
+            for phase in range(phases):
+                sent(ag_all(p, phase))
+    for q in range(len(REDUCE)):
         for phase in range(phases):
-            sent(ag_copies(p, phase))
-    for b in range(BLOCKS):
-        for part in range(parts):
-            for phase in range(phases):
-                sent(rs_copies(b, part, phase))
+            sent(rs_all(q, phase))
     for phase in range(phases):
-        sent(small_copies(phase))
+        sent(small_all(phase))
 
 
 def block_call(x, ct, counts, mats, rel, qv, hidden, gains, offs, n_fsdp, n_tensor):
@@ -910,7 +967,6 @@
     digits = plan(n_fsdp, n_tensor)
     dims = sorted(digits.values(), key=lambda d: d.dim)
     sizes = tuple(d.size for d in dims)
-    most = max(sizes) - 1
     phases = len(dims)
     perm = permutations(images)
     down, across = rel_consts()
@@ -923,10 +979,10 @@
     )
     small_rows = rel_row(n_tensor) + BLOCKS * n_tensor * GROUP
     stages = []
-    for b, part, h, phase in stage_keys(parts, phases):
-        order = reduce_order(digits, b, part, h)
+    for q, h, phase in stage_keys(phases):
+        order = [digits[n] for n in REDUCE[q][3][h]][::-1]
         left = tuple(d.size for d in dims if d not in order[: phase + 1])
-        stages.append(pltpu.VMEM((order[phase].size - 1,) + left + (per, HALF), BF16))
+        stages.append(pltpu.VMEM((order[phase].size - 1,) + left + (per, REDUCE[q][2] // 2), BF16))
     small_order = [digits[n] for n in ("core", "y", "x", "z")]
     vmem = pl.BlockSpec(memory_space=pltpu.VMEM)
     anyspace = pl.BlockSpec(memory_space=pl.ANY)
@@ -979,9 +1035,9 @@
         + [
             dma((2,)), dma((BLOCKS, 6)), dma((4,)),
             dma((n_tensor - 1,)), dma((n_tensor - 1,)), dma((n_tensor - 1,)), dma((n_tensor - 1,)),
-            dma((BLOCKS * parts, 2, phases, most)), dma((BLOCKS * parts, 2, phases, most)),
-            dma((BLOCKS, parts, 2, phases, most)), dma((BLOCKS, parts, 2, phases, most)),
-            dma((phases, most)), dma((phases, most)),
+            dma((len(GATHER), phases)), dma((len(GATHER), phases)),
+            dma((len(REDUCE), phases)), dma((len(REDUCE), phases)),
+            dma((phases,)), dma((phases,)),
         ],
         compiler_params=pltpu.CompilerParams(
             has_side_effects=True, vmem_limit_bytes=127 * MIB // 2,

time: 183 us -> 163 us (0.89)
  Pallas kernels: 181 us -> 161 us
    pallas_call x1, Pallas kernels: 175 us -> 155 us  [block_call(): pl.pallas_call(functools.partial(block_kernel, n_fsdp, n_tensor), out_sha...]
where the time goes in v4:
time: 163 us
  Pallas kernels  161 us (99%)
    pallas_call x1, Pallas kernels, block_call(): pl.pallas_call(functools.partial(block_kernel, n_fsdp, n_tensor), out_sha...  155 us
    pallas_call x1, Pallas kernels, adam_call(): pl.pallas_call(functools.partial(adam_kernel, n_tensor), out_shape=tuple(...  5.95 us

profile of v4, /device:TPU:0, one launch (start us, length us, event | category | flops | bytes accessed | tf_op | source)
XLA Modules:
  0.0 162.7 jit_solution(5146072055432954953)
XLA Ops:
  1.3 155.2 %shard_map.554 = (f32[3,196,512]{2,1,0:T(8,128)}, f32[3,196,512]{2,1,0:T(8,128)}, f32[2,64,1536]{2,1,0:T(8,128)}, f32[56,512]{1,0:T(8,128)}, bf16[4,592,512]{2,1...) custom-call(f32[3,196,512]{2,1,0:T(8,128)} %x_hbm.1, ...), custom_call_target="tpu_custom_call" | custom-call | tf_op jit(solution)/shard_map/pallas_call | solution.py:994
  156.6 5.9 %shard_map.555 = (f32[3,196,512]{2,1,0:T(8,128)}, f32[3,196,512]{2,1,0:T(8,128)}, f32[2,3,64,128]{3,2,1,0:T(8,128)}, f32[2,3,64,128]{3,2,1,0:T(8,128)}, f32[2,3,...) custom-call(s32[1]{0:T(128)} %bitcast.slot, ...), custom_call_target="tpu_custom_call" | custom-call | tf_op jit(solution)/shard_map/pallas_call | solution.py:1104

commit v5 on v4

--- a/solution.py
+++ b/solution.py
@@ -246,17 +246,6 @@
     return weight - rate * step, first_new, second_new
 
 
-def pick(index, values):
-    out = values[0]
-    for i in range(1, len(values)):
-        out = jnp.where(index == i, values[i], out)
-    return out
-
-
-def rel_row(groups):
-    return HID_ROW + BLOCKS * groups
-
-
 def solution(mesh):
     n_fsdp, n_tensor = mesh.shape["fsdp"], mesh.shape["tensor"]
     tokens = P(("fsdp", "tensor"), None, None)
@@ -277,6 +266,7 @@
 HALF = 256
 REL_LANES = 256
 BATCH = 12
+ABS_UNROLL = 16
 LOG2E = 1.4426950408889634
 Z_FIRST = (("z", "x", "y", "core"), ("z", "y", "x", "core"))
 Z_LATE = (("x", "y", "z", "core"), ("y", "x", "z", "core"))
@@ -289,70 +279,59 @@
     (0, 1024, 256, Z_FIRST),
     (0, 1280, 256, Z_FIRST),
     (1, 0, 256, Z_FIRST),
-    (1, 256, 256, Z_FIRST),
-    (1, 512, 256, Z_LATE),
-    (1, 768, 256, Z_FIRST),
+    (1, 256, 256, Z_MID),
+    (1, 512, 256, Z_FIRST),
+    (1, 768, 256, Z_MID),
     (1, 1024, 256, Z_MID),
-    (1, 1280, 256, Z_LATE),
+    (1, 1280, 256, Z_MID),
 )
 REDUCE = (
-    (1, 1024, 256, Z_FIRST),
-    (1, 1280, 256, Z_LATE),
+    (1, 1024, 256, Z_MID),
+    (1, 1280, 256, Z_MID),
     (1, 512, 256, Z_FIRST),
     (1, 768, 256, Z_FIRST),
-    (1, 0, 256, Z_MID),
-    (1, 256, 256, Z_LATE),
+    (1, 384, 128, Z_FIRST[:1]),
+    (1, 0, 256, Z_FIRST),
+    (1, 256, 128, Z_FIRST[1:]),
     (0, 1024, 256, Z_FIRST),
-    (0, 1280, 256, Z_FIRST),
+    (0, 1280, 256, Z_LATE),
     (0, 512, 256, Z_FIRST),
     (0, 768, 256, Z_FIRST),
-    (0, 0, 256, Z_MID),
-    (0, 256, 256, Z_FIRST),
+    (0, 384, 128, Z_FIRST[:1]),
+    (0, 0, 256, Z_FIRST),
+    (0, 256, 128, Z_FIRST[1:]),
 )
 SCHEDULE = {
-    "start": (("ag", 0, 0), ("ag", 1, 0), ("ag", 8, 0), ("ag", 10, 0), ("ag", 11, 0)),
-    "x0": (("ag", 2, 0),),
-    "dx": (("ag", 3, 0), ("ag", 0, 1), ("ag", 8, 1), ("ag", 11, 1)),
-    "need0": (("ag", 4, 0), ("ag", 1, 1), ("ag", 0, 2), ("ag", 5, 0), ("ag", 2, 1), ("ag", 1, 2), ("ag", 6, 0), ("ag", 3, 1), ("ag", 0, 3), ("ag", 7, 0), ("ag", 2, 2), ("ag", 4, 1), ("ag", 8, 2), ("ag", 1, 3), ("ag", 5, 1), ("ag", 3, 2)),
-    ("attend0", 1): (("ag", 2, 3), ("ag", 6, 1)),
-    ("attend0", 2): (("ag", 4, 2),),
-    ("attend0", 3): (("ag", 5, 2),),
-    "need1": (("ag", 3, 3), ("ag", 7, 1), ("ag", 9, 0), ("ag", 6, 2)),
-    ("up0", 0): (("ag", 10, 1),),
-    ("up0", 1): (("ag", 4, 3),),
-    ("up0", 3): (("ag", 5, 3),),
-    "need2": (("ag", 8, 3), ("ag", 7, 2), ("ag", 11, 2)),
-    ("down0", 1): (("ag", 9, 1),),
-    ("down0", 2): (("ag", 6, 3),),
-    "need3": (("ag", 7, 3), ("ag", 9, 2), ("ag", 10, 2)),
-    ("attend1", 3): (("ag", 9, 3),),
+    "start0": (("ag", 0, 0),),
+    "start1": (("ag", 7, 0), ("ag", 9, 0), ("ag", 10, 0), ("ag", 11, 0), ("ag", 1, 0)),
+    "dx": (("ag", 2, 0),),
+    "need0": (("ag", 0, 1), ("ag", 3, 0), ("ag", 1, 1), ("ag", 4, 0), ("ag", 0, 2), ("ag", 2, 1), ("ag", 1, 2), ("ag", 5, 0), ("ag", 3, 1), ("ag", 6, 0), ("ag", 0, 3), ("ag", 2, 2), ("ag", 7, 1), ("ag", 4, 1), ("ag", 1, 3), ("ag", 5, 1), ("ag", 3, 2)),
+    ("attend0", 3): (("ag", 2, 3), ("ag", 8, 0)),
+    "out0": (("ag", 4, 2),),
+    "need1": (("ag", 3, 3), ("ag", 5, 2), ("ag", 9, 1), ("ag", 6, 1), ("ag", 7, 2), ("ag", 4, 3)),
+    ("up0", 3): (("ag", 10, 1),),
+    "need2": (("ag", 5, 3), ("ag", 6, 2), ("ag", 8, 1), ("ag", 7, 3), ("ag", 9, 2), ("ag", 11, 1)),
+    "need3": (("ag", 6, 3), ("ag", 8, 2), ("ag", 10, 2), ("ag", 9, 3)),
+    "out1": (("ag", 8, 3), ("ag", 11, 2)),
     "need4": (("ag", 10, 3),),
     "dxt1": (("ag", 11, 3),),
     "sent12": (("rs", 0, 0), ("rs", 1, 0)),
-    ("mlpb1", 2): (("rs", 0, 1), ("rs", 1, 1)),
-    "sent11": (("rs", 2, 0), ("rs", 3, 0)),
-    ("result1", 1): (("rs", 0, 2),),
-    ("result1", 3): (("rs", 2, 1),),
-    "lnb1": (("rs", 3, 1),),
-    ("attb1", 0): (("rs", 0, 3),),
-    ("attb1", 1): (("rs", 2, 2),),
-    ("attb1", 2): (("rs", 1, 2), ("rs", 3, 2)),
-    ("attb1", 3): (("fin", 0, 0), ("rs", 1, 3), ("rs", 2, 3)),
-    "sent10": (("fin", 1, 0), ("rs", 3, 3), ("rs", 4, 0), ("rs", 5, 0)),
-    ("downb0", 0): (("fin", 2, 0),),
-    ("downb0", 1): (("rs", 4, 1),),
-    ("downb0", 2): (("rs", 5, 1),),
-    "sent02": (("fin", 3, 0), ("rs", 6, 0), ("rs", 7, 0)),
-    ("mlpb0", 2): (("rs", 6, 1), ("rs", 7, 1)),
-    ("mlpb0", 3): (("rs", 4, 2),),
-    "sent01": (("rs", 8, 0), ("rs", 9, 0)),
-    ("attb0", 0): (("rs", 6, 2), ("rs", 8, 1), ("rs", 7, 2), ("rs", 9, 1)),
-    ("attb0", 2): (("rs", 5, 2), ("rs", 6, 3)),
-    ("attb0", 3): (("rs", 4, 3), ("rs", 7, 3), ("rs", 8, 2)),
-    "sent00": (("fin", 6, 0), ("rs", 9, 2), ("rs", 10, 0), ("rs", 11, 0)),
-    "ln1b0": (("fin", 4, 0), ("rs", 5, 3)),
-    "end0": (("small", 0, 0), ("fin", 7, 0), ("rs", 8, 3), ("rs", 10, 1), ("rs", 9, 3), ("fin", 5, 0), ("small", 0, 1), ("rs", 11, 1)),
-    "end": (("fin", 8, 0), ("rs", 10, 2), ("small", 0, 2), ("fin", 9, 0), ("rs", 11, 2), ("small", 0, 3), ("rs", 11, 3), ("rs", 10, 3), ("small", 0, 4), ("fin", 10, 0), ("fin", 11, 0)),
+    "sent11": (("rs", 0, 1), ("rs", 2, 0), ("rs", 3, 0)),
+    "lnb1": (("rs", 1, 1),),
+    "outb1": (("rs", 0, 2), ("rs", 2, 1), ("rs", 4, 0)),
+    ("attb1", 2): (("rs", 3, 1), ("rs", 1, 2)),
+    "sent10": (("rs", 0, 3), ("rs", 2, 2), ("rs", 3, 2), ("rs", 5, 0), ("rs", 6, 0)),
+    ("downb0", 2): (("rs", 4, 1),),
+    "sent02": (("fin", 0, 0), ("rs", 1, 3), ("rs", 2, 3), ("rs", 5, 1), ("rs", 7, 0), ("rs", 8, 0)),
+    ("mlpb0", 2): (("rs", 3, 3), ("rs", 6, 1)),
+    ("mlpb0", 3): (("fin", 1, 0),),
+    "sent01": (("fin", 2, 0), ("rs", 4, 2), ("rs", 5, 2), ("rs", 8, 1), ("rs", 7, 1), ("fin", 3, 0), ("rs", 9, 0), ("rs", 10, 0)),
+    "outb0": (("rs", 6, 2), ("rs", 9, 1), ("rs", 11, 0)),
+    ("attb0", 2): (("rs", 7, 2),),
+    ("attb0", 3): (("rs", 4, 3), ("rs", 10, 1)),
+    "sent00": (("rs", 5, 3), ("rs", 8, 2), ("rs", 9, 2), ("fin", 4, 0), ("rs", 6, 3), ("rs", 11, 1), ("rs", 12, 0), ("rs", 13, 0)),
+    "end0": (("small", 0, 0), ("rs", 7, 3), ("rs", 10, 2)),
+    "end": (("rs", 8, 3), ("rs", 9, 3), ("fin", 5, 0), ("rs", 12, 1), ("small", 0, 1), ("fin", 6, 0), ("rs", 11, 2), ("rs", 10, 3), ("rs", 13, 1), ("fin", 7, 0), ("fin", 8, 0), ("fin", 9, 0), ("small", 0, 2), ("rs", 12, 2), ("rs", 11, 3), ("fin", 10, 0), ("small", 0, 3), ("rs", 13, 2), ("fin", 11, 0), ("rs", 12, 3), ("rs", 13, 3), ("small", 0, 4), ("fin", 12, 0), ("fin", 13, 0)),
 }
 
 
@@ -367,17 +346,41 @@
         for h in range(GROUP):
             across[h * PAD + i, h * REL_LANES + place] = 1.0
     return down, across
+PART_ROWS, QV_AT, HID_AT, REL_AT = 8, 0, 1, 1 + BLOCKS
+SHARE_ROWS, GAIN_AT, BIAS_AT = 16, 0, 2 * BLOCKS
+
+
+def small_plan(digits):
+    names = ("core", "x", "y", "z")
+    over = [digits[n] for n in names if digits[n].axis == "tensor"]
+    return over, [digits[n] for n in names if digits[n].axis == "fsdp"]
+
+
+def small_shapes(digits, width):
+    over, rest = small_plan(digits)
+    left = [d for d in sorted(digits.values(), key=lambda d: d.dim) if d.axis == "tensor"]
+    shapes = [tuple(d.size for d in left) + (PART_ROWS, width), (SHARE_ROWS, width)]
+    for digit in over:
+        left = [d for d in left if d is not digit]
+        mine = tuple(d.size for d in left) + (PART_ROWS, width)
+        shapes += [(digit.size,) + mine, (digit.size, SHARE_ROWS, width), mine]
+    return shapes + [(d.size, PART_ROWS + SHARE_ROWS, width) for d in rest]
 
 
 def stage_keys(phases):
-    return [(q, h, phase) for q in range(len(REDUCE)) for h in range(2) for phase in range(phases)]
+    return [
+        (q, h, phase)
+        for q in range(len(REDUCE))
+        for h in range(len(REDUCE[q][3]))
+        for phase in range(phases)
+    ]
 
 
 def block_kernel(
     n_fsdp, n_tensor,
     x_hbm, ct_hbm, counts, qkv_w, out_w, up_w, down_w, rel_w, qv_w, hid_w, mask, gains, offs, perm, perm_t, rel_down, rel_across,
     xo_hbm, dxo_hbm, gsum, total, keep_gl, keep_gp, keep_qkv, keep_pts,
-    wt, dgr, rels, sides, io, xs, ms, aw, qkv, pts, ow, osb, a2, gl, gp, ubuf, acc, dx, cut, awt, dwin, dsum, added, small,
+    wt, dgr, rels, sides, io, xs, ms, aw, qkv, pts, ow, osb, a2, gl, gp, ubuf, acc, dx, cut, awt, dwin, dsum, added,
     *rest,
 ):
     digits = plan(n_fsdp, n_tensor)
@@ -388,9 +391,12 @@
     for at, key in enumerate(stage_keys(phases)):
         stage[key] = rest[at]
     rest = rest[len(stage) :]
-    small_slots = rest[:phases]
+    over, beside = small_plan(digits)
+    count = 2 + 3 * len(over) + len(beside)
+    parted, shared, smalls = rest[0], rest[1], rest[2:count]
+    rest = rest[count:]
     (io_sem, own_sem, keep_sem, rel_send, rel_recv, side_send, side_recv, ag_send, ag_recv, rs_send, rs_recv,
-     sm_send, sm_recv) = rest[phases:]
+     sm_send, sm_recv) = rest
     images = io.shape[0]
     groups = n_tensor
     rows, width = xs.shape[1:]
@@ -422,10 +428,10 @@
     def ag_copies(p, phase):
         b, c, n, names = GATHER[p]
         out = []
-        for h in range(2):
+        for h in range(len(names)):
             order = [digits[name] for name in names[h]]
             digit = order[phase]
-            at = pl.ds(c + h * (n // 2), n // 2)
+            at = pl.ds(c + h * (n // len(names)), n // len(names))
             index = tuple(slice(None) if d in order[:phase] else d.here() for d in dims)
             place = wt.at[(b,) + index + (slice(None), at)]
             for s in range(1, digit.size):
@@ -473,10 +479,10 @@
     def rs_copies(q, phase):
         b, c, n, names = REDUCE[q]
         out = []
-        for h in range(2):
+        for h in range(len(names)):
             order = [digits[name] for name in names[h]][::-1]
             digit = order[phase]
-            at = pl.ds(c + h * (n // 2), n // 2)
+            at = pl.ds(c + h * (n // len(names)), n // len(names))
             for s in range(1, digit.size):
                 to, device = digit.peer(s)
                 index = tuple(
@@ -500,10 +506,10 @@
     def rs_absorb(q, phase):
         b, c, n, names = REDUCE[q]
         grad = grad_ref(b)
-        for h in range(2):
+        for h in range(len(names)):
             order = [digits[name] for name in names[h]][::-1]
             digit = order[phase]
-            at = slice(c + h * (n // 2), c + (h + 1) * (n // 2))
+            at = slice(c + h * (n // len(names)), c + (h + 1) * (n // len(names)))
             left = [d for d in dims if d not in order[: phase + 1]]
             land = stage[q, h, phase]
             steps = int(np.prod([d.size for d in left])) if left else 1
@@ -521,7 +527,7 @@
                 grad[index + (slice(None), at)] = value
                 return carry
 
-            lax.fori_loop(0, steps, one, 0, unroll=min(steps, 4))
+            lax.fori_loop(0, steps, one, 0, unroll=min(steps, ABS_UNROLL))
 
     def rs_step(q, phase):
         if phase > 0:
@@ -532,8 +538,8 @@
     def rs_finish(q):
         arrive(rs_all(q, phases - 1))
         b, c, n, names = REDUCE[q]
-        for h in range(2):
-            at = slice(c + h * (n // 2), c + (h + 1) * (n // 2))
+        for h in range(len(names)):
+            at = slice(c + h * (n // len(names)), c + (h + 1) * (n // len(names)))
             index = tuple(d.here() for d in dims)
             value = grad_ref(b)[index + (slice(None), at)].astype(F32)
             for s in range(digits[names[h][0]].size - 1):
@@ -559,38 +565,74 @@
                 def _():
                     slot((name, at))
 
-    small_order = [digits[n] for n in ("core", "y", "x", "z")]
-
     def small_copies(phase):
-        digit = small_order[phase]
-        place = small_slots[phase].at[digit.here()]
-        return [
+        order = over + beside
+        digit = order[phase]
+        pairs = []
+        if phase < len(over):
+            land_part, land_share, _ = smalls[3 * phase : 3 * phase + 3]
+            source = parted if phase == 0 else smalls[3 * phase - 1]
+            left = [d for d in tdims if d not in order[:phase]]
+            here = digit.here()
+            for s in range(1, digit.size):
+                index = tuple(digit.peer(s)[0] if d is digit else slice(None) for d in left)
+                pairs.append((s, source.at[index], land_part.at[here]))
+                pairs.append((s, land_share.at[here], land_share.at[here]))
+            rows_all = sum(int(np.prod(src.shape[:-1])) for _, src, _ in pairs)
+            whole = ubuf.at[0:rows_all]
+        else:
+            land = smalls[3 * len(over) + phase - len(over)]
+            for s in range(1, digit.size):
+                pairs.append((s, land.at[digit.here()], land.at[digit.here()]))
+            whole = land.at[0 : digit.size - 1]
+        copies = [
             pltpu.make_async_remote_copy(
-                src_ref=place, dst_ref=place, send_sem=sm_send.at[phase], recv_sem=sm_recv.at[phase],
+                src_ref=src, dst_ref=dst, send_sem=sm_send.at[phase], recv_sem=sm_recv.at[phase],
                 device_id=digit.peer(s)[1], device_id_type=MESH)
-            for s in range(1, digit.size)
+            for s, src, dst in pairs
         ]
-
-    def small_all(phase):
-        digit = small_order[phase]
-        place = small_slots[phase].at[0 : digit.size - 1]
-        return pltpu.make_async_remote_copy(
-            src_ref=place, dst_ref=place, send_sem=sm_send.at[phase], recv_sem=sm_recv.at[phase],
+        return copies, pltpu.make_async_remote_copy(
+            src_ref=whole, dst_ref=whole, send_sem=sm_send.at[phase], recv_sem=sm_recv.at[phase],
             device_id=digit.peer(1)[1], device_id_type=MESH)
 
     def small_step(phase):
-        if phase == 0:
-            value = small[...]
+        order = over + beside
+        if phase > 0:
+            arrive(small_copies(phase - 1)[1])
+            size = order[phase - 1].size
+            if phase <= len(over):
+                land_part, land_share, after = smalls[3 * phase - 3 : 3 * phase]
+                part, share = land_part[0], land_share[0]
+                for s in range(1, size):
+                    part, share = part + land_part[s], share + land_share[s]
+                after[...] = part
+            else:
+                land = smalls[3 * len(over) + phase - 1 - len(over)]
+                value = land[0]
+                for s in range(1, size):
+                    value = value + land[s]
         else:
-            arrive(small_all(phase - 1))
-            value = small_slots[phase - 1][0]
-            for s in range(1, small_order[phase - 1].size):
-                value = value + small_slots[phase - 1][s]
-        if phase < phases:
-            small_slots[phase][small_order[phase].here()] = value
-            start(small_copies(phase))
+            share = shared[...]
+        if phase < len(over):
+            digit = order[phase]
+            land_part, land_share, _ = smalls[3 * phase : 3 * phase + 3]
+            source = parted if phase == 0 else smalls[3 * phase - 1]
+            left = [d for d in tdims if d not in order[:phase]]
+            index = tuple(digit.here() if d is digit else slice(None) for d in left)
+            land_part[digit.here()] = source[index]
+            land_share[digit.here()] = share
+        elif phase < len(order):
+            land = smalls[3 * len(over) + phase - len(over)]
+            here = order[phase].here()
+            if phase == len(over):
+                land[here, 0:PART_ROWS] = smalls[3 * phase - 1][...]
+                land[here, PART_ROWS:] = share
+            else:
+                land[here] = value
         else:
             total[...] = value
+        if phase < len(order):
+            start(small_copies(phase)[0])
 
     loads = [
         pltpu.make_async_copy(x_hbm, io, io_sem.at[0]),
@@ -619,8 +661,10 @@
             wt[(b,) + mine + (slice(None), slice(j * PART, (j + 1) * PART))] = ubuf[
                 row : row + per, :
             ].astype(BF16)
-
-    slot("start")
+        slot("start%d" % b)
+
+    parted[...] = jnp.zeros_like(parted)
+    shared[...] = jnp.zeros_like(shared)
 
     rel_count = rel_w.shape[2]
     added[0, 0:8, :] = jnp.zeros((8, GROUP * PAD), F32)
@@ -790,8 +834,8 @@
         pltpu.make_async_copy(keep_pts, pts, keep_sem.at[1]),
     ]
     for b in range(BLOCKS - 1, -1, -1):
-        bias_row = BIAS_ROW + 4 * b
-        small[bias_row + 3 : bias_row + 4, :] = column_sum(dx)
+        bias_row = BIAS_AT + 4 * b
+        shared[bias_row + 3 : bias_row + 4, :] = column_sum(dx)
         cut[...] = dx[...].astype(BF16)
         slot("dxt%d" % b)
         dxt = jnp.transpose(cut[...])
@@ -821,7 +865,7 @@
             dh = dot(cut[...], weight(b, t, c_down, cols))
             du = (dh * gp[t].astype(F32)).astype(BF16)
             gp[t] = du
-            small[pl.ds(HID_ROW + b * groups + t, 1), :] = jnp.sum(
+            parted[tplace(t) + (slice(HID_AT + b, HID_AT + b + 1), slice(None))] = jnp.sum(
                 fold(du.astype(F32)), 0, keepdims=True
             )
             put_grad(b, t, c_up, c_down, dot(a_t, du))
@@ -849,9 +893,9 @@
             start(mlp_loads)
         slot("lnb%d" % b)
         sums = back_norm(ms.at[b], acc, gains[b, 1:2, :], dx)
-        small[GAIN_ROW + 2 * b + 1 : GAIN_ROW + 2 * b + 2, :] = sums[0]
-        small[bias_row + 1 : bias_row + 2, :] = sums[1]
-        small[bias_row + 2 : bias_row + 3, :] = sums[2]
+        shared[GAIN_AT + 2 * b + 1 : GAIN_AT + 2 * b + 2, :] = sums[0]
+        shared[bias_row + 1 : bias_row + 2, :] = sums[1]
+        shared[bias_row + 2 : bias_row + 3, :] = sums[2]
         cut[...] = dx[...].astype(BF16)
         dmt = jnp.transpose(cut[...])
         awt[...] = jnp.transpose(aw[b])
@@ -859,6 +903,7 @@
         da[...] = jnp.zeros_like(da)
         for t in range(groups):
             put_grad(b, t, c_out, c_up, dot(dmt, osb[b, t]))
+        slot("outb%d" % b)
         if b < last:
             for cp in att_loads:
                 cp.wait()
@@ -895,11 +940,10 @@
                 return c2
 
             lax.fori_loop(0, images * WINS // BATCH, window, 0)
-            col = pl.ds(pl.multiple_of(t * lanes, lanes), lanes)
             for j in range(2):
                 val = dwin[:, 2 * j * lanes : (2 * j + 1) * lanes].astype(F32)
-                row = QV_ROW + 2 * b + j
-                small[row : row + 1, col] = jnp.sum(fold(val), 0, keepdims=True)
+                col = slice((2 * b + j) * lanes, (2 * b + j + 1) * lanes)
+                parted[tplace(t) + (slice(QV_AT, QV_AT + 1), col)] = jnp.sum(fold(val), 0, keepdims=True)
             ds_all = dsum[...]
             high = ds_all.astype(BF16)
             rest_low = (ds_all - high.astype(F32)).astype(BF16)
@@ -915,7 +959,9 @@
                 skew = jnp.where((row_id & bit) != 0, pltpu.roll(skew, bit, 1), skew)
             skew = jnp.sum(skew, 0, keepdims=True)
             for h in range(GROUP):
-                small[pl.ds(rel_row(groups) + (b * groups + t) * GROUP + h, 1), 0:REL_LANES] = skew[
+                row = REL_AT + (b * GROUP + h) // 2
+                col = slice(h % 2 * REL_LANES, (h % 2 + 1) * REL_LANES)
+                parted[tplace(t) + (slice(row, row + 1), col)] = skew[
                     :, h * REL_LANES : (h + 1) * REL_LANES
                 ]
             put_grad(b, t, 0, c_out, dot(awt[...], dwin[...]))
@@ -935,8 +981,8 @@
             vals.append(dot(perm_t[b, i], high) + dot(perm_t[b, i], rest_low))
         put_rows(acc, vals)
         sums = back_norm(xs.at[b], acc, gains[b, 0:1, :], dx)
-        small[GAIN_ROW + 2 * b : GAIN_ROW + 2 * b + 1, :] = sums[0]
-        small[bias_row : bias_row + 1, :] = sums[1]
+        shared[GAIN_AT + 2 * b : GAIN_AT + 2 * b + 1, :] = sums[0]
+        shared[bias_row : bias_row + 1, :] = sums[1]
     slot("end0")
     x_store.wait()
     for i in range(images):
@@ -953,7 +999,7 @@
         for phase in range(phases):
             sent(rs_all(q, phase))
     for phase in range(phases):
-        sent(small_all(phase))
+        sent(small_copies(phase)[1])
 
 
 def block_call(x, ct, counts, mats, rel, qv, hidden, gains, offs, n_fsdp, n_tensor):
@@ -977,13 +1023,12 @@
         jnp.asarray(down, BF16),
         jnp.asarray(across, BF16),
     )
-    small_rows = rel_row(n_tensor) + BLOCKS * n_tensor * GROUP
+    small = small_shapes(digits, width)
     stages = []
     for q, h, phase in stage_keys(phases):
         order = [digits[n] for n in REDUCE[q][3][h]][::-1]
         left = tuple(d.size for d in dims if d not in order[: phase + 1])
-        stages.append(pltpu.VMEM((order[phase].size - 1,) + left + (per, REDUCE[q][2] // 2), BF16))
-    small_order = [digits[n] for n in ("core", "y", "x", "z")]
+        stages.append(pltpu.VMEM((order[phase].size - 1,) + left + (per, REDUCE[q][2] // len(REDUCE[q][3])), BF16))
     vmem = pl.BlockSpec(memory_space=pltpu.VMEM)
     anyspace = pl.BlockSpec(memory_space=pl.ANY)
     keep = [
@@ -997,7 +1042,7 @@
             jax.ShapeDtypeStruct(x.shape, F32),
             jax.ShapeDtypeStruct(x.shape, F32),
             jax.ShapeDtypeStruct((BLOCKS, per, cols), F32),
-            jax.ShapeDtypeStruct((small_rows, width), F32),
+            jax.ShapeDtypeStruct((PART_ROWS + SHARE_ROWS, width), F32),
         ) + tuple(jax.ShapeDtypeStruct(s, BF16) for s in keep),
         in_specs=[
             anyspace, anyspace, pl.BlockSpec(memory_space=pltpu.SMEM), anyspace, anyspace, anyspace,
@@ -1028,10 +1073,9 @@
             pltpu.VMEM((wrows, 3 * lanes), BF16),
             pltpu.VMEM((PAD, GROUP * PAD), F32),
             pltpu.VMEM((WINS, PAD, GROUP * PAD), F32),
-            pltpu.VMEM((small_rows, width), F32),
         ]
         + stages
-        + [pltpu.VMEM((d.size, small_rows, width), F32) for d in small_order]
+        + [pltpu.VMEM(shape, F32) for shape in small]
         + [
             dma((2,)), dma((BLOCKS, 6)), dma((4,)),
             dma((n_tensor - 1,)), dma((n_tensor - 1,)), dma((n_tensor - 1,)), dma((n_tensor - 1,)),
@@ -1047,7 +1091,7 @@
     return out[:4]
 
 
-def adam_kernel(groups, slot, *refs):
+def adam_kernel(*refs):
     count = 31
     ins, outs = refs[:count], refs[count : 2 * count - 2]
     held, sem = refs[2 * count - 2 : -1], refs[-1]
@@ -1056,17 +1100,17 @@
     ]
     for cp in copies:
         cp.start()
-    for cp in copies:
+    passed = [pltpu.make_async_copy(held[j], outs[j], sem.at[j]) for j in range(2)]
+    for j in range(2):
+        copies[j].wait()
+        passed[j].start()
+    for cp in copies[2:]:
         cp.wait()
-    passed = [pltpu.make_async_copy(held[j], outs[j], sem.at[j]) for j in range(2)]
-    for cp in passed:
-        cp.start()
     gsum, total = held[2:4]
     params = [held[4 + 3 * j : 7 + 3 * j] for j in range(9)]
     news = [outs[2 + 3 * j : 5 + 3 * j] for j in range(9)]
     lanes = GROUP * HEAD_DIM
     hid = params[2][0].shape[2]
-    t = slot[0]
 
     def update(kind, place, grad, rate, decay):
         new = adam(*(p[place] for p in params[kind]), grad, rate, decay)
@@ -1080,36 +1124,36 @@
         update(2, (b,), gsum[b, :, 4 * lanes : 4 * lanes + hid], MATRIX_RATE, WEIGHT_DECAY)
         update(3, (b,), gsum[b, :, 4 * lanes + hid :], MATRIX_RATE, WEIGHT_DECAY)
         heads, rels = params[4][0].shape[1:]
-        at = rel_row(groups) + b * groups * heads
-        hid_at = HID_ROW + b * groups
-        qv_rows = slice(QV_ROW + 2 * b, QV_ROW + 2 * b + 2)
-        rel = pick(t, [total[at + i * heads : at + (i + 1) * heads, 0:rels] for i in range(groups)])
-        qv = pick(t, [total[qv_rows, i * lanes : (i + 1) * lanes] for i in range(groups)])
-        hidden = pick(t, [total[hid_at + i : hid_at + i + 1, :] for i in range(groups)])
-        update(4, (b,), rel, SMALL_RATE, 0.0)
-        update(5, (b,), qv, SMALL_RATE, 0.0)
-        update(6, (slice(b, b + 1),), hidden, SMALL_RATE, 0.0)
-        update(7, (b,), total[GAIN_ROW + 2 * b : GAIN_ROW + 2 * b + 2, :], SMALL_RATE, 0.0)
-        update(8, (b,), total[BIAS_ROW + 4 * b : BIAS_ROW + 4 * b + 4, :], SMALL_RATE, 0.0)
+        for h in range(heads):
+            row, col = REL_AT + (b * GROUP + h) // 2, h % 2 * REL_LANES
+            grad = total[row : row + 1, col : col + rels]
+            update(4, (b, slice(h, h + 1)), grad, SMALL_RATE, 0.0)
+        for j in range(2):
+            grad = total[QV_AT : QV_AT + 1, (2 * b + j) * lanes : (2 * b + j + 1) * lanes]
+            update(5, (b, slice(j, j + 1)), grad, SMALL_RATE, 0.0)
+        update(6, (slice(b, b + 1),), total[HID_AT + b : HID_AT + b + 1, :], SMALL_RATE, 0.0)
+        at = PART_ROWS + GAIN_AT + 2 * b
+        update(7, (b,), total[at : at + 2, :], SMALL_RATE, 0.0)
+        at = PART_ROWS + BIAS_AT + 4 * b
+        update(8, (b,), total[at : at + 4, :], SMALL_RATE, 0.0)
     for cp in passed:
         cp.wait()
 
 
-def adam_call(x, dx, gsum, total, params, n_tensor):
+def adam_call(x, dx, gsum, total, params):
     flat = [p for group in params for p in group]
     ins = [x, dx, gsum, total] + flat
     hbm = pl.BlockSpec(memory_space=pltpu.HBM)
     vmem = pl.BlockSpec(memory_space=pltpu.VMEM)
-    slot = lax.axis_index("tensor").astype(jnp.int32).reshape(1)
     return pl.pallas_call(
-        functools.partial(adam_kernel, n_tensor),
+        adam_kernel,
         out_shape=tuple(jax.ShapeDtypeStruct(p.shape, p.dtype) for p in [x, dx] + flat),
-        in_specs=[pl.BlockSpec(memory_space=pltpu.SMEM)] + [hbm] * len(ins),
+        in_specs=[hbm] * len(ins),
         out_specs=(hbm, hbm) + tuple(vmem for _ in flat),
         scratch_shapes=[pltpu.VMEM(p.shape, p.dtype) for p in ins]
         + [pltpu.SemaphoreType.DMA((len(ins),))],
         compiler_params=pltpu.CompilerParams(vmem_limit_bytes=127 * MIB // 2),
-    )(slot, *ins)
+    )(*ins)
 
 
 def shards(n_fsdp, n_tensor, *args):
@@ -1123,7 +1167,7 @@
     x, dx, gsum, total = block_call(
         image_rows, cotangent, live_counts, mats, rel, qv, hidden, gain, bias, n_fsdp, n_tensor
     )
-    new = adam_call(x, dx, gsum, total, groups, n_tensor)
+    new = adam_call(x, dx, gsum, total, groups)
     x, dx = new[:2]
     new = [list(new[2 + 3 * j : 5 + 3 * j]) for j in range(9)]
     for j, f in turn.items():

time: 163 us -> 154 us (0.945)
  Pallas kernels: 161 us -> 152 us
    pallas_call x1, Pallas kernels: 155 us -> 146 us  [block_call(): pl.pallas_call(functools.partial(block_kernel, n_fsdp, n_tensor), out_sha...]
where the time goes in v5:
time: 154 us
  Pallas kernels  152 us (99%)
    pallas_call x1, Pallas kernels, block_call(): pl.pallas_call(functools.partial(block_kernel, n_fsdp, n_tensor), out_sha...  146 us
    pallas_call x1, Pallas kernels, adam_call(): pl.pallas_call(adam_kernel, out_shape=tuple((jax.ShapeDtypeStruct(p.shape...  6.06 us

profile of v5, /device:TPU:0, one launch (start us, length us, event | category | flops | bytes accessed | tf_op | source)
XLA Modules:
  0.0 153.6 jit_solution(11605566699548655905)
XLA Ops:
  1.3 146.0 %shard_map.554 = (f32[3,196,512]{2,1,0:T(8,128)}, f32[3,196,512]{2,1,0:T(8,128)}, f32[2,64,1536]{2,1,0:T(8,128)}, f32[24,512]{1,0:T(8,128)}, bf16[4,592,512]{2,1...) custom-call(f32[3,196,512]{2,1,0:T(8,128)} %x_hbm.1, ...), custom_call_target="tpu_custom_call" | custom-call | tf_op jit(solution)/shard_map/pallas_call | solution.py:1039
  147.4 6.1 %shard_map.555 = (f32[3,196,512]{2,1,0:T(8,128)}, f32[3,196,512]{2,1,0:T(8,128)}, f32[2,3,64,128]{3,2,1,0:T(8,128)}, f32[2,3,64,128]{3,2,1,0:T(8,128)}, f32[2,3,...) custom-call(f32[3,196,512]{2,1,0:T(8,128)} %get-tuple-element.62.ref, ...), custom_call_target="tpu_custom_call" | custom-call | tf_op jit(solution)/shard_map/pallas_call | solution.py:1148
